TPU v7x, 32 devices: a whole 2x2x4 slice. The times are simulated.
32 devices in a mesh: groups: 2 (over x), fsdp: 8 (over z, y), tenant: 2 (over core).
Axes of the slice: x: 2, y: 2, z: 4, core: 2. Of those that a mesh axis runs over, the one named last changes fastest.
Arguments:
- tokens: bfloat16 [4096, 8192], P(('groups', 'fsdp', 'tenant')), parts along dimension 0, may hold values from -6 to 6
- grad_out: bfloat16 [4096, 1024], P(('groups', 'fsdp', 'tenant')), parts along dimension 0, may hold values from -6 to 6
- base_weight: bfloat16 [8192, 1024], P('fsdp'), may hold values from -0.0625 to 0.0625
- page_a: bfloat16 [32, 128, 8192], P(('groups', 'fsdp', 'tenant')), parts along dimension 0, may hold values from -0.0625 to 0.0625
- page_b: bfloat16 [32, 128, 1024], P(('groups', 'fsdp', 'tenant')), parts along dimension 0, may hold values from -0.5 to 0.5
- page_owner: int32 [32], P('groups'), parts along dimension 0, may hold values from 0 to 15, as said below
- row_tenant: int32 [4096], P(('groups', 'fsdp', 'tenant')), parts along dimension 0, may hold values from 0 to 63, as said below
Outputs:
- projected: bfloat16 [4096, 1024], P(('groups', 'fsdp', 'tenant')), parts along dimension 0
- grad_tokens: bfloat16 [4096, 8192], P(('groups', 'fsdp', 'tenant')), parts along dimension 0
- grad_page_a: bfloat16 [32, 128, 8192], P(('groups', 'fsdp', 'tenant')), parts along dimension 0
- grad_page_b: bfloat16 [32, 128, 1024], P(('groups', 'fsdp', 'tenant')), parts along dimension 0
There are 2 independent parts, one for each index of `groups`. A program takes and returns all parts, laid end to end along the dimension named above; an argument that names none is the same for every part. Nothing has to cross between parts.
Inputs may be any that keep to these rules, and one draw needn't show every extreme that they name: A permutation: page p is stored at position page_owner[p] of page_a and page_b, that is on that device of fsdp+tenant. `row_tenant`: among the 128 rows of one device, at most 10 name tenants of any one page; some page gets exactly 10 rows from every device.
All inputs are finite; a program needn't handle non-finite values.
Results may differ from a plain program's by a relative error of at most 0.0051.
Values may be sent and summed in bfloat16 or wider, within the bound.
No kernel may reach another device: no remote copies, remote signals or barrier semaphores. Data moves between devices by JAX's collectives and lax.ppermute only.
A program may use at most 128 MiB of HBM per device.

v0:
```python
import jax
import jax.numpy as jnp
from jax import lax
from jax.sharding import PartitionSpec as P

RANK = 32


adapter_scale = 2.0


def on_device(tokens, grad_out, base_weight, page_a, page_b, page_owner, row_tenant):
    rows = tokens.shape[0]
    width = tokens.shape[1]
    narrow = grad_out.shape[1]
    fsdp_size = lax.axis_size("fsdp")
    tenant_size = lax.axis_size("tenant")
    devices = fsdp_size * tenant_size
    capacity = max(4, 4 * rows // (3 * devices))
    total_slots = devices * capacity
    per_page = page_a.shape[1] // RANK
    pages = page_owner.shape[0]
    page_index = row_tenant // per_page
    page_match = page_index[:, None] == jnp.arange(pages, dtype=jnp.int32)[None, :]
    target = jnp.sum(jnp.where(page_match, page_owner[None, :], 0), axis=1)
    target_match = (target[:, None] == jnp.arange(devices, dtype=jnp.int32)[None, :]).astype(
        jnp.int32
    )
    before = jnp.cumsum(target_match, axis=0) - target_match
    slot_of_row = target * capacity + jnp.sum(before * target_match, axis=1)
    placing = (jnp.arange(total_slots, dtype=jnp.int32)[:, None] == slot_of_row[None, :]).astype(
        jnp.bfloat16
    )
    member = (
        (row_tenant % per_page)[:, None] == jnp.arange(per_page, dtype=jnp.int32)[None, :]
    ).astype(jnp.bfloat16)
    send_tokens = jnp.dot(placing, tokens, preferred_element_type=jnp.float32).astype(jnp.bfloat16)
    send_grads = jnp.dot(placing, grad_out, preferred_element_type=jnp.float32).astype(jnp.bfloat16)
    send_member = jnp.dot(placing, member, preferred_element_type=jnp.float32).astype(jnp.bfloat16)
    got_tokens, got_grads, got_member = (
        lax.all_to_all(
            lax.all_to_all(
                send_tokens.reshape(fsdp_size, tenant_size, capacity, width),
                "fsdp",
                split_axis=0,
                concat_axis=0,
                tiled=True,
            ),
            "tenant",
            split_axis=1,
            concat_axis=1,
            tiled=True,
        ),
        lax.all_to_all(
            lax.all_to_all(
                send_grads.reshape(fsdp_size, tenant_size, capacity, narrow),
                "fsdp",
                split_axis=0,
                concat_axis=0,
                tiled=True,
            ),
            "tenant",
            split_axis=1,
            concat_axis=1,
            tiled=True,
        ),
        lax.all_to_all(
            lax.all_to_all(
                send_member.reshape(fsdp_size, tenant_size, capacity, per_page),
                "fsdp",
                split_axis=0,
                concat_axis=0,
                tiled=True,
            ),
            "tenant",
            split_axis=1,
            concat_axis=1,
            tiled=True,
        ),
    )
    got_tokens = got_tokens.reshape(total_slots, width)
    got_grads = got_grads.reshape(total_slots, narrow)
    got_member = got_member.reshape(total_slots, per_page)
    mask = jnp.repeat(got_member.astype(jnp.float32), RANK, axis=1)
    left_factor = page_a[0]
    right_factor = page_b[0]
    reduced_rank_rows = (
        lax.dot_general(
            got_tokens, left_factor, (((1,), (1,)), ((), ())), preferred_element_type=jnp.float32
        )
        * mask
    ).astype(jnp.bfloat16)
    adapter_output = (
        adapter_scale * jnp.dot(reduced_rank_rows, right_factor, preferred_element_type=jnp.float32)
    ).astype(jnp.bfloat16)
    reduced_gradient = (
        lax.dot_general(
            got_grads, right_factor, (((1,), (1,)), ((), ())), preferred_element_type=jnp.float32
        )
        * mask
    ).astype(jnp.bfloat16)
    adapter_backward = (
        adapter_scale * jnp.dot(reduced_gradient, left_factor, preferred_element_type=jnp.float32)
    ).astype(jnp.bfloat16)
    back_out, back_grad = (
        lax.all_to_all(
            lax.all_to_all(
                adapter_output.reshape(fsdp_size, tenant_size, capacity, narrow),
                "fsdp",
                split_axis=0,
                concat_axis=0,
                tiled=True,
            ),
            "tenant",
            split_axis=1,
            concat_axis=1,
            tiled=True,
        ),
        lax.all_to_all(
            lax.all_to_all(
                adapter_backward.reshape(fsdp_size, tenant_size, capacity, width),
                "fsdp",
                split_axis=0,
                concat_axis=0,
                tiled=True,
            ),
            "tenant",
            split_axis=1,
            concat_axis=1,
            tiled=True,
        ),
    )
    back_out = back_out.reshape(total_slots, narrow)
    back_grad = back_grad.reshape(total_slots, width)
    left_factor_gradient = (
        adapter_scale
        * lax.dot_general(
            reduced_gradient,
            got_tokens,
            (((0,), (0,)), ((), ())),
            preferred_element_type=jnp.float32,
        )
    ).astype(jnp.bfloat16)
    right_factor_gradient = (
        adapter_scale
        * lax.dot_general(
            reduced_rank_rows,
            got_grads,
            (((0,), (0,)), ((), ())),
            preferred_element_type=jnp.float32,
        )
    ).astype(jnp.bfloat16)
    base_out = jnp.dot(
        tokens,
        lax.all_gather(base_weight, "fsdp", axis=0, tiled=True),
        preferred_element_type=jnp.float32,
    )
    base_back = lax.dot_general(
        grad_out,
        lax.all_gather(base_weight, "fsdp", axis=0, tiled=True),
        (((1,), (1,)), ((), ())),
        preferred_element_type=jnp.float32,
    )
    out_rows = lax.dot_general(
        placing, back_out, (((0,), (0,)), ((), ())), preferred_element_type=jnp.float32
    )
    back_rows = lax.dot_general(
        placing, back_grad, (((0,), (0,)), ((), ())), preferred_element_type=jnp.float32
    )
    projected = (base_out + out_rows).astype(jnp.bfloat16)
    grad_tokens = (base_back + back_rows).astype(jnp.bfloat16)
    return (projected, grad_tokens, left_factor_gradient[None], right_factor_gradient[None])


def solution(mesh):
    placed = (
        P(("groups", "fsdp", "tenant"), None),
        P(("groups", "fsdp", "tenant"), None),
        P("fsdp", None),
        P(("groups", "fsdp", "tenant"), None, None),
        P(("groups", "fsdp", "tenant"), None, None),
        P("groups"),
        P(("groups", "fsdp", "tenant")),
    )
    return jax.shard_map(
        on_device,
        mesh=mesh,
        in_specs=placed,
        out_specs=(
            P(("groups", "fsdp", "tenant"), None),
            P(("groups", "fsdp", "tenant"), None),
            P(("groups", "fsdp", "tenant"), None, None),
            P(("groups", "fsdp", "tenant"), None, None),
        ),
        check_vma=False,
    )
```

profile of v0, /device:TPU:13, one launch (start us, length us, event | category | flops | bytes accessed | tf_op | source)
XLA Modules:
  0.0 385.8 jit_solution(734896135673281114)
XLA Ops:
  7.2 0.0 copy-start
  7.2 0.0 all-gather.2.cloned.1.call-start
  7.2 0.7 all-gather.2.cloned.1.call-update
  7.9 0.7 and_select_fusion
  8.6 0.8 select_reduce_fusion.1
  9.4 0.1 fusion.20
  9.5 0.2 reduce_window_sum.11
  9.7 0.2 select_reduce_fusion
  9.9 0.2 convolution_convert_fusion.2
  10.1 0.1 reshape.53
  10.2 0.6 copy.33
  10.9 5.7 %all-to-all-start.2 = ((bf16[8,2,10,4]{2,1,3,0:T(2,128)(2,1)}), bf16[8,2,10,4]{2,1,3,0:T(2,128)(2,1)S(1)}, u32[]{:S(2)}, u32[]{:S(2)}) async-start(bf16[8,2,10,4]{2,1,3,0:T(2,128)(2,1)} %copy.33), calls=%async_computation.2 | async-start | bytes 32768 | tf_op jit(solution)/shard_map/all_to_all | solution.py:68
  16.5 0.2 convolution_convert_fusion.1
  16.8 0.1 reshape.57
  16.9 1.1 copy.40
  18.0 1.9 all-to-all-done.2
  19.9 5.4 %all-to-all-start.6 = ((bf16[8,2,10,1024]{3,1,2,0:T(2,128)(2,1)}), bf16[8,2,10,1024]{3,1,2,0:T(2,128)(2,1)S(1)}, u32[]{:S(2)}, u32[]{:S(2)}) async-start(bf16[8,2,10,1024]{3,1,2,0:T(2,128)(2,1)} %copy.40), calls=%async_computation.6 | async-start | bytes 655360 | tf_op jit(solution)/shard_map/all_to_all | solution.py:55
  25.3 2.3 convolution_convert_fusion
  27.7 4.7 %reshape.51 = bf16[8,2,10,8192]{3,2,1,0:T(8,128)(2,1)} reshape(bf16[160,8192]{1,0:T(8,128)(2,1)} %convolution_convert_fusion) | data formatting | bytes 5242880 | tf_op jit(solution)/shard_map/reshape | solution.py:43
  32.4 6.5 %copy.30 = bf16[8,2,10,8192]{3,1,2,0:T(2,128)(2,1)} copy(bf16[8,2,10,8192]{3,2,1,0:T(8,128)(2,1)} %reshape.51) | data formatting | bytes 5242880 | tf_op jit(solution)/shard_map/reshape | solution.py:43
  38.8 0.7 reshape.62
  39.5 7.5 %all-to-all-start.3 = ((bf16[2,2,160]{2,1,0:T(2,128)(2,1)}), bf16[2,2,160]{2,1,0:T(2,128)(2,1)S(1)}, u32[]{:S(2)}, u32[]{:S(2)}) async-start(bf16[2,2,160]{2,1,0:T(2,128)(2,1)} %reshape.62), calls=%async_computation.3 | async-start | bytes 4096 | tf_op jit(solution)/shard_map/all_to_all | solution.py:67
  47.0 0.1 copy.41
  47.1 0.9 all-to-all-done.3
  48.1 3.9 %all_to_all.50 = bf16[8,2,10,1024]{3,0,2,1:T(8,128)(2,1)S(1)} all-to-all(bf16[8,2,10,1024]{3,0,2,1:T(8,128)(2,1)S(1)} %copy.41), channel_id=1, replica_groups=mesh['groups'=2,'fsdp'=8,'tenant'=2] {'tenant'}, dimensions={1} | all-to-all | bytes 655360 | tf_op jit(solution)/shard_map/all_to_all | solution.py:54
  52.0 8.0 %all-to-all-start = ((bf16[8,2,10,8192]{3,1,2,0:T(2,128)(2,1)}), bf16[8,2,10,8192]{3,1,2,0:T(2,128)(2,1)}, u32[]{:S(2)}, u32[]{:S(2)}) async-start(bf16[8,2,10,8192]{3,1,2,0:T(2,128)(2,1)} %copy.30), calls=%async_computation | async-start | bytes 5242880 | tf_op jit(solution)/shard_map/all_to_all | solution.py:42
  60.0 0.1 reshape.63
  60.1 0.1 reshape.61
  60.2 0.1 copy.36
  60.3 0.2 copy.42
  60.6 0.1 reshape.58
  60.7 0.3 fusion.14
  61.0 3.9 %fusion = bf16[160,8192]{1,0:T(8,128)(2,1)} fusion(bf16[160,128]{1,0:T(8,128)(2,1)S(1)} %fusion.14, bf16[1,128,8192]{2,1,0:T(8,128)(2,1)} %param.10), kind=kOutput, calls=%fused_computation.3 | convolution fusion | flops 338165760 | bytes 4759552 | tf_op jit(solution)/shard_map/dot_general | solution.py:103
  64.9 4.7 %reshape.59 = bf16[8,2,10,8192]{3,2,1,0:T(8,128)(2,1)} reshape(bf16[160,8192]{1,0:T(8,128)(2,1)} %fusion) | data formatting | bytes 5242880 | tf_op jit(solution)/shard_map/reshape | solution.py:121
  69.6 6.4 %copy.44 = bf16[8,2,10,8192]{3,1,2,0:T(2,128)(2,1)} copy(bf16[8,2,10,8192]{3,2,1,0:T(8,128)(2,1)} %reshape.59) | data formatting | bytes 5242880 | tf_op jit(solution)/shard_map/reshape | solution.py:121
  76.1 77.0 %all-to-all-done = bf16[8,2,10,8192]{3,1,2,0:T(2,128)(2,1)} async-done(((bf16[8,2,10,8192]{3,1,2,0:T(2,128)(2,1)}), bf16[8,2,10,8192]{3,1,2,0:T(2,128)(2,1)}, u32[]{:S(2)}, u32[]{:S(2)}) %all-to-all-start) | async-done | bytes 2621472 | tf_op jit(solution)/shard_map/all_to_all | solution.py:42
  153.0 4.0 %copy.31 = bf16[8,2,10,8192]{3,0,2,1:T(8,128)(2,1)S(1)} copy(bf16[8,2,10,8192]{3,1,2,0:T(2,128)(2,1)} %all-to-all-done) | data formatting | bytes 5242880 | tf_op jit(solution)/shard_map/all_to_all | solution.py:42
  157.0 12.2 %all_to_all.51 = bf16[8,2,10,8192]{3,0,2,1:T(8,128)(2,1)} all-to-all(bf16[8,2,10,8192]{3,0,2,1:T(8,128)(2,1)S(1)} %copy.31), channel_id=1, replica_groups=mesh['groups'=2,'fsdp'=8,'tenant'=2] {'tenant'}, dimensions={1} | all-to-all | bytes 5242880 | tf_op jit(solution)/shard_map/all_to_all | solution.py:41
  169.2 9.2 %all-to-all-start.8 = ((bf16[8,2,10,8192]{3,1,2,0:T(2,128)(2,1)}), bf16[8,2,10,8192]{3,1,2,0:T(2,128)(2,1)}, u32[]{:S(2)}, u32[]{:S(2)}) async-start(bf16[8,2,10,8192]{3,1,2,0:T(2,128)(2,1)} %copy.44), calls=%async_computation.8 | async-start | bytes 5242880 | tf_op jit(solution)/shard_map/all_to_all | solution.py:120
  178.4 5.4 %copy.32 = bf16[8,2,10,8192]{3,2,1,0:T(8,128)(2,1)} copy(bf16[8,2,10,8192]{3,0,2,1:T(8,128)(2,1)} %all_to_all.51) | data formatting | bytes 5242880 | tf_op jit(solution)/shard_map/all_to_all | solution.py:41
  183.8 4.7 %reshape.52 = bf16[160,8192]{1,0:T(8,128)(2,1)} reshape(bf16[8,2,10,8192]{3,2,1,0:T(8,128)(2,1)} %copy.32) | data formatting | bytes 5242880 | tf_op jit(solution)/shard_map/reshape | solution.py:81
  188.5 3.3 fusion.15
  191.8 0.6 copy-done.7
  192.4 0.2 fusion.7
  192.7 0.1 reshape.55
  192.8 1.1 copy.37
  193.8 110.9 %all-to-all-done.8 = bf16[8,2,10,8192]{3,1,2,0:T(2,128)(2,1)} async-done(((bf16[8,2,10,8192]{3,1,2,0:T(2,128)(2,1)}), bf16[8,2,10,8192]{3,1,2,0:T(2,128)(2,1)}, u32[]{:S(2)}, u32[]{:S(2)}) %all-to-all-start.8) | async-done | bytes 2621472 | tf_op jit(solution)/shard_map/all_to_all | solution.py:120
  304.7 3.2 copy.45
  307.9 6.9 %all_to_all.52 = bf16[8,2,10,8192]{3,0,2,1:T(8,128)(2,1)} all-to-all(bf16[8,2,10,8192]{3,0,2,1:T(8,128)(2,1)S(1)} %copy.45), channel_id=1, replica_groups=mesh['groups'=2,'fsdp'=8,'tenant'=2] {'tenant'}, dimensions={1} | all-to-all | bytes 5242880 | tf_op jit(solution)/shard_map/all_to_all | solution.py:119
  314.9 7.5 %all-to-all-start.4 = ((bf16[8,2,10,1024]{3,1,2,0:T(2,128)(2,1)}), bf16[8,2,10,1024]{3,1,2,0:T(2,128)(2,1)S(1)}, u32[]{:S(2)}, u32[]{:S(2)}) async-start(bf16[8,2,10,1024]{3,1,2,0:T(2,128)(2,1)} %copy.37), calls=%async_computation.4 | async-start | bytes 655360 | tf_op jit(solution)/shard_map/all_to_all | solution.py:107
  322.4 1.0 fusion.10
  323.4 3.8 fusion.3
  327.2 3.6 copy.46
  330.8 4.7 %reshape.60 = bf16[160,8192]{1,0:T(8,128)(2,1)} reshape(bf16[8,2,10,8192]{3,2,1,0:T(8,128)(2,1)} %copy.46) | data formatting | bytes 5242880 | tf_op jit(solution)/shard_map/reshape | solution.py:134
  335.5 0.7 all-to-all-done.4
  336.2 0.1 copy.38
  336.3 4.9 %all_to_all.53 = bf16[8,2,10,1024]{3,0,2,1:T(8,128)(2,1)S(1)} all-to-all(bf16[8,2,10,1024]{3,0,2,1:T(8,128)(2,1)S(1)} %copy.38), channel_id=1, replica_groups=mesh['groups'=2,'fsdp'=8,'tenant'=2] {'tenant'}, dimensions={1} | all-to-all | bytes 655360 | tf_op jit(solution)/shard_map/all_to_all | solution.py:106
  341.2 0.2 copy.39
  341.4 0.1 reshape.56
  341.5 10.1 %all-gather.2.cloned.1.call-done = bf16[8192,1024]{1,0:T(8,128)(2,1)} async-done(((bf16[1024,1024]{1,0:T(8,128)(2,1)}), bf16[8192,1024]{1,0:T(8,128)(2,1)}) %all-gather.2.cloned.1.call-update) | async-done | bytes 16777232 | tf_op jit(solution)/shard_map/all_gather | solution.py:155
  351.6 13.3 %fusion.28 = f32[128,8192]{1,0:T(8,128)} fusion(bf16[128,1024]{1,0:T(8,128)(2,1)S(1)} %copy-done.2, bf16[8192,1024]{1,0:T(8,128)(2,1)} %all-gather.2.cloned.1.call-done), kind=kOutput, calls=%fused_computation.47 | convolution fusion | flops 2147483648 | bytes 21233664 | tf_op jit(solution)/shard_map/dot_general | solution.py:158
  364.8 5.1 %fusion.1 = bf16[128,8192]{1,0:T(8,128)(2,1)} fusion(f32[128,8192]{1,0:T(8,128)} %fusion.28, bf16[160,8192]{1,0:T(8,128)(2,1)} %reshape.60, s32[128]{0:T(128)S(1)} %copy-done.10), kind=kOutput, calls=%fused_computation.5 | convolution fusion | flops 337661952 | bytes 8913408 | tf_op jit(solution)/shard_map/dot_general | solution.py:167
  369.9 8.1 %fusion.27 = f32[128,1024]{1,0:T(8,128)S(1)} fusion(bf16[128,8192]{1,0:T(8,128)(2,1)S(1)} %copy-done, bf16[8192,1024]{1,0:T(8,128)(2,1)} %all-gather.2.cloned.1.call-done), kind=kOutput, calls=%fused_computation.46 | convolution fusion | flops 2147483648 | bytes 19398656 | tf_op jit(solution)/shard_map/dot_general | solution.py:153
  378.0 1.0 fusion.8
  (25 shorter events, 0.1 us)
Async XLA Ops:
  7.2 18.2 %copy-start = (bf16[128,8192]{1,0:T(8,128)(2,1)S(1)}, bf16[128,8192]{1,0:T(8,128)(2,1)}, u32[]{:S(2)}) copy-start(bf16[128,8192]{1,0:T(8,128)(2,1)} %param.7) | copy-start | bytes 6291460
  7.2 9.4 %copy-start.2 = (bf16[128,1024]{1,0:T(8,128)(2,1)S(1)}, bf16[128,1024]{1,0:T(8,128)(2,1)}, u32[]{:S(2)}) copy-start(bf16[128,1024]{1,0:T(8,128)(2,1)} %param.8) | copy-start | bytes 786436
  7.2 344.4 %all-gather.2.cloned.1.call-start = ((), (), s32[]{:S(2)}) async-start(), calls=%async_computation.10 | async-start | bytes 18874368 | tf_op jit(solution)/shard_map/all_gather | solution.py:155
  9.9 17.8 %copy-start.9 = (s32[128]{0:T(128)}, s32[128]{0:T(128)S(1)}, u32[]{:S(2)}) copy-start(s32[128]{0:T(128)S(1)} %multiply_add_fusion) | copy-start | bytes 1540
  10.9 9.0 %all-to-all-start.2 = ((bf16[8,2,10,4]{2,1,3,0:T(2,128)(2,1)}), bf16[8,2,10,4]{2,1,3,0:T(2,128)(2,1)S(1)}, u32[]{:S(2)}, u32[]{:S(2)}) async-start(bf16[8,2,10,4]{2,1,3,0:T(2,128)(2,1)} %copy.33), calls=%async_computation.2 | async-start | bytes 32768 | tf_op jit(solution)/shard_map/all_to_all | solution.py:68
  19.9 19.6 %all-to-all-start.6 = ((bf16[8,2,10,1024]{3,1,2,0:T(2,128)(2,1)}), bf16[8,2,10,1024]{3,1,2,0:T(2,128)(2,1)S(1)}, u32[]{:S(2)}, u32[]{:S(2)}) async-start(bf16[8,2,10,1024]{3,1,2,0:T(2,128)(2,1)} %copy.40), calls=%async_computation.6 | async-start | bytes 655360 | tf_op jit(solution)/shard_map/all_to_all | solution.py:55
  39.5 8.5 %all-to-all-start.3 = ((bf16[2,2,160]{2,1,0:T(2,128)(2,1)}), bf16[2,2,160]{2,1,0:T(2,128)(2,1)S(1)}, u32[]{:S(2)}, u32[]{:S(2)}) async-start(bf16[2,2,160]{2,1,0:T(2,128)(2,1)} %reshape.62), calls=%async_computation.3 | async-start | bytes 4096 | tf_op jit(solution)/shard_map/all_to_all | solution.py:67
  52.0 8.7 %copy-start.3 = (bf16[1,128,1024]{2,1,0:T(8,128)(2,1)S(1)}, bf16[1,128,1024]{2,1,0:T(8,128)(2,1)}, u32[]{:S(2)}) copy-start(bf16[1,128,1024]{2,1,0:T(8,128)(2,1)} %param.11) | copy-start | bytes 786436
  52.0 101.0 %all-to-all-start = ((bf16[8,2,10,8192]{3,1,2,0:T(2,128)(2,1)}), bf16[8,2,10,8192]{3,1,2,0:T(2,128)(2,1)}, u32[]{:S(2)}, u32[]{:S(2)}) async-start(bf16[8,2,10,8192]{3,1,2,0:T(2,128)(2,1)} %copy.30), calls=%async_computation | async-start | bytes 5242880 | tf_op jit(solution)/shard_map/all_to_all | solution.py:42
  60.9 8.7 %copy-start.5 = (bf16[160,128]{1,0:T(8,128)(2,1)}, bf16[160,128]{1,0:T(8,128)(2,1)S(1)}, u32[]{:S(2)}) copy-start(bf16[160,128]{1,0:T(8,128)(2,1)S(1)} %fusion.14) | copy-start | bytes 122884
  169.2 135.5 %all-to-all-start.8 = ((bf16[8,2,10,8192]{3,1,2,0:T(2,128)(2,1)}), bf16[8,2,10,8192]{3,1,2,0:T(2,128)(2,1)}, u32[]{:S(2)}, u32[]{:S(2)}) async-start(bf16[8,2,10,8192]{3,1,2,0:T(2,128)(2,1)} %copy.44), calls=%async_computation.8 | async-start | bytes 5242880 | tf_op jit(solution)/shard_map/all_to_all | solution.py:120
  188.5 3.9 %copy-start.4 = (bf16[1,128,1024]{2,1,0:T(8,128)(2,1)S(1)}, bf16[1,128,1024]{2,1,0:T(8,128)(2,1)}, u32[]{:S(2)}) copy-start(bf16[1,128,1024]{2,1,0:T(8,128)(2,1)} %param.11) | copy-start | bytes 786436
  191.8 0.6 copy-start.7
  307.9 14.5 %copy-start.8 = (bf16[160,128]{1,0:T(8,128)(2,1)S(1)}, bf16[160,128]{1,0:T(8,128)(2,1)}, u32[]{:S(2)}) copy-start(bf16[160,128]{1,0:T(8,128)(2,1)} %copy-done.7) | copy-start | bytes 122884
  307.9 15.5 %copy-start.6 = (bf16[160,128]{1,0:T(8,128)(2,1)S(1)}, bf16[160,128]{1,0:T(8,128)(2,1)}, u32[]{:S(2)}) copy-start(bf16[160,128]{1,0:T(8,128)(2,1)} %copy-done.5) | copy-start | bytes 122884
  314.9 21.3 %all-to-all-start.4 = ((bf16[8,2,10,1024]{3,1,2,0:T(2,128)(2,1)}), bf16[8,2,10,1024]{3,1,2,0:T(2,128)(2,1)S(1)}, u32[]{:S(2)}, u32[]{:S(2)}) async-start(bf16[8,2,10,1024]{3,1,2,0:T(2,128)(2,1)} %copy.37), calls=%async_computation.4 | async-start | bytes 655360 | tf_op jit(solution)/shard_map/all_to_all | solution.py:107
  322.4 4.8 %copy-start.1 = (bf16[8,2,10,8192]{3,0,2,1:T(8,128)(2,1)S(1)}, bf16[8,2,10,8192]{3,0,2,1:T(8,128)(2,1)}, u32[]{:S(2)}) copy-start(bf16[8,2,10,8192]{3,0,2,1:T(8,128)(2,1)} %all_to_all.52) | copy-start | bytes 7864324
  341.5 23.4 %copy-start.10 = (s32[128]{0:T(128)S(1)}, s32[128]{0:T(128)}, u32[]{:S(2)}) copy-start(s32[128]{0:T(128)} %copy-done.9) | copy-start | bytes 1540
Sparse Core Ops, SparseCore 0:
  10.2 341.3 all-gather.1
where the time goes:
time: 392 us; the launch traced here: 386 us
  waiting for transfers between devices  202 us (52%)
  local copies, waits for them, and re-layouts  53.5 us (14%)
  starting transfers between devices  43.3 us (11%)
  matrix products  42.7 us (11%)
  blocking collectives  28 us (7%)
  between operations  14.3 us (4%)
    all_to_all x1, waiting for transfers between devices, on_device(): lax.all_to_all(adapter_backward.reshape(fsdp_size, tenant_size, capacity,...  111 us
    all_to_all x1, waiting for transfers between devices, on_device(): lax.all_to_all(send_tokens.reshape(fsdp_size, tenant_size, capacity, widt...  77 us
    dot_general x1, matrix products, on_device(): lax.dot_general(grad_out, lax.all_gather(base_weight, 'fsdp', axis=0, til...  13.3 us
    all_to_all x1, blocking collectives, on_device(): lax.all_to_all(lax.all_to_all(send_tokens.reshape(fsdp_size, tenant_size,...  12.2 us
    reshape x2, local copies, waits for them, and re-layouts, on_device(): send_tokens.reshape(fsdp_size, tenant_size, capacity, width)  11.2 us
    reshape x2, local copies, waits for them, and re-layouts, on_device(): adapter_backward.reshape(fsdp_size, tenant_size, capacity, width)  11.1 us
    all_gather x1, waiting for transfers between devices, on_device(): lax.all_gather(base_weight, 'fsdp', axis=0, tiled=True)  10.1 us
    all_to_all x1, starting transfers between devices, on_device(): lax.all_to_all(adapter_backward.reshape(fsdp_size, tenant_size, capacity,...  9.2 us
  transfers between devices with their start and end apart: 7, of which 6 were waited for; matrix products, arithmetic and copies ran while one was open for 18% of the time, Pallas kernels for 0%

commit v1 on v0

v1 whole, which is shorter than its diff:
```python
import functools

import jax
import jax.numpy as jnp
from jax import lax
from jax.experimental import pallas as pl
from jax.experimental.pallas import tpu as pltpu
from jax.sharding import PartitionSpec as P

RANK = 32
CHUNKS = 8
VMEM_LIMIT = 48 * 1024 * 1024

adapter_scale = 2.0

F32 = jnp.float32
BF16 = jnp.bfloat16
NT = (((1,), (1,)), ((), ()))
TN = (((0,), (0,)), ((), ()))


def iota(shape, dim):
    return lax.broadcasted_iota(jnp.int32, shape, dim)


def piece_and_slot(index, cap):
    piece = jnp.zeros_like(index)
    for k in range(1, CHUNKS + 1):
        piece = piece + (index >= k * cap).astype(jnp.int32)
    return piece, index - piece * cap


def spread_mask(rows, cap, lanes):
    block = CHUNKS * cap
    piece, _ = piece_and_slot(iota((block, CHUNKS * lanes), 0), cap)
    group = jnp.zeros_like(piece)
    lane = iota(piece.shape, 1)
    for k in range(1, CHUNKS):
        group = group + (lane >= k * lanes).astype(jnp.int32)
    mask = (piece == group).astype(F32).astype(BF16)
    return jnp.concatenate([mask] * (rows // block), axis=0)


def spread(rows, cap):
    return jnp.concatenate([rows] * CHUNKS, axis=1) * spread_mask(
        rows.shape[0], cap, rows.shape[1]
    )


def pick_piece(wide, cap, height, lanes):
    n = wide.shape[0]
    piece, _ = piece_and_slot(iota((height, lanes), 0), cap)
    piece = jnp.concatenate([piece] * (n // height), axis=0)
    total = jnp.zeros((n, lanes), F32)
    for k in range(CHUNKS):
        total = total + jnp.where(piece == k, wide[:, k * lanes : (k + 1) * lanes], 0.0)
    return total


def same_slot(cap, columns):
    shape = (CHUNKS * cap, columns)
    _, slot = piece_and_slot(iota(shape, 0), cap)
    piece_c, slot_c = piece_and_slot(iota(shape, 1), cap)
    return ((slot == slot_c) & (piece_c < CHUNKS)).astype(F32)


def mask_of_slot(cap, columns):
    shape = (CHUNKS * cap, columns)
    _, slot = piece_and_slot(iota(shape, 0), cap)
    return (iota(shape, 1) == CHUNKS * cap + slot).astype(F32)


def load_pieces(src, dst, sem, height, width):
    copies = [
        pltpu.make_async_copy(
            src.at[:, pl.ds(k * width, width)], dst.at[pl.ds(k * height, height), :], sem.at[k]
        )
        for k in range(CHUNKS)
    ]
    for copy in copies:
        copy.start()
    for copy in copies:
        copy.wait()


def route_kernel(
    devices, cap, per_page, owner_ref, tenant_ref, grads_ref, send_ref, row_ref, col_ref
):
    rows = tenant_ref.shape[1]
    block = CHUNKS * cap
    height = send_ref.shape[1]
    width = send_ref.shape[2]
    tenant = tenant_ref[...]
    page = tenant // per_page
    member = tenant - page * per_page

    def add_page(p, target):
        return target + jnp.where(page == p, owner_ref[p], 0)

    target = lax.fori_loop(0, owner_ref.shape[0], add_page, jnp.zeros_like(page))
    chosen = (iota((devices, rows), 0) == target).astype(F32)
    earlier = (iota((rows, rows), 0) < iota((rows, rows), 1)).astype(F32)
    before = jnp.dot(chosen.astype(BF16), earlier.astype(BF16), preferred_element_type=F32)
    slot = target.astype(F32) * cap + jnp.sum(before * chosen, axis=0, keepdims=True)
    row_ref[...] = slot
    col_ref[...] = jnp.transpose(jnp.broadcast_to(slot, (rows, rows)))

    member_mask = (iota((width, rows), 0) // RANK == member).astype(F32).astype(BF16)
    pieces = jnp.concatenate(
        [grads_ref[:, k * width : (k + 1) * width] for k in range(CHUNKS)], axis=0
    )
    _, slot_of = piece_and_slot(iota((block, rows), 0), cap)
    tail = iota((height - block, rows), 0)
    tail = jnp.where(tail < cap, tail, -(10**6))
    for d in range(devices):
        here = (slot == (slot_of + d * cap).astype(F32)).astype(F32).astype(BF16)
        send_ref[d, 0:block, :] = jnp.dot(
            spread(here, cap), pieces, preferred_element_type=F32
        ).astype(BF16)
        here = (slot == (tail + d * cap).astype(F32)).astype(F32).astype(BF16)
        send_ref[d, block:height, :] = lax.dot_general(
            here, member_mask, NT, preferred_element_type=F32
        ).astype(BF16)


def dispatch_kernel(cap, slot_ref, tokens_ref, out_ref, pieces, sem):
    step = pl.program_id(0)
    rows = slot_ref.shape[1]
    width = pieces.shape[1]
    block = CHUNKS * cap

    @pl.when(step == 0)
    def _():
        load_pieces(tokens_ref, pieces, sem, rows, width)

    group = out_ref.shape[0] // block
    _, slot_of = piece_and_slot(iota((block, rows), 0), cap)
    slot = slot_ref[...]
    here = jnp.concatenate(
        [
            (slot == (slot_of + (step * group + d) * cap).astype(F32)).astype(F32).astype(BF16)
            for d in range(group)
        ],
        axis=0,
    )
    out_ref[...] = jnp.dot(spread(here, cap), pieces[...], preferred_element_type=F32).astype(BF16)


def back_kernel(cap, got_ref, b_ref, a_ref, back_ref, rank_ref, mask_ref, pieces, sem):
    step = pl.program_id(0)
    ranks = b_ref.shape[0]
    group, height, width = got_ref.shape
    block = CHUNKS * cap

    @pl.when(step == 0)
    def _():
        load_pieces(a_ref, pieces, sem, ranks, pieces.shape[1])

    b_pieces = jnp.concatenate(
        [b_ref[:, k * width : (k + 1) * width] for k in range(CHUNKS)], axis=0
    )
    fold = same_slot(cap, height)
    member = mask_of_slot(cap, height).astype(BF16)
    ranks_of = []
    for d in range(group):
        got = got_ref[d]
        wide = lax.dot_general(got, b_pieces, NT, preferred_element_type=F32)
        part = pick_piece(wide, cap, height, ranks)
        full = jnp.dot(fold, part, precision=lax.Precision.HIGHEST, preferred_element_type=F32)
        mask = jnp.dot(member, got, preferred_element_type=F32)
        ranks_of.append((full * mask).astype(BF16))
        mask_ref[d * block : (d + 1) * block, :] = mask.astype(BF16)
    rank_rows = jnp.concatenate(ranks_of, axis=0)
    rank_ref[...] = rank_rows
    back_ref[...] = (
        adapter_scale * jnp.dot(spread(rank_rows, cap), pieces[...], preferred_element_type=F32)
    ).astype(BF16)


def forth_kernel(cap, got_ref, mask_ref, a_ref, b_ref, out_ref, rank_ref, pieces, sem):
    step = pl.program_id(0)
    ranks = b_ref.shape[0]
    block = CHUNKS * cap
    width = out_ref.shape[1]
    group = got_ref.shape[0] // block

    @pl.when(step == 0)
    def _():
        load_pieces(a_ref, pieces, sem, ranks, pieces.shape[1])

    b_pieces = jnp.concatenate(
        [b_ref[:, k * width : (k + 1) * width] for k in range(CHUNKS)], axis=0
    )
    wide = lax.dot_general(got_ref[...], pieces[...], NT, preferred_element_type=F32)
    part = pick_piece(wide, cap, block, ranks)
    fold = same_slot(cap, block)
    full = jnp.concatenate(
        [
            jnp.dot(
                fold,
                part[d * block : (d + 1) * block, :],
                precision=lax.Precision.HIGHEST,
                preferred_element_type=F32,
            )
            for d in range(group)
        ],
        axis=0,
    )
    rank_rows = (full * mask_ref[...].astype(F32)).astype(BF16)
    rank_ref[...] = rank_rows
    out_ref[...] = (
        adapter_scale * jnp.dot(spread(rank_rows, cap), b_pieces, preferred_element_type=F32)
    ).astype(BF16)


def page_grad_kernel(cap, tok_ref, grad_ref, low_ref, rank_ref, ga_ref, gb_ref):
    ranks = rank_ref.shape[1]
    block = CHUNKS * cap
    wide = tok_ref.shape[1]
    narrow = grad_ref.shape[2]
    left = lax.dot_general(
        spread(rank_ref[...], cap), tok_ref[...], TN, preferred_element_type=F32
    )
    grads = jnp.concatenate(
        [grad_ref[d, 0:block, :] for d in range(grad_ref.shape[0])], axis=0
    )
    right = lax.dot_general(spread(low_ref[...], cap), grads, TN, preferred_element_type=F32)
    for k in range(CHUNKS):
        ga_ref[:, k * wide : (k + 1) * wide] = (
            adapter_scale * left[k * ranks : (k + 1) * ranks, :]
        ).astype(BF16)
        gb_ref[:, k * narrow : (k + 1) * narrow] = (
            adapter_scale * right[k * ranks : (k + 1) * ranks, :]
        ).astype(BF16)


def base_kernel(tok_ref, grad_ref, w_ref, out_ref, back_ref):
    @pl.when(pl.program_id(0) == 0)
    def _():
        out_ref[...] = jnp.zeros_like(out_ref)

    weight = w_ref[...]
    out_ref[...] += jnp.dot(tok_ref[...], weight, preferred_element_type=F32)
    back_ref[...] = lax.dot_general(grad_ref[...], weight, NT, preferred_element_type=F32)


def own_slots(col, cap, total, piece):
    block = CHUNKS * cap
    rows = col.shape[0]
    piece_of, slot_of = piece_and_slot(iota((rows, block), 1), cap)
    key = jnp.where(piece_of == piece, slot_of, -(10**6))
    parts = []
    for d in range(total // block):
        parts.append((col == (key + d * cap).astype(F32)).astype(F32).astype(BF16))
    return jnp.concatenate(parts, axis=1)


def combine_back_kernel(cap, col_ref, got_ref, base_ref, out_ref):
    here = own_slots(col_ref[:, 0:1], cap, got_ref.shape[0], pl.program_id(0))
    rows = jnp.dot(here, got_ref[...], preferred_element_type=F32)
    out_ref[...] = (base_ref[...] + rows).astype(BF16)


def combine_out_kernel(cap, col_ref, got_ref, base_ref, out_ref):
    width = got_ref.shape[1]
    for k in range(CHUNKS):
        here = own_slots(col_ref[:, 0:1], cap, got_ref.shape[0], k)
        rows = jnp.dot(here, got_ref[...], preferred_element_type=F32)
        at = slice(k * width, (k + 1) * width)
        out_ref[:, at] = (base_ref[:, at] + rows).astype(BF16)


def whole(shape):
    return pl.BlockSpec(shape, lambda *_: (0,) * len(shape))


def params(semantics=None):
    return pltpu.CompilerParams(vmem_limit_bytes=VMEM_LIMIT, dimension_semantics=semantics)


def cost(flops, nbytes):
    return pl.CostEstimate(flops=int(flops), bytes_accessed=int(nbytes), transcendentals=0)


def on_device(tokens, grad_out, base_weight, page_a, page_b, page_owner, row_tenant):
    rows, width = tokens.shape
    narrow = grad_out.shape[1]
    fsdp_size = lax.axis_size("fsdp")
    tenant_size = lax.axis_size("tenant")
    group_size = lax.axis_size("groups")
    devices = fsdp_size * tenant_size
    cap = max(4, 4 * rows // (3 * devices))
    per_page = page_a.shape[1] // RANK
    ranks = page_a.shape[1]
    block = CHUNKS * cap
    total = devices * block
    height = block + -(-cap // 16) * 16
    wp, np_ = width // CHUNKS, narrow // CHUNKS
    left_factor, right_factor = page_a[0], page_b[0]
    axes = ("fsdp", "tenant")

    def exchange(x):
        return lax.all_to_all(x, axes, split_axis=0, concat_axis=0, tiled=True)

    any_spec = pl.BlockSpec(memory_space=pl.ANY)

    shares = group_size * tenant_size
    share = base_weight.shape[0] // shares
    which = lax.axis_index("groups") * tenant_size + lax.axis_index("tenant")
    mine = lax.dynamic_slice_in_dim(base_weight, which * share, share, 0)
    weight = lax.all_gather(mine, ("fsdp", "groups", "tenant"), axis=0, tiled=True)

    send_grads, slot_row, slot_col = pl.pallas_call(
        functools.partial(route_kernel, devices, cap, per_page),
        out_shape=(
            jax.ShapeDtypeStruct((devices, height, np_), BF16),
            jax.ShapeDtypeStruct((1, rows), F32),
            jax.ShapeDtypeStruct((rows, rows), F32),
        ),
        in_specs=[
            pl.BlockSpec(memory_space=pltpu.SMEM),
            pl.BlockSpec(memory_space=pltpu.VMEM),
            pl.BlockSpec(memory_space=pltpu.VMEM),
        ],
        out_specs=tuple(pl.BlockSpec(memory_space=pltpu.VMEM) for _ in range(3)),
        compiler_params=params(),
        cost_estimate=cost(2 * total * rows * narrow, 2 * total * np_ * 2),
        name="route",
    )(page_owner, row_tenant.reshape(1, rows), grad_out)
    got_grads = exchange(send_grads)

    steps = 4 if devices % 4 == 0 else 1
    part = total // steps
    send_tokens = pl.pallas_call(
        functools.partial(dispatch_kernel, cap),
        out_shape=jax.ShapeDtypeStruct((total, wp), BF16),
        grid=(steps,),
        in_specs=[whole((1, rows)), any_spec],
        out_specs=pl.BlockSpec((part, wp), lambda i: (i, 0)),
        scratch_shapes=[
            pltpu.VMEM((CHUNKS * rows, wp), BF16),
            pltpu.SemaphoreType.DMA((CHUNKS,)),
        ],
        compiler_params=params(("arbitrary",)),
        cost_estimate=cost(2 * total * rows * width, 2 * (total * wp + rows * width)),
        name="dispatch",
    )(slot_row, tokens)
    got_tokens = exchange(send_tokens.reshape(devices, block, wp)).reshape(total, wp)

    back, rank_rows, mask_rows = pl.pallas_call(
        functools.partial(back_kernel, cap),
        out_shape=(
            jax.ShapeDtypeStruct((total, wp), BF16),
            jax.ShapeDtypeStruct((total, ranks), BF16),
            jax.ShapeDtypeStruct((total, ranks), BF16),
        ),
        grid=(steps,),
        in_specs=[
            pl.BlockSpec((devices // steps, height, np_), lambda i: (i, 0, 0)),
            whole((ranks, narrow)),
            any_spec,
        ],
        out_specs=(
            pl.BlockSpec((part, wp), lambda i: (i, 0)),
            pl.BlockSpec((part, ranks), lambda i: (i, 0)),
            pl.BlockSpec((part, ranks), lambda i: (i, 0)),
        ),
        scratch_shapes=[
            pltpu.VMEM((CHUNKS * ranks, wp), BF16),
            pltpu.SemaphoreType.DMA((CHUNKS,)),
        ],
        compiler_params=params(("arbitrary",)),
        cost_estimate=cost(2 * total * ranks * width, 2 * (total * wp + ranks * width)),
        name="rank_grad_back",
    )(got_grads, right_factor, left_factor)
    got_back = exchange(back.reshape(devices, block, wp)).reshape(total, wp)

    out_packed, low_rows = pl.pallas_call(
        functools.partial(forth_kernel, cap),
        out_shape=(
            jax.ShapeDtypeStruct((total, np_), BF16),
            jax.ShapeDtypeStruct((total, ranks), BF16),
        ),
        grid=(steps,),
        in_specs=[
            pl.BlockSpec((part, wp), lambda i: (i, 0)),
            pl.BlockSpec((part, ranks), lambda i: (i, 0)),
            any_spec,
            whole((ranks, narrow)),
        ],
        out_specs=(
            pl.BlockSpec((part, np_), lambda i: (i, 0)),
            pl.BlockSpec((part, ranks), lambda i: (i, 0)),
        ),
        scratch_shapes=[
            pltpu.VMEM((CHUNKS * ranks, wp), BF16),
            pltpu.SemaphoreType.DMA((CHUNKS,)),
        ],
        compiler_params=params(("arbitrary",)),
        cost_estimate=cost(2 * total * ranks * width, 2 * (total * wp + ranks * width)),
        name="lowrank_out",
    )(got_tokens, mask_rows, left_factor, right_factor)
    got_out = exchange(out_packed.reshape(devices, block, np_)).reshape(total, np_)

    grad_a, grad_b = pl.pallas_call(
        functools.partial(page_grad_kernel, cap),
        out_shape=(
            jax.ShapeDtypeStruct((ranks, width), BF16),
            jax.ShapeDtypeStruct((ranks, narrow), BF16),
        ),
        compiler_params=params(),
        cost_estimate=cost(2 * total * ranks * width, 2 * (total * wp + ranks * width)),
        name="page_grads",
    )(got_tokens, got_grads, low_rows, rank_rows)

    base_out, base_back = pl.pallas_call(
        base_kernel,
        out_shape=(
            jax.ShapeDtypeStruct((rows, narrow), F32),
            jax.ShapeDtypeStruct((rows, width), F32),
        ),
        grid=(CHUNKS,),
        in_specs=[
            pl.BlockSpec((rows, wp), lambda i: (0, i)),
            whole((rows, narrow)),
            pl.BlockSpec((wp, narrow), lambda i: (i, 0)),
        ],
        out_specs=(whole((rows, narrow)), pl.BlockSpec((rows, wp), lambda i: (0, i))),
        compiler_params=params(("arbitrary",)),
        cost_estimate=cost(4 * rows * width * narrow, 2 * width * narrow),
        name="base",
    )(tokens, grad_out, weight)

    projected = pl.pallas_call(
        functools.partial(combine_out_kernel, cap),
        out_shape=jax.ShapeDtypeStruct((rows, narrow), BF16),
        compiler_params=params(),
        cost_estimate=cost(2 * rows * total * narrow, 2 * total * np_),
        name="combine_out",
    )(slot_col, got_out, base_out)

    grad_tokens = pl.pallas_call(
        functools.partial(combine_back_kernel, cap),
        out_shape=jax.ShapeDtypeStruct((rows, width), BF16),
        grid=(CHUNKS,),
        in_specs=[
            whole((rows, rows)),
            whole((total, wp)),
            pl.BlockSpec((rows, wp), lambda i: (0, i)),
        ],
        out_specs=pl.BlockSpec((rows, wp), lambda i: (0, i)),
        compiler_params=params(("arbitrary",)),
        cost_estimate=cost(2 * rows * total * width, 2 * total * wp + 6 * rows * width),
        name="combine_back",
    )(slot_col, got_back, base_back)

    return projected, grad_tokens, grad_a[None], grad_b[None]


def solution(mesh):
    rows = P(("groups", "fsdp", "tenant"), None)
    pages = P(("groups", "fsdp", "tenant"), None, None)
    return jax.shard_map(
        on_device,
        mesh=mesh,
        in_specs=(
            rows,
            rows,
            P("fsdp", None),
            pages,
            pages,
            P("groups"),
            P(("groups", "fsdp", "tenant")),
        ),
        out_specs=(rows, rows, pages, pages),
        check_vma=False,
    )
```

time: 392 us -> 269 us (0.69); the launches traced: 386 us -> 267 us
  Pallas kernels: 0 us -> 55.4 us
  waiting for transfers between devices: 202 us -> 159 us
  matrix products: 42.7 us -> 0 us
  local copies, waits for them, and re-layouts: 53.5 us -> 14.9 us
  blocking collectives: 28 us -> 0 us
  starting transfers between devices: 43.3 us -> 23.7 us
    pallas_call x0 -> x8, Pallas kernels: none -> 55.4 us  [the longest x1 13.9 us: on_device(): pl.pallas_call(base_kernel, out_shape=(jax.ShapeDtypeStruct((rows, narrow...]
    dot_general x13 -> x0, matrix products: 42.7 us -> none  [the longest x1 13.3 us: on_device(): lax.dot_general(grad_out, lax.all_gather(base_weight, 'fsdp', axis=0, til...]
    reshape x15 -> x0, local copies, waits for them, and re-layouts: 35.2 us -> none  [the longest x2 11.2 us: on_device(): send_tokens.reshape(fsdp_size, tenant_size, capacity, width)]
    all_to_all x6 -> x4, waiting for transfers between devices: 191 us -> 159 us  [exchange(): return lax.all_to_all(x, axes, split_axis=0, concat_axis=0, tiled=True)]
    all_to_all x4 -> x0, blocking collectives: 28 us -> none  [the longest x1 12.2 us: on_device(): lax.all_to_all(lax.all_to_all(send_tokens.reshape(fsdp_size, tenant_size,...]
    all_to_all x6 -> x4, starting transfers between devices: 43.3 us -> 23.6 us  [exchange(): return lax.all_to_all(x, axes, split_axis=0, concat_axis=0, tiled=True)]
    all_to_all x9 -> x0, local copies, waits for them, and re-layouts: 16.8 us -> none  [the longest x1 5.36 us: on_device(): lax.all_to_all(lax.all_to_all(send_tokens.reshape(fsdp_size, tenant_size,...]
    unnamed x24 -> x28, local copies, waits for them, and re-layouts: 1.43 us -> 14 us
  transfers between devices with their start and end apart: 7 -> 5, of which waited for: 6 -> 3; matrix products, arithmetic and copies ran while one was open for 18% -> 0% of each run, Pallas kernels for 0% -> 20%
where the time goes in v1:
time: 269 us; the launch traced here: 267 us
  waiting for transfers between devices  159 us (59%)
  Pallas kernels  55.4 us (21%)
  starting transfers between devices  23.7 us (9%)
  local copies, waits for them, and re-layouts  14.9 us (6%)
  between operations  14.2 us (5%)
    all_to_all x4, waiting for transfers between devices, exchange(): return lax.all_to_all(x, axes, split_axis=0, concat_axis=0, tiled=True)  159 us
    all_to_all x4, starting transfers between devices, exchange(): return lax.all_to_all(x, axes, split_axis=0, concat_axis=0, tiled=True)  23.6 us
    unnamed x28, local copies, waits for them, and re-layouts  14 us
    pallas_call x1, Pallas kernels, on_device(): pl.pallas_call(base_kernel, out_shape=(jax.ShapeDtypeStruct((rows, narrow...  13.9 us
    pallas_call x1, Pallas kernels, on_device(): pl.pallas_call(functools.partial(combine_back_kernel, cap), out_shape=jax...  9.43 us
    pallas_call x1, Pallas kernels, on_device(): pl.pallas_call(functools.partial(forth_kernel, cap), out_shape=(jax.Shape...  8.72 us
    pallas_call x1, Pallas kernels, on_device(): pl.pallas_call(functools.partial(back_kernel, cap), out_shape=(jax.ShapeD...  7.91 us
    pallas_call x1, Pallas kernels, on_device(): pl.pallas_call(functools.partial(page_grad_kernel, cap), out_shape=(jax.S...  6.76 us
  transfers between devices with their start and end apart: 5, of which 3 were waited for; matrix products, arithmetic and copies ran while one was open for 0% of the time, Pallas kernels for 20%

profile of v1, /device:TPU:13, one launch (start us, length us, event | category | flops | bytes accessed | tf_op | source)
XLA Modules:
  0.0 267.4 jit_solution(8861511139507163067)
XLA Ops:
  7.2 0.0 copy-start
  7.2 0.0 all-gather.2.cloned.1.call-start
  7.2 1.5 copy-done
  8.8 0.8 constant_dynamic-slice_fusion
  9.6 0.0 all-gather.2.cloned.1.call-update
  9.6 0.0 copy-start.5
  9.6 0.9 copy-done.5
  10.6 0.0 copy-start.10
  10.6 0.7 copy-done.10
  11.2 0.0 copy-start.11
  11.2 0.7 copy-done.11
  11.9 2.6 route.1
  14.5 6.6 %all-to-all-start.1 = ((bf16[16,96,128]{2,1,0:T(8,128)(2,1)}), bf16[16,96,128]{2,1,0:T(8,128)(2,1)S(1)}, u32[]{:S(2)}, u32[]{:S(2)}) async-start(bf16[16,96,128]{2,1,0:T(8,128)(2,1)} %get-tuple-element.18), calls=%async_computation.1 | async-start | bytes 786432 | tf_op jit(solution)/shard_map/all_to_all | solution.py:303
  21.0 0.0 copy-start.3
  21.0 1.7 copy-done.3
  22.8 3.6 %dispatch.1 = bf16[1280,1024]{1,0:T(8,128)(2,1)S(1)} custom-call(f32[1,128]{1,0:T(1,128)S(1)} %get-tuple-element.17.slot_ref, bf16[128,8192]{1,0:T(8,128)(2,1)S(1)} %copy-done.3), custom_call_target="tpu_custom_call" | custom-call | flops 2684354560 | bytes 4718592 | tf_op jit(solution)/shard_map/dispatch/pallas_call | solution.py:334
  26.4 0.0 copy-start.2
  26.4 1.5 copy-done.2
  27.9 12.3 %all-to-all-done.1.got_ref.grad_ref = bf16[16,96,128]{2,1,0:T(8,128)(2,1)S(1)} async-done(((bf16[16,96,128]{2,1,0:T(8,128)(2,1)}), bf16[16,96,128]{2,1,0:T(8,128)(2,1)S(1)}, u32[]{:S(2)}, u32[]{:S(2)}) %all-to-all-start.1) | async-done | bytes 393248 | tf_op jit(solution)/shard_map/all_to_all | solution.py:303
  40.3 0.0 copy-start.9
  40.3 4.9 %all-to-all-start = ((bf16[16,80,1024]{2,1,0:T(8,128)(2,1)}), bf16[16,80,1024]{2,1,0:T(8,128)(2,1)}, u32[]{:S(2)}, u32[]{:S(2)}) async-start(bf16[16,80,1024]{2,1,0:T(8,128)(2,1)} %bitcast.12), calls=%async_computation | async-start | bytes 5242880 | tf_op jit(solution)/shard_map/all_to_all | solution.py:303
  45.2 0.0 copy-done.9
  45.2 0.0 copy-start.7
  45.2 1.6 copy-done.7
  46.8 7.9 %rank_grad_back.1 = (bf16[1280,1024]{1,0:T(8,128)(2,1)S(1)}, bf16[1280,128]{1,0:T(8,128)(2,1)S(1)}, bf16[1280,128]{1,0:T(8,128)(2,1)S(1)}) custom-call(bf16[16,96,128]{2,1,0:T(8,128)(2,1)S(1)} %all-to-all-done.1.got_ref.grad_ref, bf16[128,1024]{1,0:T(8,128)(2,1)S(1)} %bitcast.16, bf16[128,8192]{1,0:T(8,128)(2,1)S(1)} %bitcast.14), custom_call_target="tpu_custom_call" | custom-call | flops 2684354560 | bytes 4718592 | tf_op jit(solution)/shard_map/rank_grad_back/pallas_call | solution.py:350
  54.7 0.0 copy-start.1
  54.7 1.5 copy-done.1
  56.2 0.0 copy-start.12
  56.2 0.7 copy-done.12
  56.9 86.8 %all-to-all-done = bf16[16,80,1024]{2,1,0:T(8,128)(2,1)} async-done(((bf16[16,80,1024]{2,1,0:T(8,128)(2,1)}), bf16[16,80,1024]{2,1,0:T(8,128)(2,1)}, u32[]{:S(2)}, u32[]{:S(2)}) %all-to-all-start) | async-done | bytes 2621472 | tf_op jit(solution)/shard_map/all_to_all | solution.py:303
  143.8 6.8 %all-to-all-start.3 = ((bf16[16,80,1024]{2,1,0:T(8,128)(2,1)}), bf16[16,80,1024]{2,1,0:T(8,128)(2,1)}, u32[]{:S(2)}, u32[]{:S(2)}) async-start(bf16[16,80,1024]{2,1,0:T(8,128)(2,1)} %bitcast.11), calls=%async_computation.3 | async-start | bytes 5242880 | tf_op jit(solution)/shard_map/all_to_all | solution.py:303
  150.6 0.0 copy-start.8
  150.6 1.6 copy-done.8
  152.2 0.0 copy-start.13
  152.2 8.7 %lowrank_out.1 = (bf16[1280,128]{1,0:T(8,128)(2,1)}, bf16[1280,128]{1,0:T(8,128)(2,1)S(1)}) custom-call(bf16[1280,1024]{1,0:T(8,128)(2,1)} %bitcast.2.got_ref.tok_ref, bf16[1280,128]{1,0:T(8,128)(2,1)S(1)} %get-tuple-element.19.mask_ref, bf16[128,8192]{1,0:T(8,128)(2,1)S(1)} %bitcast.15, bf16[128,1024]{1,0:T(8,128)(2,1)S(1)} %bitcast.17), custom_call_target="tpu_custom_call" | custom-call | flops 2684354560 | bytes 4718592 | tf_op jit(solution)/shard_map/lowrank_out/pallas_call | solution.py:378
  160.9 0.0 copy-done.13
  160.9 0.0 copy-start.6
  160.9 6.8 %page_grads.1 = (bf16[128,8192]{1,0:T(8,128)(2,1)}, bf16[128,1024]{1,0:T(8,128)(2,1)}) custom-call(bf16[1280,1024]{1,0:T(8,128)(2,1)} %bitcast.2.got_ref.tok_ref, bf16[16,96,128]{2,1,0:T(8,128)(2,1)S(1)} %all-to-all-done.1.got_ref.grad_ref, bf16[1280,128]{1,0:T(8,128)(2,1)S(1)} %get-tuple-element.24.low_ref, bf16[1280,128]{1,0:T(8,128)(2,1)S(1)} %copy-done.13), custom_call_target="tpu_custom_call" | custom-call | flops 2684354560 | bytes 4718592 | tf_op jit(solution)/shard_map/page_grads/pallas_call | solution.py:405
  167.7 60.1 %all-to-all-done.3 = bf16[16,80,1024]{2,1,0:T(8,128)(2,1)} async-done(((bf16[16,80,1024]{2,1,0:T(8,128)(2,1)}), bf16[16,80,1024]{2,1,0:T(8,128)(2,1)}, u32[]{:S(2)}, u32[]{:S(2)}) %all-to-all-start.3) | async-done | bytes 2621472 | tf_op jit(solution)/shard_map/all_to_all | solution.py:303
  227.8 5.3 %all-to-all-start.2 = ((bf16[16,80,128]{2,1,0:T(8,128)(2,1)}), bf16[16,80,128]{2,1,0:T(8,128)(2,1)S(1)}, u32[]{:S(2)}, u32[]{:S(2)}) async-start(bf16[16,80,128]{2,1,0:T(8,128)(2,1)} %bitcast.5), calls=%async_computation.2 | async-start | bytes 655360 | tf_op jit(solution)/shard_map/all_to_all | solution.py:303
  233.2 0.0 all-gather.2.cloned.1.call-done.w_ref
  233.2 0.0 copy-done.6
  233.2 0.0 copy-start.4
  233.2 1.6 copy-done.4
  234.8 13.9 %base.1 = (f32[128,1024]{1,0:T(8,128)S(1)}, f32[128,8192]{1,0:T(8,128)}) custom-call(bf16[128,8192]{1,0:T(8,128)(2,1)S(1)} %copy-done.4, bf16[128,1024]{1,0:T(8,128)(2,1)S(1)} %copy-done.6, bf16[8192,1024]{1,0:T(8,128)(2,1)} %all-gather.2.cloned.1.call-done.w_ref), custom_call_target="tpu_custom_call" | custom-call | flops 4294967296 | bytes 16777216 | tf_op jit(solution)/shard_map/base/pallas_call | solution.py:416
  248.7 9.4 %combine_back.1 = bf16[128,8192]{1,0:T(8,128)(2,1)} custom-call(f32[128,128]{1,0:T(8,128)S(1)} %get-tuple-element.16.col_ref, bf16[1280,1024]{1,0:T(8,128)(2,1)} %bitcast.8.got_ref, f32[128,8192]{1,0:T(8,128)} %get-tuple-element.23.base_ref), custom_call_target="tpu_custom_call" | custom-call | flops 2684354560 | bytes 8912896 | tf_op jit(solution)/shard_map/combine_back/pallas_call | solution.py:442
  258.1 0.0 all-to-all-done.2
  258.1 2.4 combine_out.1
Async XLA Ops:
  7.2 1.6 copy-start
  7.2 226.0 %all-gather.2.cloned.1.call-start = ((), (), s32[]{:S(2)}) async-start(), calls=%async_computation.4 | async-start | bytes 17301504 | tf_op jit(solution)/shard_map/all_gather | solution.py:311
  9.6 1.0 copy-start.5
  10.6 0.7 copy-start.10
  11.2 0.7 copy-start.11
  14.5 25.8 %all-to-all-start.1 = ((bf16[16,96,128]{2,1,0:T(8,128)(2,1)}), bf16[16,96,128]{2,1,0:T(8,128)(2,1)S(1)}, u32[]{:S(2)}, u32[]{:S(2)}) async-start(bf16[16,96,128]{2,1,0:T(8,128)(2,1)} %get-tuple-element.18), calls=%async_computation.1 | async-start | bytes 786432 | tf_op jit(solution)/shard_map/all_to_all | solution.py:303
  21.0 1.7 copy-start.3
  26.4 1.5 copy-start.2
  40.3 4.9 %copy-start.9 = (bf16[1,128,1024]{2,1,0:T(8,128)(2,1)S(1)}, bf16[1,128,1024]{2,1,0:T(8,128)(2,1)}, u32[]{:S(2)}) copy-start(bf16[1,128,1024]{2,1,0:T(8,128)(2,1)} %param.11) | copy-start | bytes 786436
  40.3 103.5 %all-to-all-start = ((bf16[16,80,1024]{2,1,0:T(8,128)(2,1)}), bf16[16,80,1024]{2,1,0:T(8,128)(2,1)}, u32[]{:S(2)}, u32[]{:S(2)}) async-start(bf16[16,80,1024]{2,1,0:T(8,128)(2,1)} %bitcast.12), calls=%async_computation | async-start | bytes 5242880 | tf_op jit(solution)/shard_map/all_to_all | solution.py:303
  45.2 1.6 copy-start.7
  54.7 1.5 copy-start.1
  56.2 0.7 copy-start.12
  143.8 84.1 %all-to-all-start.3 = ((bf16[16,80,1024]{2,1,0:T(8,128)(2,1)}), bf16[16,80,1024]{2,1,0:T(8,128)(2,1)}, u32[]{:S(2)}, u32[]{:S(2)}) async-start(bf16[16,80,1024]{2,1,0:T(8,128)(2,1)} %bitcast.11), calls=%async_computation.3 | async-start | bytes 5242880 | tf_op jit(solution)/shard_map/all_to_all | solution.py:303
  150.6 1.6 copy-start.8
  152.2 8.7 %copy-start.13 = (bf16[1280,128]{1,0:T(8,128)(2,1)S(1)}, bf16[1280,128]{1,0:T(8,128)(2,1)}, u32[]{:S(2)}) copy-start(bf16[1280,128]{1,0:T(8,128)(2,1)} %copy-done.12) | copy-start | bytes 983044
  160.9 72.3 %copy-start.6 = (bf16[128,1024]{1,0:T(8,128)(2,1)S(1)}, bf16[128,1024]{1,0:T(8,128)(2,1)}, u32[]{:S(2)}) copy-start(bf16[128,1024]{1,0:T(8,128)(2,1)} %grad_ref.1) | copy-start | bytes 786436
  227.8 30.3 %all-to-all-start.2 = ((bf16[16,80,128]{2,1,0:T(8,128)(2,1)}), bf16[16,80,128]{2,1,0:T(8,128)(2,1)S(1)}, u32[]{:S(2)}, u32[]{:S(2)}) async-start(bf16[16,80,128]{2,1,0:T(8,128)(2,1)} %bitcast.5), calls=%async_computation.2 | async-start | bytes 655360 | tf_op jit(solution)/shard_map/all_to_all | solution.py:303
  233.2 1.6 copy-start.4
Sparse Core Ops, SparseCore 0:
  11.4 197.1 all-gather.1

commit v2 on v1

v2 whole, which is shorter than its diff:
```python
import functools

import jax
import jax.numpy as jnp
from jax import lax
from jax.experimental import pallas as pl
from jax.experimental.pallas import tpu as pltpu
from jax.sharding import PartitionSpec as P

RANK = 32
CHUNKS = 8
VMEM_LIMIT = 48 * 1024 * 1024

adapter_scale = 2.0

F32 = jnp.float32
BF16 = jnp.bfloat16
NT = (((1,), (1,)), ((), ()))
TN = (((0,), (0,)), ((), ()))


def iota(shape, dim):
    return lax.broadcasted_iota(jnp.int32, shape, dim)


def piece_and_slot(index, cap):
    piece = jnp.zeros_like(index)
    for k in range(1, CHUNKS + 1):
        piece = piece + (index >= k * cap).astype(jnp.int32)
    return piece, index - piece * cap


def spread_mask(rows, cap, lanes):
    block = CHUNKS * cap
    piece, _ = piece_and_slot(iota((block, CHUNKS * lanes), 0), cap)
    group = jnp.zeros_like(piece)
    lane = iota(piece.shape, 1)
    for k in range(1, CHUNKS):
        group = group + (lane >= k * lanes).astype(jnp.int32)
    mask = (piece == group).astype(F32).astype(BF16)
    return jnp.concatenate([mask] * (rows // block), axis=0)


def spread(rows, cap):
    return jnp.concatenate([rows] * CHUNKS, axis=1) * spread_mask(
        rows.shape[0], cap, rows.shape[1]
    )


def pick_piece(wide, cap, lanes):
    block, n = CHUNKS * cap, wide.shape[0]
    piece, _ = piece_and_slot(iota((block, lanes), 0), cap)
    piece = jnp.concatenate([piece] * (n // block), axis=0)
    total = jnp.zeros((n, lanes), F32)
    for k in range(CHUNKS):
        total = total + jnp.where(piece == k, wide[:, k * lanes : (k + 1) * lanes], 0.0)
    return total


def same_slot(cap):
    shape = (CHUNKS * cap, CHUNKS * cap)
    _, slot = piece_and_slot(iota(shape, 0), cap)
    _, slot_c = piece_and_slot(iota(shape, 1), cap)
    return (slot == slot_c).astype(F32)


def load_pieces(src, dst, sem, height, stride, start, width):
    return [
        pltpu.make_async_copy(
            src.at[:, pl.ds(k * stride + start, width)],
            dst.at[pl.ds(k * height, height), pl.ds(0, width)],
            sem.at[k],
        )
        for k in range(CHUNKS)
    ]


def start_all(copies):
    for copy in copies:
        copy.start()


def wait_all(copies):
    for copy in copies:
        copy.wait()


def rows_of_slots(slot, cap, first, group):
    _, slot_of = piece_and_slot(iota((CHUNKS * cap, slot.shape[1]), 0), cap)
    return jnp.concatenate(
        [
            (slot == (slot_of + (first + d) * cap).astype(F32)).astype(F32).astype(BF16)
            for d in range(group)
        ],
        axis=0,
    )


def earlier_rows(rows):
    return (iota((rows, rows), 0) < iota((rows, rows), 1)).astype(F32).astype(BF16)


def join(ref, first, group, block, start, count):
    return jnp.concatenate(
        [
            jnp.concatenate(
                [ref[d, (start + n) * block : (start + n + 1) * block, :] for n in range(count)],
                axis=1,
            )
            for d in range(first, first + group)
        ],
        axis=0,
    )


def route_kernel(
    devices, cap, per_page, owner_ref, tenant_ref, tokens_ref, grads_ref,
    send_ref, row_ref, col_ref, pieces, sem,
):
    step = pl.program_id(0)
    rows = tenant_ref.shape[1]
    group, height, lanes = send_ref.shape
    block = CHUNKS * cap
    half = pieces.shape[1] - lanes
    page = tenant_ref[...] // per_page
    member = tenant_ref[...] - page * per_page

    @pl.when(step == 0)
    def _():
        copies = load_pieces(tokens_ref, pieces, sem, rows, 2 * half, 0, half)
        copies += [
            pltpu.make_async_copy(
                grads_ref.at[:, pl.ds(k * lanes, lanes)],
                pieces.at[pl.ds(k * rows, rows), pl.ds(half, lanes)],
                sem.at[CHUNKS + k],
            )
            for k in range(CHUNKS)
        ]
        start_all(copies)

        def add_page(p, target):
            return target + jnp.where(page == p, owner_ref[p], 0)

        target = lax.fori_loop(0, owner_ref.shape[0], add_page, jnp.zeros_like(page))
        chosen = (iota((devices, rows), 0) == target).astype(F32)
        before = jnp.dot(chosen.astype(BF16), earlier_rows(rows), preferred_element_type=F32)
        slot = target.astype(F32) * cap + jnp.sum(before * chosen, axis=0, keepdims=True)
        row_ref[...] = slot
        col_ref[...] = jnp.transpose(jnp.broadcast_to(slot, (rows, rows)))
        wait_all(copies)

    slot = row_ref[...]
    here = spread(rows_of_slots(slot, cap, step * group, group), cap)
    packed = jnp.dot(here, pieces[...], preferred_element_type=F32).astype(BF16)
    of_member = (iota((lanes, rows), 0) // RANK == member).astype(F32).astype(BF16)
    count = packed.shape[1] // lanes
    tail = iota((height - count * block, rows), 0)
    tail = jnp.where(tail < cap, tail, -(10**6))
    for d in range(group):
        for n in range(count):
            send_ref[d, n * block : (n + 1) * block, :] = packed[
                d * block : (d + 1) * block, n * lanes : (n + 1) * lanes
            ]
        in_slot = (slot == (tail + (step * group + d) * cap).astype(F32)).astype(F32).astype(BF16)
        send_ref[d, count * block :, :] = lax.dot_general(
            in_slot, of_member, NT, preferred_element_type=F32
        ).astype(BF16)


def dispatch_kernel(cap, slot_ref, tokens_ref, out_ref, pieces, sem):
    step = pl.program_id(0)
    half = pieces.shape[1]
    group = out_ref.shape[0] // (CHUNKS * cap)

    @pl.when(step == 0)
    def _():
        copies = load_pieces(tokens_ref, pieces, sem, slot_ref.shape[1], 2 * half, half, half)
        start_all(copies)
        wait_all(copies)

    here = rows_of_slots(slot_ref[...], cap, step * group, group)
    out_ref[...] = jnp.dot(spread(here, cap), pieces[...], preferred_element_type=F32).astype(BF16)


def back_kernel(
    cap, got_ref, b_ref, a_ref, first_ref, second_ref, rank_ref, mask_ref, pieces, sem
):
    step = pl.program_id(0)
    ranks = b_ref.shape[0]
    group, height, width = got_ref.shape
    block = CHUNKS * cap
    half = pieces.shape[1] // 2
    count = half // width
    copies = load_pieces(a_ref, pieces, sem, ranks, 2 * half, 0, 2 * half)

    @pl.when(step == 0)
    def _():
        start_all(copies)

    tail = height - (count + 1) * block
    _, slot = piece_and_slot(iota((block, tail), 0), cap)
    pick_mask = (iota((block, tail), 1) == slot).astype(F32).astype(BF16)
    b_pieces = jnp.concatenate(
        [b_ref[:, k * width : (k + 1) * width] for k in range(CHUNKS)], axis=0
    )
    wide = lax.dot_general(
        join(got_ref, 0, group, block, count, 1), b_pieces, NT, preferred_element_type=F32
    )
    part = pick_piece(wide, cap, ranks)
    fold = same_slot(cap)
    ranks_of = []
    for d in range(group):
        at = slice(d * block, (d + 1) * block)
        full = jnp.dot(
            fold, part[at, :], precision=lax.Precision.HIGHEST, preferred_element_type=F32
        )
        mask = jnp.dot(
            pick_mask, got_ref[d, (count + 1) * block :, :], preferred_element_type=F32
        )
        ranks_of.append((full * mask).astype(BF16))
        mask_ref[at, :] = mask.astype(BF16)
    rank_rows = jnp.concatenate(ranks_of, axis=0)
    rank_ref[...] = rank_rows

    @pl.when(step == 0)
    def _():
        wait_all(copies)

    back = (
        adapter_scale * jnp.dot(spread(rank_rows, cap), pieces[...], preferred_element_type=F32)
    ).astype(BF16)
    first_ref[...] = back[:, 0:half]
    second_ref[:, 0:half] = back[:, half:]
    second_ref[:, half:] = jnp.zeros((second_ref.shape[0], second_ref.shape[1] - half), BF16)


def forth_kernel(
    cap, first_ref, second_ref, mask_ref, a_ref, b_ref, _, out_ref, rank_ref, pieces, sem
):
    step = pl.program_id(0)
    ranks = b_ref.shape[0]
    block = CHUNKS * cap
    width = out_ref.shape[1]
    half = pieces.shape[1] // 2
    group = first_ref.shape[0]

    @pl.when(step == 0)
    def _():
        copies = load_pieces(a_ref, pieces, sem, ranks, 2 * half, 0, 2 * half)
        start_all(copies)
        wait_all(copies)

    b_pieces = jnp.concatenate(
        [b_ref[:, k * width : (k + 1) * width] for k in range(CHUNKS)], axis=0
    )
    wide = lax.dot_general(
        join(first_ref, 0, group, block, 0, half // first_ref.shape[2]),
        pieces[:, 0:half],
        NT,
        preferred_element_type=F32,
    ) + lax.dot_general(second_ref[...], pieces[:, half:], NT, preferred_element_type=F32)
    part = pick_piece(wide, cap, ranks)
    fold = same_slot(cap)
    full = jnp.concatenate(
        [
            jnp.dot(
                fold,
                part[d * block : (d + 1) * block, :],
                precision=lax.Precision.HIGHEST,
                preferred_element_type=F32,
            )
            for d in range(group)
        ],
        axis=0,
    )
    rank_rows = (full * mask_ref[...].astype(F32)).astype(BF16)
    rank_ref[...] = rank_rows
    out_ref[...] = (
        adapter_scale * jnp.dot(spread(rank_rows, cap), b_pieces, preferred_element_type=F32)
    ).astype(BF16)


def page_grad_kernel(cap, first_ref, second_ref, low_ref, rank_ref, ga_ref, gb_ref):
    ranks = rank_ref.shape[1]
    half = second_ref.shape[1]
    devices, _, narrow = first_ref.shape
    block = CHUNKS * cap
    count = half // narrow
    tokens = join(first_ref, 0, devices, block, 0, count)
    grads = join(first_ref, 0, devices, block, count, 1)
    rank_rows = spread(rank_ref[...], cap)
    left = lax.dot_general(rank_rows, tokens, TN, preferred_element_type=F32)
    right = lax.dot_general(rank_rows, second_ref[...], TN, preferred_element_type=F32)
    low = lax.dot_general(
        spread(low_ref[...], cap), grads, TN, preferred_element_type=F32
    )
    for k in range(CHUNKS):
        at, col = slice(k * ranks, (k + 1) * ranks), 2 * k * half
        ga_ref[:, col : col + half] = (adapter_scale * left[at, :]).astype(BF16)
        ga_ref[:, col + half : col + 2 * half] = (adapter_scale * right[at, :]).astype(BF16)
        gb_ref[:, k * narrow : (k + 1) * narrow] = (adapter_scale * low[at, :]).astype(BF16)


def pair_kernel(other_ref, tokens_ref, grads_ref, out_ref, sem):
    rows, narrow = grads_ref.shape
    half = (out_ref.shape[1] - narrow) // CHUNKS
    at = pl.multiple_of(other_ref[0] * half, half)
    copies = [
        pltpu.make_async_copy(
            tokens_ref.at[:, pl.ds(2 * k * half + at, half)],
            out_ref.at[:, pl.ds(k * half, half)],
            sem.at[k],
        )
        for k in range(CHUNKS)
    ]
    copies.append(
        pltpu.make_async_copy(
            grads_ref, out_ref.at[:, pl.ds(CHUNKS * half, narrow)], sem.at[CHUNKS]
        )
    )
    start_all(copies)
    wait_all(copies)


def pair_base_kernel(at_ref, tok_ref, grad_ref, pair_ref, *refs):
    weights, (out_ref, back_ref, theirs_ref) = refs[:-3], refs[-3:]
    rows, narrow = grad_ref.shape
    half_width = back_ref.shape[1]
    grads = jnp.concatenate([grad_ref[...], pair_ref[:, half_width:]], axis=0)
    total = jnp.zeros((2 * rows, narrow), F32)
    for n, ref in enumerate(weights):
        weight = ref[...]
        share = weight.shape[0]
        full = pl.multiple_of(at_ref[2 * n] * share, share)
        part = pl.multiple_of(at_ref[2 * n + 1] * share, share)
        toks = jnp.concatenate(
            [tok_ref[:, pl.ds(full, share)], pair_ref[:, pl.ds(part, share)]], axis=0
        )
        total = total + jnp.dot(toks, weight, preferred_element_type=F32)
        back = lax.dot_general(grads, weight, NT, preferred_element_type=F32)
        back_ref[:, pl.ds(part, share)] = back[0:rows, :]
        theirs_ref[:, pl.ds(part, share)] = back[rows:, :]
    out_ref[...] = total[0:rows, :]
    theirs_ref[:, half_width:] = total[rows:, :]


def base_kernel(tok_ref, grad_ref, w_ref, out_ref, back_ref):
    @pl.when(pl.program_id(0) == 0)
    def _():
        out_ref[...] = jnp.zeros_like(out_ref)

    weight = w_ref[...]
    out_ref[...] += jnp.dot(tok_ref[...], weight, preferred_element_type=F32)
    back_ref[...] = lax.dot_general(grad_ref[...], weight, NT, preferred_element_type=F32)


def combine_kernel(cap, half, which_ref, col_ref, got_ref, mine_ref, pair_ref, *refs):
    out_hbm, out, sem, base, base_sem = refs[-5:]
    devices, block, width = got_ref.shape
    cols = out.shape[2]
    stride = mine_ref.shape[1] // (CHUNKS * cols)
    offset = half if stride == 2 else 0
    rows = col_ref.shape[0]

    def load(ref):
        copies = [
            pltpu.make_async_copy(
                ref.at[:, pl.ds((stride * k + offset) * cols, cols)], base.at[k], base_sem.at[k]
            )
            for k in range(CHUNKS)
        ]
        start_all(copies)

    @pl.when(which_ref[0] == half)
    def _():
        load(mine_ref)

    @pl.when(which_ref[0] != half)
    def _():
        load(pair_ref)

    col = col_ref[:, 0:1]
    copies = []
    for k in range(CHUNKS):
        low = k * cap // 16 * 16
        high = min(-(-(k + 1) * cap // 16) * 16, block)
        count = high - low
        lane = iota((1, devices * count), 1)
        row = jnp.zeros_like(lane)
        for d in range(1, devices):
            row = row + (lane >= d * count).astype(jnp.int32)
        slot = lane - row * count + (low - k * cap)
        key = jnp.where((slot >= 0) & (slot < cap), row * cap + slot, -1).astype(F32)
        here = (col == key).astype(F32).astype(BF16)
        packed = jnp.concatenate([got_ref[d, low:high, :] for d in range(devices)], axis=0)
        back = jnp.dot(here, packed, preferred_element_type=F32)
        pltpu.make_async_copy(
            mine_ref.at[:, pl.ds(0, cols)], base.at[k], base_sem.at[k]
        ).wait()
        out[k] = (base[k] + back[:, 0:cols]).astype(BF16)
        copy = pltpu.make_async_copy(
            out.at[k], out_hbm.at[:, pl.ds((2 * k + half) * cols, cols)], sem.at[k]
        )
        copy.start()
        copies.append(copy)
        if half == 1:
            base_out_ref, projected_ref = refs[0], refs[2]
            at = slice(k * (width - cols), (k + 1) * (width - cols))
            projected_ref[:, at] = (base_out_ref[:, at] + back[:, cols:]).astype(BF16)
    wait_all(copies)


def call(kernel, deps=(), **options):
    deps = tuple(deps)
    specs = list(options.pop("in_specs"))
    count = len(specs)

    def body(*refs):
        kernel(*refs[:count], *refs[count + len(deps) :])

    run = pl.pallas_call(
        body, in_specs=specs + [pl.BlockSpec(memory_space=pl.ANY)] * len(deps), **options
    )
    return lambda *args: run(*args, *deps)


def held(x, deps):
    deps = tuple(deps)
    if not deps:
        return x
    any_spec = pl.BlockSpec(memory_space=pl.ANY)
    return call(
        lambda x_ref, out_ref: None,
        deps=deps,
        out_shape=in_hbm(x.shape, x.dtype),
        in_specs=[any_spec],
        out_specs=any_spec,
        input_output_aliases={0: 0},
        cost_estimate=cost(0, 0),
        name="held",
    )(x)


def pick_kernel(count, which_ref, *refs):
    for n in range(count):

        @pl.when(which_ref[0] == n)
        def _():
            refs[count][...] = refs[n][...]


def pick(which, *arrays):
    x = arrays[0]
    return call(
        functools.partial(pick_kernel, len(arrays)),
        out_shape=jax.ShapeDtypeStruct(x.shape, x.dtype),
        in_specs=[pl.BlockSpec(memory_space=pltpu.SMEM)]
        + [pl.BlockSpec(memory_space=pltpu.VMEM)] * len(arrays),
        out_specs=pl.BlockSpec(memory_space=pltpu.VMEM),
        cost_estimate=cost(0, 2 * x.size * x.dtype.itemsize),
        name="pick",
    )(which.astype(jnp.int32).reshape(1), *arrays)


def in_hbm(shape, dtype):
    return pltpu.HBM(shape, dtype)


def whole(shape):
    return pl.BlockSpec(shape, lambda *_: (0,) * len(shape))


def params(semantics=None):
    return pltpu.CompilerParams(vmem_limit_bytes=VMEM_LIMIT, dimension_semantics=semantics)


def cost(flops, nbytes):
    return pl.CostEstimate(flops=int(flops), bytes_accessed=int(nbytes), transcendentals=0)


def swap(x, axis):
    size = lax.axis_size(axis)
    return lax.ppermute(x, axis, [(i, i ^ 1) for i in range(size)])


def gather_shares(base_weight, inner):
    count = lax.axis_size("fsdp")
    z = lax.axis_index("fsdp") // inner
    share = base_weight.shape[0] // 4
    at = lax.axis_index("tenant") * 2 + lax.axis_index("groups")
    mine = lax.dynamic_slice_in_dim(base_weight, at * share, share, 0)

    up_pairs = [(i, i + inner) for i in range(count - inner)]
    up, down = [mine], [mine]
    for j in range(1, 4):
        moved = [p for p in up_pairs if p[0] // inner >= j - 1]
        up.append(lax.ppermute(up[-1], "fsdp", moved))
        moved = [(b, a) for a, b in up_pairs if b // inner <= 4 - j]
        down.append(lax.ppermute(down[-1], "fsdp", moved))

    def of_z(*values):
        return functools.reduce(
            lambda rest, k: jnp.where(z == k, values[k], rest), range(3), values[3]
        )

    held_shares = [
        (mine, z),
        (pick(of_z(0, 1, 1, 1), down[1], up[1]), of_z(1, 0, 1, 2)),
        (pick(of_z(0, 1, 1, 2), down[2], down[1], up[2]), of_z(2, 2, 3, 1)),
        (pick(of_z(0, 1, 2, 3), down[3], down[2], up[2], up[3]), of_z(3, 3, 0, 0)),
    ]
    blocks, y_of, x_of, both_of = [], [], [], []

    def spread_share(n, deps=()):
        own, place = held_shares[n]
        y_of.append(held(swap(own, "fsdp"), deps))
        x_of.append(swap(own, "groups"))
        both_of.append(swap(y_of[n], "groups"))
        blocks.extend(
            [
                (own, place, 0, 0),
                (y_of[n], place, 1, 0),
                (x_of[n], place, 0, 1),
                (both_of[n], place, 1, 1),
            ]
        )

    for n in range(3):
        spread_share(n)
    after = {
        "first": [up[1], down[1]],
        "second": [up[2], down[2], y_of[0], x_of[0], y_of[1], x_of[1]],
        "third": [up[3], down[3], y_of[2], x_of[2], both_of[0], both_of[1]],
    }

    def last(deps):
        spread_share(3, deps)
        return [y_of[3], x_of[3], both_of[2]]

    return {"blocks": blocks, "after": after, "last": last}


def for_pair(tokens, grad_out):
    rows, width = tokens.shape
    narrow = grad_out.shape[1]
    any_spec = pl.BlockSpec(memory_space=pl.ANY)
    other = (1 - lax.axis_index("tenant")).astype(jnp.int32).reshape(1)
    return call(
        pair_kernel,
        out_shape=in_hbm((rows, width // 2 + narrow), BF16),
        in_specs=[pl.BlockSpec(memory_space=pltpu.SMEM), any_spec, any_spec],
        out_specs=any_spec,
        scratch_shapes=[pltpu.SemaphoreType.DMA((CHUNKS + 1,))],
        compiler_params=params(),
        cost_estimate=cost(0, 4 * rows * (width // 2 + narrow)),
        name="for_pair",
    )(other, tokens, grad_out)


def paired_base(tokens, grad_out, pair, shares, fsdp_size, inner):
    rows, width = tokens.shape
    narrow = grad_out.shape[1]
    tenant, group = lax.axis_index("tenant"), lax.axis_index("groups")
    fsdp = lax.axis_index("fsdp")
    y = fsdp % inner
    gathered = shares["blocks"]
    any_spec = pl.BlockSpec(memory_space=pl.ANY)
    vmem = pl.BlockSpec(memory_space=pltpu.VMEM)
    smem = pl.BlockSpec(memory_space=pltpu.SMEM)

    half = width // 2
    at = []
    for _, place, dy, dx in gathered:
        shard = place * inner + (y ^ dy)
        x = group ^ dx
        at += [shard * 4 + tenant * 2 + x, shard * 2 + x]
    out, back, theirs = call(
        pair_base_kernel,
        out_shape=(
            jax.ShapeDtypeStruct((rows, narrow), F32),
            jax.ShapeDtypeStruct((rows, half), F32),
            jax.ShapeDtypeStruct((rows, half + narrow), F32),
        ),
        in_specs=[smem] + [vmem] * (3 + len(gathered)),
        out_specs=(vmem, vmem, vmem),
        compiler_params=params(),
        cost_estimate=cost(4 * rows * width * narrow, width * narrow),
        name="base",
    )(jnp.stack(at).astype(jnp.int32), tokens, grad_out, pair, *[g[0] for g in gathered])
    theirs = swap(theirs, "tenant")
    return out + theirs[:, half:], back, theirs


def whole_base(tokens, grad_out, base_weight):
    rows, width = tokens.shape
    narrow = grad_out.shape[1]
    wp = width // CHUNKS
    group_size, tenant_size = lax.axis_size("groups"), lax.axis_size("tenant")
    shares = group_size * tenant_size
    share = base_weight.shape[0] // shares
    which = lax.axis_index("groups") * tenant_size + lax.axis_index("tenant")
    mine = lax.dynamic_slice_in_dim(base_weight, which * share, share, 0)
    weight = lax.all_gather(mine, ("fsdp", "groups", "tenant"), axis=0, tiled=True)
    return call(
        base_kernel,
        out_shape=(
            jax.ShapeDtypeStruct((rows, narrow), F32),
            jax.ShapeDtypeStruct((rows, width), F32),
        ),
        grid=(CHUNKS,),
        in_specs=[
            pl.BlockSpec((rows, wp), lambda i: (0, i)),
            whole((rows, narrow)),
            pl.BlockSpec((wp, narrow), lambda i: (i, 0)),
        ],
        out_specs=(whole((rows, narrow)), pl.BlockSpec((rows, wp), lambda i: (0, i))),
        compiler_params=params(("arbitrary",)),
        cost_estimate=cost(4 * rows * width * narrow, 2 * width * narrow),
        name="base",
    )(tokens, grad_out, weight)


def on_device(tokens, grad_out, base_weight, page_a, page_b, page_owner, row_tenant):
    rows, width = tokens.shape
    narrow = grad_out.shape[1]
    fsdp_size = lax.axis_size("fsdp")
    tenant_size = lax.axis_size("tenant")
    devices = fsdp_size * tenant_size
    cap = max(4, 4 * rows // (3 * devices))
    per_page = page_a.shape[1] // RANK
    ranks = page_a.shape[1]
    block = CHUNKS * cap
    total = devices * block
    wp, np_ = width // CHUNKS, narrow // CHUNKS
    half = wp // 2
    height = (half // np_ + 1) * block + -(-cap // 16) * 16
    left_factor, right_factor = page_a[0], page_b[0]
    axes = ("fsdp", "tenant")
    which = lax.axis_index("tenant").astype(jnp.int32).reshape(1)

    def exchange(x):
        return lax.all_to_all(x, axes, split_axis=0, concat_axis=0, tiled=True)

    any_spec = pl.BlockSpec(memory_space=pl.ANY)
    smem = pl.BlockSpec(memory_space=pltpu.SMEM)
    paired = (
        fsdp_size == 8
        and tenant_size == 2
        and lax.axis_size("groups") == 2
        and width // fsdp_size == wp
    )

    steps = 4 if devices % 4 == 0 else 1
    send_first, slot_row, slot_col = call(
        functools.partial(route_kernel, devices, cap, per_page),
        out_shape=(
            in_hbm((devices, height, np_), BF16),
            jax.ShapeDtypeStruct((1, rows), F32),
            jax.ShapeDtypeStruct((rows, rows), F32),
        ),
        grid=(steps,),
        in_specs=[smem, whole((1, rows)), any_spec, any_spec],
        out_specs=(
            pl.BlockSpec((devices // steps, height, np_), lambda i: (i, 0, 0)),
            whole((1, rows)),
            whole((rows, rows)),
        ),
        scratch_shapes=[
            pltpu.VMEM((CHUNKS * rows, half + np_), BF16),
            pltpu.SemaphoreType.DMA((2 * CHUNKS,)),
        ],
        compiler_params=params(("arbitrary",)),
        cost_estimate=cost(total * rows * width, 2 * total * half),
        name="route",
    )(page_owner, row_tenant.reshape(1, rows), tokens, grad_out)
    after = {}
    if paired:
        shares = gather_shares(base_weight, 2)
        after = shares["after"]
    part = total // steps
    send_second = call(
        functools.partial(dispatch_kernel, cap),
        out_shape=in_hbm((total, half), BF16),
        grid=(steps,),
        in_specs=[whole((1, rows)), any_spec],
        out_specs=pl.BlockSpec((part, half), lambda i: (i, 0)),
        scratch_shapes=[
            pltpu.VMEM((CHUNKS * rows, half), BF16),
            pltpu.SemaphoreType.DMA((CHUNKS,)),
        ],
        compiler_params=params(("arbitrary",)),
        cost_estimate=cost(total * rows * width, 2 * total * half),
        name="dispatch",
    )(slot_row, tokens)
    if paired:
        pair = for_pair(tokens, grad_out)
    got_first = exchange(held(send_first, after.get("first", ())))
    got_second = exchange(held(send_second, [got_first] + after.get("second", [])))

    back_first, back_second, rank_rows, mask_rows = call(
        functools.partial(back_kernel, cap),
        out_shape=(
            in_hbm((total, half), BF16),
            in_hbm((total, half + np_), BF16),
            jax.ShapeDtypeStruct((total, ranks), BF16),
            jax.ShapeDtypeStruct((total, ranks), BF16),
        ),
        grid=(steps,),
        in_specs=[
            pl.BlockSpec((devices // steps, height, np_), lambda i: (i, 0, 0)),
            whole((ranks, narrow)),
            any_spec,
        ],
        out_specs=(
            pl.BlockSpec((part, half), lambda i: (i, 0)),
            pl.BlockSpec((part, half + np_), lambda i: (i, 0)),
            pl.BlockSpec((part, ranks), lambda i: (i, 0)),
            pl.BlockSpec((part, ranks), lambda i: (i, 0)),
        ),
        scratch_shapes=[
            pltpu.VMEM((CHUNKS * ranks, wp), BF16),
            pltpu.SemaphoreType.DMA((CHUNKS,)),
        ],
        compiler_params=params(("arbitrary",)),
        cost_estimate=cost(2 * total * ranks * width, 2 * (total * wp + ranks * width)),
        name="rank_grad_back",
    )(got_first, right_factor, left_factor)
    got_back = exchange(held(back_first, [got_second] + after.get("third", [])))

    back_second, low_rows = call(
        functools.partial(forth_kernel, cap),
        out_shape=(
            in_hbm((total, half + np_), BF16),
            jax.ShapeDtypeStruct((total, ranks), BF16),
        ),
        grid=(steps,),
        in_specs=[
            pl.BlockSpec((devices // steps, height, np_), lambda i: (i, 0, 0)),
            pl.BlockSpec((part, half), lambda i: (i, 0)),
            pl.BlockSpec((part, ranks), lambda i: (i, 0)),
            any_spec,
            whole((ranks, narrow)),
            any_spec,
        ],
        out_specs=(
            pl.BlockSpec((part, np_), lambda i: (i, half // np_)),
            pl.BlockSpec((part, ranks), lambda i: (i, 0)),
        ),
        scratch_shapes=[
            pltpu.VMEM((CHUNKS * ranks, wp), BF16),
            pltpu.SemaphoreType.DMA((CHUNKS,)),
        ],
        input_output_aliases={5: 0},
        compiler_params=params(("arbitrary",)),
        cost_estimate=cost(2 * total * ranks * width, 2 * (total * wp + ranks * width)),
        name="lowrank_out",
    )(got_first, got_second, mask_rows, left_factor, right_factor, back_second)
    fourth = shares["last"]([low_rows]) if paired else []
    got_rest = exchange(held(back_second, [got_back] + fourth))

    if paired:
        base_out, base_mine, base_pair = paired_base(
            tokens, grad_out, held(swap(pair, "tenant"), [low_rows]), shares, fsdp_size, 2
        )
    else:
        base_out, base_mine = whole_base(tokens, grad_out, base_weight)
        base_pair = base_mine

    grad_a, grad_b = call(
        functools.partial(page_grad_kernel, cap),
        in_specs=[pl.BlockSpec(memory_space=pltpu.VMEM)] * 4,
        out_shape=(
            jax.ShapeDtypeStruct((ranks, width), BF16),
            jax.ShapeDtypeStruct((ranks, narrow), BF16),
        ),
        compiler_params=params(),
        cost_estimate=cost(2 * total * ranks * width, 2 * (total * wp + ranks * width)),
        name="page_grads",
    )(got_first, got_second, low_rows, rank_rows)

    combine_cost = cost(rows * total * width, 2 * total * half + 4 * rows * width)
    combine_scratch = [
        pltpu.VMEM((CHUNKS, rows, half), BF16),
        pltpu.SemaphoreType.DMA((CHUNKS,)),
        pltpu.VMEM((CHUNKS, rows, half), F32),
        pltpu.SemaphoreType.DMA((CHUNKS,)),
    ]
    vmem = pl.BlockSpec(memory_space=pltpu.VMEM)
    grad_tokens = call(
        functools.partial(combine_kernel, cap, 0),
        out_shape=jax.ShapeDtypeStruct((rows, width), BF16),
        in_specs=[smem, vmem, vmem, any_spec, any_spec],
        out_specs=any_spec,
        scratch_shapes=combine_scratch,
        compiler_params=params(),
        cost_estimate=combine_cost,
        name="combine_first",
    )(which, slot_col, got_back.reshape(devices, block, half), base_mine, base_pair)
    projected, grad_tokens = call(
        functools.partial(combine_kernel, cap, 1),
        out_shape=(
            jax.ShapeDtypeStruct((rows, narrow), BF16),
            jax.ShapeDtypeStruct((rows, width), BF16),
        ),
        in_specs=[smem, vmem, vmem, any_spec, any_spec, vmem, any_spec],
        out_specs=(vmem, any_spec),
        scratch_shapes=combine_scratch,
        input_output_aliases={6: 1},
        compiler_params=params(),
        cost_estimate=combine_cost,
        name="combine_rest",
    )(
        which,
        slot_col,
        got_rest.reshape(devices, block, half + np_),
        base_mine,
        base_pair,
        base_out,
        grad_tokens,
    )

    return projected, grad_tokens, grad_a[None], grad_b[None]


def solution(mesh):
    rows = P(("groups", "fsdp", "tenant"), None)
    pages = P(("groups", "fsdp", "tenant"), None, None)
    return jax.shard_map(
        on_device,
        mesh=mesh,
        in_specs=(
            rows,
            rows,
            P("fsdp", None),
            pages,
            pages,
            P("groups"),
            P(("groups", "fsdp", "tenant")),
        ),
        out_specs=(rows, rows, pages, pages),
        check_vma=False,
    )
```

time: 269 us -> 215 us (0.80)
  waiting for transfers between devices: 159 us -> 70.2 us
  starting transfers between devices: 23.7 us -> 53 us
  local copies, waits for them, and re-layouts: 14.9 us -> 31.8 us
  between operations: 14.2 us -> 1.12 us
    all_to_all x4, waiting for transfers between devices: 159 us -> 8.49 us  [exchange(): return lax.all_to_all(x, axes, split_axis=0, concat_axis=0, tiled=True)]
    ppermute x0 -> x20, waiting for transfers between devices: none -> 61.7 us  [the longest x3 32 us: gather_shares(): down.append(lax.ppermute(down[-1], 'fsdp', moved))]
    ppermute x0 -> x20, starting transfers between devices: none -> 25.7 us  [the longest x14 10.7 us: swap(): return lax.ppermute(x, axis, [(i, i ^ 1) for i in range(size)])]
    unnamed x28 -> x86, local copies, waits for them, and re-layouts: 14 us -> 31.7 us
    all_to_all x4, starting transfers between devices: 23.6 us -> 27.3 us  [exchange(): return lax.all_to_all(x, axes, split_axis=0, concat_axis=0, tiled=True)]
    pallas_call x8 -> x18, Pallas kernels: 55.4 us -> 56.8 us  [call(): return lambda *args: run(*args, *deps)]
  transfers between devices with their start and end apart: 5 -> 24, of which waited for: 3 -> 12; matrix products, arithmetic and copies ran while one was open for 0% -> 0% of each run, Pallas kernels for 20% -> 24%
where the time goes in v2:
time: 215 us; the launch traced here: 213 us
  waiting for transfers between devices  70.2 us (33%)
  Pallas kernels  56.8 us (26%)
  starting transfers between devices  53 us (25%)
  local copies, waits for them, and re-layouts  31.8 us (15%)
    pallas_call x18, Pallas kernels, call(): return lambda *args: run(*args, *deps)  56.8 us
    ppermute x3, waiting for transfers between devices, gather_shares(): down.append(lax.ppermute(down[-1], 'fsdp', moved))  32 us
    unnamed x86, local copies, waits for them, and re-layouts  31.7 us
    ppermute x14, waiting for transfers between devices, swap(): return lax.ppermute(x, axis, [(i, i ^ 1) for i in range(size)])  27.9 us
    all_to_all x4, starting transfers between devices, exchange(): return lax.all_to_all(x, axes, split_axis=0, concat_axis=0, tiled=True)  27.3 us
    ppermute x14, starting transfers between devices, swap(): return lax.ppermute(x, axis, [(i, i ^ 1) for i in range(size)])  10.7 us
    ppermute x3, starting transfers between devices, gather_shares(): up.append(lax.ppermute(up[-1], 'fsdp', moved))  8.69 us
    all_to_all x4, waiting for transfers between devices, exchange(): return lax.all_to_all(x, axes, split_axis=0, concat_axis=0, tiled=True)  8.49 us
  transfers between devices with their start and end apart: 24, of which 12 were waited for; matrix products, arithmetic and copies ran while one was open for 0% of the time, Pallas kernels for 24%

profile of v2, /device:TPU:13, one launch (start us, length us, event | category | flops | bytes accessed | tf_op | source)
XLA Modules:
  0.0 213.0 jit_solution(17792478063187012790)
XLA Ops:
  0.7 1.6 copy-done
  2.3 2.1 collective-permute-start.1
  4.4 3.2 %collective-permute-start = (bf16[256,1024]{1,0:T(8,128)(2,1)S(1)}, bf16[256,1024]{1,0:T(8,128)(2,1)S(1)}, u32[]{:S(2)}, u32[]{:S(2)}) collective-permute-start(bf16[256,1024]{1,0:T(8,128)(2,1)S(1)} %constant_dynamic-slice_fusion.refs_4_), channel_id=1, source_target_pairs={{0,4},{2,6},{4,8},{6,10},{8,12},{10,14},{1,5},{3,7},{5,9},{7,11},{... | collective-permute-start | bytes 1572872 | tf_op jit(solution)/shard_map/ppermute | solution.py:497
  7.6 1.6 copy-done.9
  9.2 0.9 copy-done.26
  11.4 5.0 %route.1 = (bf16[16,416,128]{2,1,0:T(8,128)(2,1)}, f32[1,128]{1,0:T(1,128)S(1)}, f32[128,128]{1,0:T(8,128)S(1)}) custom-call(s32[16]{0:T(128)S(1)} %copy-done.33, s32[1,128]{1,0:T(1,128)S(1)} %bitcast.55, bf16[128,8192]{1,0:T(8,128)(2,1)S(1)} %copy-done.9, bf16[128,1024]{1,0:T(8,128)(2,1)S(1)} %copy-done.26), custom_call_target="tpu_custom_call" | custom-call | flops 1342177280 | bytes 1310720 | tf_op jit(solution)/shard_map/route/pallas_call | solution.py:424
  17.0 1.8 collective-permute-done.refs_1_.refs_2_
  18.7 0.8 copy-done.40
  19.6 7.8 %all-to-all-start = ((bf16[16,416,128]{2,1,0:T(8,128)(2,1)}), bf16[16,416,128]{2,1,0:T(8,128)(2,1)}, u32[]{:S(2)}, u32[]{:S(2)}) async-start(bf16[16,416,128]{2,1,0:T(8,128)(2,1)} %held.6), calls=%async_computation | async-start | bytes 3407872 | tf_op jit(solution)/shard_map/all_to_all | solution.py:642
  27.3 1.2 collective-permute-start.5
  28.8 2.0 pick.3.refs_8_
  31.1 2.0 collective-permute-start.3
  33.1 1.5 collective-permute-start.6
  34.6 6.1 %collective-permute-done.5.refs_5_.refs_6_ = bf16[256,1024]{1,0:T(8,128)(2,1)S(1)} collective-permute-done((bf16[256,1024]{1,0:T(8,128)(2,1)}, bf16[256,1024]{1,0:T(8,128)(2,1)S(1)}, u32[]{:S(2)}, u32[]{:S(2)}) %collective-permute-start.5) | collective-permute-done | bytes 524320 | tf_op jit(solution)/shard_map/ppermute | solution.py:483
  40.7 4.0 %collective-permute-start.2 = (bf16[256,1024]{1,0:T(8,128)(2,1)}, bf16[256,1024]{1,0:T(8,128)(2,1)}, u32[]{:S(2)}, u32[]{:S(2)}) collective-permute-start(bf16[256,1024]{1,0:T(8,128)(2,1)} %copy-done.40), channel_id=1, source_target_pairs={{4,8},{6,10},{8,12},{10,14},{5,9},{7,11},{9,13},{11,15},{20,24},{2... | collective-permute-start | bytes 1572872 | tf_op jit(solution)/shard_map/ppermute | solution.py:497
  44.7 1.6 copy-done.10
  46.3 3.2 %dispatch.1.refs_0_ = bf16[1280,512]{1,0:T(8,128)(2,1)} custom-call(f32[1,128]{1,0:T(1,128)S(1)} %get-tuple-element.22.refs_0_, bf16[128,8192]{1,0:T(8,128)(2,1)S(1)} %copy-done.10), custom_call_target="tpu_custom_call" | custom-call | flops 1342177280 | bytes 1310720 | tf_op jit(solution)/shard_map/dispatch/pallas_call | solution.py:424
  49.5 2.6 %collective-permute-done.4.refs_4_.refs_5_ = bf16[256,1024]{1,0:T(8,128)(2,1)S(1)} collective-permute-done((bf16[256,1024]{1,0:T(8,128)(2,1)}, bf16[256,1024]{1,0:T(8,128)(2,1)S(1)}, u32[]{:S(2)}, u32[]{:S(2)}) %collective-permute-start.4) | collective-permute-done | bytes 524320 | tf_op jit(solution)/shard_map/ppermute | solution.py:483
  52.1 25.5 %collective-permute-done.3.refs_3_.refs_1_.refs_2_ = bf16[256,1024]{1,0:T(8,128)(2,1)} collective-permute-done((bf16[256,1024]{1,0:T(8,128)(2,1)}, bf16[256,1024]{1,0:T(8,128)(2,1)}, u32[]{:S(2)}, u32[]{:S(2)}) %collective-permute-start.3) | collective-permute-done | bytes 524320 | tf_op jit(solution)/shard_map/ppermute | solution.py:499
  77.7 4.7 %all-to-all-start.1 = ((bf16[16,80,512]{2,1,0:T(8,128)(2,1)}), bf16[16,80,512]{2,1,0:T(8,128)(2,1)S(1)}, u32[]{:S(2)}, u32[]{:S(2)}) async-start(bf16[16,80,512]{2,1,0:T(8,128)(2,1)} %bitcast.58), calls=%async_computation.1 | async-start | bytes 2621440 | tf_op jit(solution)/shard_map/all_to_all | solution.py:642
  82.4 1.2 collective-permute-start.12
  83.7 2.2 %pick.4.refs_12_ = bf16[256,1024]{1,0:T(8,128)(2,1)} custom-call(s32[1]{0:T(128)} %bitcast.7.refs_0_, bf16[256,1024]{1,0:T(8,128)(2,1)} %collective-permute-done.3.refs_3_.refs_1_.refs_2_, bf16[256,1024]{1,0:T(8,128)(2,1)} %copy-done.39, bf16[256,1024]{1,0:T(8,128)(2,1)} %collective-permute-done.2.refs_2_.refs_3_), custom_call_target="tpu_custom_call" | custom-call | bytes 1048576 | tf_op jit(solution)/shard_map/pick/pallas_call | solution.py:424
  86.1 2.2 %collective-permute-start.9 = (bf16[256,1024]{1,0:T(8,128)(2,1)}, bf16[256,1024]{1,0:T(8,128)(2,1)S(1)}, u32[]{:S(2)}, u32[]{:S(2)}) collective-permute-start(bf16[256,1024]{1,0:T(8,128)(2,1)} %collective-permute-done.3.refs_3_.refs_1_.refs_2_), channel_id=1, source_target_pairs={{4,0},{6,2},{5,1},{7,3},{20,16},{22,18},{21,17},{23,19}} | collective-permute-start | bytes 1572872 | tf_op jit(solution)/shard_map/ppermute | solution.py:499
  88.3 1.3 collective-permute-start.13
  89.7 6.2 %collective-permute-done.12.refs_6_.refs_7_ = bf16[256,1024]{1,0:T(8,128)(2,1)} collective-permute-done((bf16[256,1024]{1,0:T(8,128)(2,1)}, bf16[256,1024]{1,0:T(8,128)(2,1)}, u32[]{:S(2)}, u32[]{:S(2)}) %collective-permute-start.12) | collective-permute-done | bytes 524320 | tf_op jit(solution)/shard_map/ppermute | solution.py:483
  95.9 1.4 collective-permute-start.8
  97.4 1.6 copy-done.29
  99.0 0.9 copy-done.31
  99.9 7.8 %rank_grad_back.1 = (bf16[1280,512]{1,0:T(8,128)(2,1)}, bf16[1280,640]{1,0:T(8,128)(2,1)}, bf16[1280,128]{1,0:T(8,128)(2,1)S(1)}, bf16[1280,128]{1,0:T(8,128)(2,1)S(1)}) custom-call(bf16[16,416,128]{2,1,0:T(8,128)(2,1)} %all-to-all-done.refs_1_.refs_0_, bf16[128,1024]{1,0:T(8,128)(2,1)S(1)} %bitcast.53, bf16[128,8192]{1,0:T(8,128)(2,1)S(1)} %bitcast.51), custom_call_target="tpu_custom_call" | custom-call | flops 2684354560 | bytes 4718592 | tf_op jit(solution)/shard_map/rank_grad_back/pallas_call | solution.py:424
  109.2 6.0 %collective-permute-done.9.refs_3_.refs_1_ = bf16[256,1024]{1,0:T(8,128)(2,1)S(1)} collective-permute-done((bf16[256,1024]{1,0:T(8,128)(2,1)}, bf16[256,1024]{1,0:T(8,128)(2,1)S(1)}, u32[]{:S(2)}, u32[]{:S(2)}) %collective-permute-start.9) | collective-permute-done | bytes 524320 | tf_op jit(solution)/shard_map/ppermute | solution.py:499
  115.1 3.1 %collective-permute-done.13.refs_7_.refs_11_ = bf16[256,1024]{1,0:T(8,128)(2,1)S(1)} collective-permute-done((bf16[256,1024]{1,0:T(8,128)(2,1)}, bf16[256,1024]{1,0:T(8,128)(2,1)S(1)}, u32[]{:S(2)}, u32[]{:S(2)}) %collective-permute-start.13) | collective-permute-done | bytes 524320 | tf_op jit(solution)/shard_map/ppermute | solution.py:483
  118.3 0.8 copy-done.19
  119.3 0.8 copy-done.21
  120.1 1.1 copy-done.6
  121.1 6.8 %all-to-all-start.2 = ((bf16[16,80,512]{2,1,0:T(8,128)(2,1)}), bf16[16,80,512]{2,1,0:T(8,128)(2,1)S(1)}, u32[]{:S(2)}, u32[]{:S(2)}) async-start(bf16[16,80,512]{2,1,0:T(8,128)(2,1)} %bitcast.57), calls=%async_computation.2 | async-start | bytes 2621440 | tf_op jit(solution)/shard_map/all_to_all | solution.py:642
  128.0 1.6 copy-done.11
  129.6 0.9 copy-done.27
  130.5 1.1 for_pair.1
  132.1 2.4 %pick.5.refs_16_ = bf16[256,1024]{1,0:T(8,128)(2,1)} custom-call(s32[1]{0:T(128)} %bitcast.10.refs_0_, bf16[256,1024]{1,0:T(8,128)(2,1)} %copy-done.41, bf16[256,1024]{1,0:T(8,128)(2,1)} %collective-permute-done.3.refs_3_.refs_1_.refs_2_, bf16[256,1024]{1,0:T(8,128)(2,1)} %collective-permute-done.2.refs_2_.refs_3_, ...), custom_call_target="tpu_custom_call" | custom-call | bytes 1048576 | tf_op jit(solution)/shard_map/pick/pallas_call | solution.py:424
  134.7 1.2 collective-permute-start.15
  136.2 1.3 copy-done.7
  137.5 1.6 copy-done.30
  139.1 0.9 copy-done.32
  140.0 1.0 copy-done.36
  141.0 8.6 %lowrank_out.1 = (bf16[1280,640]{1,0:T(8,128)(2,1)}, bf16[1280,128]{1,0:T(8,128)(2,1)S(1)}) custom-call(bf16[16,416,128]{2,1,0:T(8,128)(2,1)} %all-to-all-done.refs_1_.refs_0_, bf16[1280,512]{1,0:T(8,128)(2,1)S(1)} %bitcast.49, bf16[1280,128]{1,0:T(8,128)(2,1)S(1)} %copy-done.36, bf16[128,8192]{1,0:T(8,128)(2,1)S(1)} %bitcast.52, ...), custom_call_target="tpu_custom_call", output_to_operand_aliasing={{0}: (5, {})} | custom-call | flops 2684354560 | bytes 4718592 | tf_op jit(solution)/shard_map/lowrank_out/pallas_call | solution.py:424
  150.3 4.8 %collective-permute-done.14.refs_0_ = bf16[256,1024]{1,0:T(8,128)(2,1)} collective-permute-done((bf16[256,1024]{1,0:T(8,128)(2,1)}, bf16[256,1024]{1,0:T(8,128)(2,1)}, u32[]{:S(2)}, u32[]{:S(2)}) %collective-permute-start.14) | collective-permute-done | bytes 524320 | tf_op jit(solution)/shard_map/ppermute | solution.py:483
  155.1 1.2 collective-permute-start.18
  156.5 2.8 %collective-permute-done.16.refs_4_.refs_15_ = bf16[256,1024]{1,0:T(8,128)(2,1)} collective-permute-done((bf16[256,1024]{1,0:T(8,128)(2,1)}, bf16[256,1024]{1,0:T(8,128)(2,1)}, u32[]{:S(2)}, u32[]{:S(2)}) %collective-permute-start.16) | collective-permute-done | bytes 524320 | tf_op jit(solution)/shard_map/ppermute | solution.py:483
  159.3 1.1 copy-done.2
  160.4 7.9 %all-to-all-start.3 = ((bf16[16,80,640]{2,1,0:T(8,128)(2,1)}), bf16[16,80,640]{2,1,0:T(8,128)(2,1)}, u32[]{:S(2)}, u32[]{:S(2)}) async-start(bf16[16,80,640]{2,1,0:T(8,128)(2,1)} %bitcast.56), calls=%async_computation.3 | async-start | bytes 3276800 | tf_op jit(solution)/shard_map/all_to_all | solution.py:642
  168.3 2.2 %collective-permute-done.18.refs_19_ = bf16[256,1024]{1,0:T(8,128)(2,1)} collective-permute-done((bf16[256,1024]{1,0:T(8,128)(2,1)}, bf16[256,1024]{1,0:T(8,128)(2,1)}, u32[]{:S(2)}, u32[]{:S(2)}) %collective-permute-start.18) | collective-permute-done | bytes 524320 | tf_op jit(solution)/shard_map/ppermute | solution.py:483
  170.5 1.0 copy-done.17
  171.6 1.0 copy-done.18
  172.6 1.0 copy-done.20
  173.7 1.0 copy-done.22
  174.7 1.0 copy-done.23
  175.8 1.0 copy-done.25
  176.8 10.0 %base.1 = (f32[128,1024]{1,0:T(8,128)S(1)}, f32[128,4096]{1,0:T(8,128)}, f32[128,5120]{1,0:T(8,128)}) custom-call(s32[32]{0:T(128)S(1)} %stack.131.refs_0_, bf16[128,8192]{1,0:T(8,128)(2,1)} %refs_1_.5, bf16[128,1024]{1,0:T(8,128)(2,1)S(1)} %copy-done.28, bf16[128,5120]{1,0:T(8,128)(2,1)} %held.11.refs_3_, bf16[256,1024]{1,0:T(8,128)(2,1)S(1)} %copy-done.25, ...), custom_call_target="tpu_custom_call" | custom-call | flops 4294967296 | bytes 8388608 | tf_op jit(solution)/shard_map/base/pallas_call | solution.py:424
  186.8 1.3 collective-permute-start.19
  188.1 6.6 %page_grads.1 = (bf16[128,8192]{1,0:T(8,128)(2,1)}, bf16[128,1024]{1,0:T(8,128)(2,1)}) custom-call(bf16[16,416,128]{2,1,0:T(8,128)(2,1)} %all-to-all-done.refs_1_.refs_0_, bf16[1280,512]{1,0:T(8,128)(2,1)S(1)} %bitcast.50, bf16[1280,128]{1,0:T(8,128)(2,1)S(1)} %copy-done.13, bf16[1280,128]{1,0:T(8,128)(2,1)S(1)} %copy-done.38), custom_call_target="tpu_custom_call" | custom-call | flops 2684354560 | bytes 4718592 | tf_op jit(solution)/shard_map/page_grads/pallas_call | solution.py:424
  194.7 2.7 %combine_first.1.refs_6_ = bf16[128,8192]{1,0:T(8,128)(2,1)} custom-call(s32[1]{0:T(128)} %bitcast.refs_0_, f32[128,128]{1,0:T(8,128)S(1)} %get-tuple-element.20.refs_1_, bf16[16,80,512]{2,1,0:T(8,128)(2,1)S(1)} %copy-done.3, f32[128,4096]{1,0:T(8,128)S(1)} %copy-done.4, f32[128,5120]{1,0:T(8,128)S(1)} %collective-permute-done.19.refs_4_), custom_call_target="tpu_custom_call" | custom-call | flops 1342177280 | bytes 5505024 | tf_op jit(solution)/shard_map/combine_first/pallas_call | solution.py:424
  197.5 8.5 %all-to-all-done.3.refs_2_ = bf16[16,80,640]{2,1,0:T(8,128)(2,1)} async-done(((bf16[16,80,640]{2,1,0:T(8,128)(2,1)}), bf16[16,80,640]{2,1,0:T(8,128)(2,1)}, u32[]{:S(2)}, u32[]{:S(2)}) %all-to-all-start.3) | async-done | bytes 1638432 | tf_op jit(solution)/shard_map/all_to_all | solution.py:642
  206.0 1.6 copy-done.5
  207.6 5.2 %combine_rest.1 = (bf16[128,1024]{1,0:T(8,128)(2,1)}, bf16[128,8192]{1,0:T(8,128)(2,1)}) custom-call(s32[1]{0:T(128)} %bitcast.refs_0_, f32[128,128]{1,0:T(8,128)S(1)} %get-tuple-element.20.refs_1_, bf16[16,80,640]{2,1,0:T(8,128)(2,1)} %all-to-all-done.3.refs_2_, f32[128,4096]{1,0:T(8,128)S(1)} %copy-done.5, ...), custom_call_target="tpu_custom_call", output_to_operand_aliasing={{1}: (6, {})} | custom-call | flops 1342177280 | bytes 5505024 | tf_op jit(solution)/shard_map/combine_rest/pallas_call | solution.py:424
  (91 shorter events, 6.4 us)
Async XLA Ops:
  0.6 1.6 copy-start
  2.3 17.3 %copy-start.24 = (bf16[256,1024]{1,0:T(8,128)(2,1)}, bf16[256,1024]{1,0:T(8,128)(2,1)S(1)}, u32[]{:S(2)}) copy-start(bf16[256,1024]{1,0:T(8,128)(2,1)S(1)} %constant_dynamic-slice_fusion.refs_4_) | copy-start | bytes 1572868
  2.3 14.7 %collective-permute-start.1 = (bf16[256,1024]{1,0:T(8,128)(2,1)S(1)}, bf16[256,1024]{1,0:T(8,128)(2,1)S(1)}, u32[]{:S(2)}, u32[]{:S(2)}) collective-permute-start(bf16[256,1024]{1,0:T(8,128)(2,1)S(1)} %constant_dynamic-slice_fusion.refs_4_), channel_id=1, source_target_pairs={{4,0},{6,2},{8,4},{10,6},{12,8},{14,10},{5,1},{7,3},{9,5},{11,7},{... | collective-permute-start | bytes 1572872 | tf_op jit(solution)/shard_map/ppermute | solution.py:499
  4.4 14.4 %collective-permute-start = (bf16[256,1024]{1,0:T(8,128)(2,1)S(1)}, bf16[256,1024]{1,0:T(8,128)(2,1)S(1)}, u32[]{:S(2)}, u32[]{:S(2)}) collective-permute-start(bf16[256,1024]{1,0:T(8,128)(2,1)S(1)} %constant_dynamic-slice_fusion.refs_4_), channel_id=1, source_target_pairs={{0,4},{2,6},{4,8},{6,10},{8,12},{10,14},{1,5},{3,7},{5,9},{7,11},{... | collective-permute-start | bytes 1572872 | tf_op jit(solution)/shard_map/ppermute | solution.py:497
  7.6 1.6 copy-start.9
  9.2 0.9 copy-start.26
  17.0 1.8 copy-start.39
  18.7 0.8 copy-start.40
  19.6 58.1 %all-to-all-start = ((bf16[16,416,128]{2,1,0:T(8,128)(2,1)}), bf16[16,416,128]{2,1,0:T(8,128)(2,1)}, u32[]{:S(2)}, u32[]{:S(2)}) async-start(bf16[16,416,128]{2,1,0:T(8,128)(2,1)} %held.6), calls=%async_computation | async-start | bytes 3407872 | tf_op jit(solution)/shard_map/all_to_all | solution.py:642
  27.3 13.4 %collective-permute-start.5 = (bf16[256,1024]{1,0:T(8,128)(2,1)}, bf16[256,1024]{1,0:T(8,128)(2,1)S(1)}, u32[]{:S(2)}, u32[]{:S(2)}) collective-permute-start(bf16[256,1024]{1,0:T(8,128)(2,1)} %copy-done.24), channel_id=1, source_target_pairs={{0,16},{16,0},{1,17},{17,1},{2,18},{18,2},{3,19},{19,3},{4,20},{20... | collective-permute-start | bytes 1572872 | tf_op jit(solution)/shard_map/ppermute | solution.py:483
  28.5 23.6 %collective-permute-start.4 = (bf16[256,1024]{1,0:T(8,128)(2,1)}, bf16[256,1024]{1,0:T(8,128)(2,1)S(1)}, u32[]{:S(2)}, u32[]{:S(2)}) collective-permute-start(bf16[256,1024]{1,0:T(8,128)(2,1)} %copy-done.24), channel_id=1, source_target_pairs={{0,2},{2,0},{4,6},{6,4},{8,10},{10,8},{12,14},{14,12},{1,3},{3,1},... | collective-permute-start | bytes 1572872 | tf_op jit(solution)/shard_map/ppermute | solution.py:483
  30.9 46.8 %collective-permute-start.7 = (bf16[256,1024]{1,0:T(8,128)(2,1)}, bf16[256,1024]{1,0:T(8,128)(2,1)}, u32[]{:S(2)}, u32[]{:S(2)}) collective-permute-start(bf16[256,1024]{1,0:T(8,128)(2,1)} %pick.3.refs_8_), channel_id=1, source_target_pairs={{0,16},{16,0},{1,17},{17,1},{2,18},{18,2},{3,19},{19,3},{4,20},{20... | collective-permute-start | bytes 1572872 | tf_op jit(solution)/shard_map/ppermute | solution.py:483
  31.1 46.5 %collective-permute-start.3 = (bf16[256,1024]{1,0:T(8,128)(2,1)}, bf16[256,1024]{1,0:T(8,128)(2,1)}, u32[]{:S(2)}, u32[]{:S(2)}) collective-permute-start(bf16[256,1024]{1,0:T(8,128)(2,1)} %copy-done.39), channel_id=1, source_target_pairs={{4,0},{6,2},{8,4},{10,6},{5,1},{7,3},{9,5},{11,7},{20,16},{22,18},... | collective-permute-start | bytes 1572872 | tf_op jit(solution)/shard_map/ppermute | solution.py:499
  33.1 44.6 %collective-permute-start.6 = (bf16[256,1024]{1,0:T(8,128)(2,1)}, bf16[256,1024]{1,0:T(8,128)(2,1)}, u32[]{:S(2)}, u32[]{:S(2)}) collective-permute-start(bf16[256,1024]{1,0:T(8,128)(2,1)} %pick.3.refs_8_), channel_id=1, source_target_pairs={{0,2},{2,0},{4,6},{6,4},{8,10},{10,8},{12,14},{14,12},{1,3},{3,1},... | collective-permute-start | bytes 1572872 | tf_op jit(solution)/shard_map/ppermute | solution.py:483
  40.7 8.8 %copy-start.14 = (bf16[256,1024]{1,0:T(8,128)(2,1)}, bf16[256,1024]{1,0:T(8,128)(2,1)S(1)}, u32[]{:S(2)}) copy-start(bf16[256,1024]{1,0:T(8,128)(2,1)S(1)} %collective-permute-done.5.refs_5_.refs_6_) | copy-start | bytes 1572868
  40.7 37.0 %collective-permute-start.2 = (bf16[256,1024]{1,0:T(8,128)(2,1)}, bf16[256,1024]{1,0:T(8,128)(2,1)}, u32[]{:S(2)}, u32[]{:S(2)}) collective-permute-start(bf16[256,1024]{1,0:T(8,128)(2,1)} %copy-done.40), channel_id=1, source_target_pairs={{4,8},{6,10},{8,12},{10,14},{5,9},{7,11},{9,13},{11,15},{20,24},{2... | collective-permute-start | bytes 1572872 | tf_op jit(solution)/shard_map/ppermute | solution.py:497
  44.7 1.6 copy-start.10
  52.1 25.6 %copy-start.16 = (bf16[256,1024]{1,0:T(8,128)(2,1)}, bf16[256,1024]{1,0:T(8,128)(2,1)S(1)}, u32[]{:S(2)}) copy-start(bf16[256,1024]{1,0:T(8,128)(2,1)S(1)} %collective-permute-done.4.refs_4_.refs_5_) | copy-start | bytes 1572868
  77.7 42.3 %all-to-all-start.1 = ((bf16[16,80,512]{2,1,0:T(8,128)(2,1)}), bf16[16,80,512]{2,1,0:T(8,128)(2,1)S(1)}, u32[]{:S(2)}, u32[]{:S(2)}) async-start(bf16[16,80,512]{2,1,0:T(8,128)(2,1)} %bitcast.58), calls=%async_computation.1 | async-start | bytes 2621440 | tf_op jit(solution)/shard_map/all_to_all | solution.py:642
  82.4 13.5 %collective-permute-start.12 = (bf16[256,1024]{1,0:T(8,128)(2,1)}, bf16[256,1024]{1,0:T(8,128)(2,1)}, u32[]{:S(2)}, u32[]{:S(2)}) collective-permute-start(bf16[256,1024]{1,0:T(8,128)(2,1)} %copy-done.16), channel_id=1, source_target_pairs={{0,16},{16,0},{1,17},{17,1},{2,18},{18,2},{3,19},{19,3},{4,20},{20... | collective-permute-start | bytes 1572872 | tf_op jit(solution)/shard_map/ppermute | solution.py:483
  85.9 32.4 %collective-permute-start.11 = (bf16[256,1024]{1,0:T(8,128)(2,1)}, bf16[256,1024]{1,0:T(8,128)(2,1)S(1)}, u32[]{:S(2)}, u32[]{:S(2)}) collective-permute-start(bf16[256,1024]{1,0:T(8,128)(2,1)} %pick.4.refs_12_), channel_id=1, source_target_pairs={{0,16},{16,0},{1,17},{17,1},{2,18},{18,2},{3,19},{19,3},{4,20},{20... | collective-permute-start | bytes 1572872 | tf_op jit(solution)/shard_map/ppermute | solution.py:483
  86.1 29.0 %collective-permute-start.9 = (bf16[256,1024]{1,0:T(8,128)(2,1)}, bf16[256,1024]{1,0:T(8,128)(2,1)S(1)}, u32[]{:S(2)}, u32[]{:S(2)}) collective-permute-start(bf16[256,1024]{1,0:T(8,128)(2,1)} %collective-permute-done.3.refs_3_.refs_1_.refs_2_), channel_id=1, source_target_pairs={{4,0},{6,2},{5,1},{7,3},{20,16},{22,18},{21,17},{23,19}} | collective-permute-start | bytes 1572872 | tf_op jit(solution)/shard_map/ppermute | solution.py:499
  88.3 29.9 %collective-permute-start.13 = (bf16[256,1024]{1,0:T(8,128)(2,1)}, bf16[256,1024]{1,0:T(8,128)(2,1)S(1)}, u32[]{:S(2)}, u32[]{:S(2)}) collective-permute-start(bf16[256,1024]{1,0:T(8,128)(2,1)} %collective-permute-done.6.refs_6_.refs_9_), channel_id=1, source_target_pairs={{0,16},{16,0},{1,17},{17,1},{2,18},{18,2},{3,19},{19,3},{4,20},{20... | collective-permute-start | bytes 1572872 | tf_op jit(solution)/shard_map/ppermute | solution.py:483
  89.6 28.7 %collective-permute-start.10 = (bf16[256,1024]{1,0:T(8,128)(2,1)}, bf16[256,1024]{1,0:T(8,128)(2,1)S(1)}, u32[]{:S(2)}, u32[]{:S(2)}) collective-permute-start(bf16[256,1024]{1,0:T(8,128)(2,1)} %pick.4.refs_12_), channel_id=1, source_target_pairs={{0,2},{2,0},{4,6},{6,4},{8,10},{10,8},{12,14},{14,12},{1,3},{3,1},... | collective-permute-start | bytes 1572872 | tf_op jit(solution)/shard_map/ppermute | solution.py:483
  95.9 24.1 %collective-permute-start.8 = (bf16[256,1024]{1,0:T(8,128)(2,1)}, bf16[256,1024]{1,0:T(8,128)(2,1)}, u32[]{:S(2)}, u32[]{:S(2)}) collective-permute-start(bf16[256,1024]{1,0:T(8,128)(2,1)} %collective-permute-done.2.refs_2_.refs_3_), channel_id=1, source_target_pairs={{8,12},{10,14},{9,13},{11,15},{24,28},{26,30},{25,29},{27,31}} | collective-permute-start | bytes 1572872 | tf_op jit(solution)/shard_map/ppermute | solution.py:497
  97.4 1.6 copy-start.29
  98.9 0.9 copy-start.31
  107.7 0.8 copy-start.35
  108.4 0.7 copy-start.37
  115.1 3.2 %copy-start.41 = (bf16[256,1024]{1,0:T(8,128)(2,1)}, bf16[256,1024]{1,0:T(8,128)(2,1)S(1)}, u32[]{:S(2)}) copy-start(bf16[256,1024]{1,0:T(8,128)(2,1)S(1)} %collective-permute-done.9.refs_3_.refs_1_) | copy-start | bytes 1572868
  118.3 0.8 copy-start.19
  118.3 1.0 copy-start.42
  119.3 0.8 copy-start.21
  120.1 1.1 copy-start.6
  121.1 38.2 %all-to-all-start.2 = ((bf16[16,80,512]{2,1,0:T(8,128)(2,1)}), bf16[16,80,512]{2,1,0:T(8,128)(2,1)S(1)}, u32[]{:S(2)}, u32[]{:S(2)}) async-start(bf16[16,80,512]{2,1,0:T(8,128)(2,1)} %bitcast.57), calls=%async_computation.2 | async-start | bytes 2621440 | tf_op jit(solution)/shard_map/all_to_all | solution.py:642
  128.0 1.6 copy-start.11
  129.6 0.9 copy-start.27
  131.6 24.8 %collective-permute-start.17 = (bf16[128,5120]{1,0:T(8,128)(2,1)}, bf16[128,5120]{1,0:T(8,128)(2,1)}, u32[]{:S(2)}, u32[]{:S(2)}) collective-permute-start(bf16[128,5120]{1,0:T(8,128)(2,1)} %for_pair.1), channel_id=1, source_target_pairs={{0,1},{1,0},{2,3},{3,2},{4,5},{5,4},{6,7},{7,6},{8,9},{9,8},{10,11... | collective-permute-start | bytes 3932168 | tf_op jit(solution)/shard_map/ppermute | solution.py:483
  134.4 20.7 %collective-permute-start.14 = (bf16[256,1024]{1,0:T(8,128)(2,1)}, bf16[256,1024]{1,0:T(8,128)(2,1)}, u32[]{:S(2)}, u32[]{:S(2)}) collective-permute-start(bf16[256,1024]{1,0:T(8,128)(2,1)} %pick.5.refs_16_), channel_id=1, source_target_pairs={{0,2},{2,0},{4,6},{6,4},{8,10},{10,8},{12,14},{14,12},{1,3},{3,1},... | collective-permute-start | bytes 1572872 | tf_op jit(solution)/shard_map/ppermute | solution.py:483
  134.7 24.6 %collective-permute-start.15 = (bf16[256,1024]{1,0:T(8,128)(2,1)}, bf16[256,1024]{1,0:T(8,128)(2,1)}, u32[]{:S(2)}, u32[]{:S(2)}) collective-permute-start(bf16[256,1024]{1,0:T(8,128)(2,1)} %pick.5.refs_16_), channel_id=1, source_target_pairs={{0,16},{16,0},{1,17},{17,1},{2,18},{18,2},{3,19},{19,3},{4,20},{20... | collective-permute-start | bytes 1572872 | tf_op jit(solution)/shard_map/ppermute | solution.py:483
  135.9 23.4 %collective-permute-start.16 = (bf16[256,1024]{1,0:T(8,128)(2,1)}, bf16[256,1024]{1,0:T(8,128)(2,1)}, u32[]{:S(2)}, u32[]{:S(2)}) collective-permute-start(bf16[256,1024]{1,0:T(8,128)(2,1)} %copy-done.21), channel_id=1, source_target_pairs={{0,16},{16,0},{1,17},{17,1},{2,18},{18,2},{3,19},{19,3},{4,20},{20... | collective-permute-start | bytes 1572872 | tf_op jit(solution)/shard_map/ppermute | solution.py:483
  136.2 1.3 copy-start.7
  137.5 1.6 copy-start.30
  139.1 0.9 copy-start.32
  140.0 1.0 copy-start.36
  155.1 15.4 %collective-permute-start.18 = (bf16[256,1024]{1,0:T(8,128)(2,1)}, bf16[256,1024]{1,0:T(8,128)(2,1)}, u32[]{:S(2)}, u32[]{:S(2)}) collective-permute-start(bf16[256,1024]{1,0:T(8,128)(2,1)} %held.9.refs_2_.refs_17_), channel_id=1, source_target_pairs={{0,16},{16,0},{1,17},{17,1},{2,18},{18,2},{3,19},{19,3},{4,20},{20... | collective-permute-start | bytes 1572872 | tf_op jit(solution)/shard_map/ppermute | solution.py:483
  159.3 1.1 copy-start.2
  160.4 10.2 %copy-start.15 = (bf16[256,1024]{1,0:T(8,128)(2,1)S(1)}, bf16[256,1024]{1,0:T(8,128)(2,1)}, u32[]{:S(2)}) copy-start(bf16[256,1024]{1,0:T(8,128)(2,1)} %copy-done.14) | copy-start | bytes 1572868
  160.4 10.2 %copy-start.28 = (bf16[128,1024]{1,0:T(8,128)(2,1)S(1)}, bf16[128,1024]{1,0:T(8,128)(2,1)}, u32[]{:S(2)}) copy-start(bf16[128,1024]{1,0:T(8,128)(2,1)} %refs_2_.5) | copy-start | bytes 786436
  160.4 45.6 %all-to-all-start.3 = ((bf16[16,80,640]{2,1,0:T(8,128)(2,1)}), bf16[16,80,640]{2,1,0:T(8,128)(2,1)}, u32[]{:S(2)}, u32[]{:S(2)}) async-start(bf16[16,80,640]{2,1,0:T(8,128)(2,1)} %bitcast.56), calls=%async_computation.3 | async-start | bytes 3276800 | tf_op jit(solution)/shard_map/all_to_all | solution.py:642
  168.3 19.8 %copy-start.8 = (bf16[16,80,512]{2,1,0:T(8,128)(2,1)S(1)}, bf16[16,80,512]{2,1,0:T(8,128)(2,1)}, u32[]{:S(2)}) copy-start(bf16[16,80,512]{2,1,0:T(8,128)(2,1)} %copy-done.6) | copy-start | bytes 3932164
  168.3 19.8 %copy-start.13 = (bf16[1280,128]{1,0:T(8,128)(2,1)S(1)}, bf16[1280,128]{1,0:T(8,128)(2,1)}, u32[]{:S(2)}) copy-start(bf16[1280,128]{1,0:T(8,128)(2,1)} %copy-done.12) | copy-start | bytes 983044
  170.5 1.0 copy-start.17
  171.6 1.0 copy-start.18
  172.6 1.0 copy-start.20
  173.7 1.0 copy-start.22
  174.7 1.0 copy-start.23
  175.8 1.0 copy-start.25
  176.8 11.3 %copy-start.38 = (bf16[1280,128]{1,0:T(8,128)(2,1)S(1)}, bf16[1280,128]{1,0:T(8,128)(2,1)}, u32[]{:S(2)}) copy-start(bf16[1280,128]{1,0:T(8,128)(2,1)} %copy-done.37) | copy-start | bytes 983044
  186.8 7.9 %collective-permute-start.19 = (f32[128,5120]{1,0:T(8,128)}, f32[128,5120]{1,0:T(8,128)S(1)}, u32[]{:S(2)}, u32[]{:S(2)}) collective-permute-start(f32[128,5120]{1,0:T(8,128)} %get-tuple-element.29), channel_id=1, source_target_pairs={{0,1},{1,0},{2,3},{3,2},{4,5},{5,4},{6,7},{7,6},{8,9},{9,8},{10,11... | collective-permute-start | bytes 7864328 | tf_op jit(solution)/shard_map/ppermute | solution.py:483
  188.1 6.6 %copy-start.3 = (bf16[16,80,512]{2,1,0:T(8,128)(2,1)S(1)}, bf16[16,80,512]{2,1,0:T(8,128)(2,1)}, u32[]{:S(2)}) copy-start(bf16[16,80,512]{2,1,0:T(8,128)(2,1)} %copy-done.2) | copy-start | bytes 3932164
  188.1 6.6 %copy-start.4 = (f32[128,4096]{1,0:T(8,128)S(1)}, f32[128,4096]{1,0:T(8,128)}, u32[]{:S(2)}) copy-start(f32[128,4096]{1,0:T(8,128)} %get-tuple-element.28.refs_3_) | copy-start | bytes 6291460
  194.7 2.8 %copy-start.1 = (f32[128,5120]{1,0:T(8,128)}, f32[128,5120]{1,0:T(8,128)S(1)}, u32[]{:S(2)}) copy-start(f32[128,5120]{1,0:T(8,128)S(1)} %collective-permute-done.19.refs_4_) | copy-start | bytes 7864324
  206.0 1.6 copy-start.5
  (3 other events, 2.0 us)

commit v3 on v2

v3 whole, which is shorter than its diff:
```python
import functools

import jax
import jax.numpy as jnp
from jax import lax
from jax.experimental import pallas as pl
from jax.experimental.pallas import tpu as pltpu
from jax.sharding import PartitionSpec as P

RANK = 32
CHUNKS = 8
FIRST = 4
VMEM_LIMIT = 60 * 1024 * 1024

adapter_scale = 2.0

F32 = jnp.float32
BF16 = jnp.bfloat16
NT = (((1,), (1,)), ((), ()))
TN = (((0,), (0,)), ((), ()))


def iota(shape, dim):
    return lax.broadcasted_iota(jnp.int32, shape, dim)


def piece_and_slot(index, cap):
    piece = jnp.zeros_like(index)
    for k in range(1, CHUNKS + 1):
        piece = piece + (index >= k * cap).astype(jnp.int32)
    return piece, index - piece * cap


def spread_mask(rows, cap, lanes):
    block = CHUNKS * cap
    piece, _ = piece_and_slot(iota((block, CHUNKS * lanes), 0), cap)
    group = jnp.zeros_like(piece)
    lane = iota(piece.shape, 1)
    for k in range(1, CHUNKS):
        group = group + (lane >= k * lanes).astype(jnp.int32)
    mask = (piece == group).astype(F32).astype(BF16)
    return jnp.concatenate([mask] * (rows // block), axis=0)


def spread(rows, cap):
    return jnp.concatenate([rows] * CHUNKS, axis=1) * spread_mask(
        rows.shape[0], cap, rows.shape[1]
    )


def pick_piece(wide, cap, lanes):
    block, n = CHUNKS * cap, wide.shape[0]
    piece, _ = piece_and_slot(iota((block, lanes), 0), cap)
    piece = jnp.concatenate([piece] * (n // block), axis=0)
    total = jnp.zeros((n, lanes), F32)
    for k in range(CHUNKS):
        total = total + jnp.where(piece == k, wide[:, k * lanes : (k + 1) * lanes], 0.0)
    return total


def same_slot(cap):
    shape = (CHUNKS * cap, CHUNKS * cap)
    _, slot = piece_and_slot(iota(shape, 0), cap)
    _, slot_c = piece_and_slot(iota(shape, 1), cap)
    return (slot == slot_c).astype(F32)


def fold_pieces(fold, part):
    terms, left = [], part
    for _ in range(3):
        terms.append(left.astype(BF16))
        left = left - terms[-1].astype(F32)
    wide = jnp.dot(
        fold.astype(BF16), jnp.concatenate(terms, axis=1), preferred_element_type=F32
    )
    n = part.shape[1]
    return wide[:, 0:n] + (wide[:, n : 2 * n] + wide[:, 2 * n :])


def load_pieces(src, dst, sem, height, stride, start, width):
    return [
        pltpu.make_async_copy(
            src.at[:, pl.ds(k * stride + start, width)],
            dst.at[pl.ds(k * height, height), pl.ds(0, width)],
            sem.at[k],
        )
        for k in range(CHUNKS)
    ]


def start_all(copies):
    for copy in copies:
        copy.start()


def wait_all(copies):
    for copy in copies:
        copy.wait()


def rows_of_slots(slot, cap, first, group):
    _, slot_of = piece_and_slot(iota((CHUNKS * cap, slot.shape[1]), 0), cap)
    return jnp.concatenate(
        [
            (slot == (slot_of + (first + d) * cap).astype(F32)).astype(F32).astype(BF16)
            for d in range(group)
        ],
        axis=0,
    )


def earlier_rows(rows):
    return (iota((rows, rows), 0) < iota((rows, rows), 1)).astype(F32).astype(BF16)


def grad_pieces(ref, block):
    return jnp.concatenate([ref[d, 0:block, :] for d in range(ref.shape[0])], axis=0)


def route_kernel(
    devices, cap, per_page, owner_ref, tenant_ref, grads_ref, send_ref, row_ref, col_ref
):
    rows = tenant_ref.shape[1]
    height, lanes = send_ref.shape[1:]
    block = CHUNKS * cap
    page = tenant_ref[...] // per_page
    member = tenant_ref[...] - page * per_page

    def add_page(p, target):
        return target + jnp.where(page == p, owner_ref[p], 0)

    target = lax.fori_loop(0, owner_ref.shape[0], add_page, jnp.zeros_like(page))
    chosen = (iota((devices, rows), 0) == target).astype(F32)
    before = jnp.dot(chosen.astype(BF16), earlier_rows(rows), preferred_element_type=F32)
    slot = target.astype(F32) * cap + jnp.sum(before * chosen, axis=0, keepdims=True)
    row_ref[...] = slot
    col_ref[...] = jnp.transpose(jnp.broadcast_to(slot, (rows, rows)))

    pieces = jnp.concatenate(
        [grads_ref[:, k * lanes : (k + 1) * lanes] for k in range(CHUNKS)], axis=0
    )
    here = spread(rows_of_slots(slot, cap, 0, devices), cap)
    packed = jnp.dot(here, pieces, preferred_element_type=F32).astype(BF16)
    of_member = (iota((lanes, rows), 0) // RANK == member).astype(F32).astype(BF16)
    tail = iota((height - block, rows), 0)
    tail = jnp.where(tail < cap, tail, -(10**6))
    in_slot = jnp.concatenate(
        [(slot == (tail + d * cap).astype(F32)).astype(F32).astype(BF16) for d in range(devices)],
        axis=0,
    )
    masks = lax.dot_general(in_slot, of_member, NT, preferred_element_type=F32).astype(BF16)
    extra = height - block
    for d in range(devices):
        send_ref[d, 0:block, :] = packed[d * block : (d + 1) * block, :]
        send_ref[d, block:, :] = masks[d * extra : (d + 1) * extra, :]


def dispatch_kernel(cap, slot_ref, tokens_ref, out_ref, pieces, sem):
    step = pl.program_id(0)
    rows, width = slot_ref.shape[1], pieces.shape[1]
    group = out_ref.shape[0] // (CHUNKS * cap)

    @pl.when(step == 0)
    def _():
        copies = load_pieces(tokens_ref, pieces, sem, rows, width, 0, width)
        start_all(copies)
        wait_all(copies)

    here = rows_of_slots(slot_ref[...], cap, step * group, group)
    out_ref[...] = jnp.dot(spread(here, cap), pieces[...], preferred_element_type=F32).astype(BF16)


def back_kernel(
    cap, got_ref, b_ref, a_ref, first_ref, second_ref, rank_ref, mask_ref, pieces, sem
):
    step = pl.program_id(0)
    ranks = b_ref.shape[0]
    group, height, width = got_ref.shape
    block = CHUNKS * cap
    split = first_ref.shape[1]
    rest = pieces.shape[1] - split
    copies = load_pieces(a_ref, pieces, sem, ranks, split + rest, 0, split + rest)

    @pl.when(step == 0)
    def _():
        start_all(copies)

    tail = height - block
    _, slot = piece_and_slot(iota((block, tail), 0), cap)
    pick_mask = (iota((block, tail), 1) == slot).astype(F32).astype(BF16)
    b_pieces = jnp.concatenate(
        [b_ref[:, k * width : (k + 1) * width] for k in range(CHUNKS)], axis=0
    )
    wide = lax.dot_general(
        grad_pieces(got_ref, block), b_pieces, NT, preferred_element_type=F32
    )
    part = pick_piece(wide, cap, ranks)
    fold = same_slot(cap)
    ranks_of = []
    for d in range(group):
        at = slice(d * block, (d + 1) * block)
        full = fold_pieces(fold, part[at, :])
        mask = jnp.dot(pick_mask, got_ref[d, block:, :], preferred_element_type=F32)
        ranks_of.append((full * mask).astype(BF16))
        mask_ref[at, :] = mask.astype(BF16)
    rank_rows = jnp.concatenate(ranks_of, axis=0)
    rank_ref[...] = rank_rows

    @pl.when(step == 0)
    def _():
        wait_all(copies)

    back = (
        adapter_scale * jnp.dot(spread(rank_rows, cap), pieces[...], preferred_element_type=F32)
    ).astype(BF16)
    first_ref[...] = back[:, 0:split]
    second_ref[:, 0:rest] = back[:, split:]
    second_ref[:, rest:] = jnp.zeros((second_ref.shape[0], second_ref.shape[1] - rest), BF16)


def forth_kernel(
    cap, tok_ref, mask_ref, a_ref, b_ref, _, out_ref, rank_ref, pieces, sem
):
    step = pl.program_id(0)
    ranks = b_ref.shape[0]
    block = CHUNKS * cap
    width = out_ref.shape[1]
    wide_piece = pieces.shape[1]
    group = tok_ref.shape[0] // block

    @pl.when(step == 0)
    def _():
        copies = load_pieces(a_ref, pieces, sem, ranks, wide_piece, 0, wide_piece)
        start_all(copies)
        wait_all(copies)

    b_pieces = jnp.concatenate(
        [b_ref[:, k * width : (k + 1) * width] for k in range(CHUNKS)], axis=0
    )
    wide = lax.dot_general(tok_ref[...], pieces[...], NT, preferred_element_type=F32)
    part = pick_piece(wide, cap, ranks)
    fold = same_slot(cap)
    full = jnp.concatenate(
        [
            fold_pieces(fold, part[d * block : (d + 1) * block, :])
            for d in range(group)
        ],
        axis=0,
    )
    rank_rows = (full * mask_ref[...].astype(F32)).astype(BF16)
    rank_ref[...] = rank_rows
    out_ref[...] = (
        adapter_scale * jnp.dot(spread(rank_rows, cap), b_pieces, preferred_element_type=F32)
    ).astype(BF16)


def page_grad_kernel(cap, tok_ref, grad_ref, low_ref, rank_ref, ga_ref, gb_ref):
    ranks = rank_ref.shape[1]
    wide, narrow = tok_ref.shape[1], grad_ref.shape[2]
    left = lax.dot_general(
        spread(rank_ref[...], cap), tok_ref[...], TN, preferred_element_type=F32
    )
    grads = grad_pieces(grad_ref, CHUNKS * cap)
    right = lax.dot_general(spread(low_ref[...], cap), grads, TN, preferred_element_type=F32)
    for k in range(CHUNKS):
        at = slice(k * ranks, (k + 1) * ranks)
        ga_ref[:, k * wide : (k + 1) * wide] = (adapter_scale * left[at, :]).astype(BF16)
        gb_ref[:, k * narrow : (k + 1) * narrow] = (adapter_scale * right[at, :]).astype(BF16)


def pair_kernel(other_ref, tokens_ref, grads_ref, out_ref, sem):
    rows, narrow = grads_ref.shape
    half = (out_ref.shape[1] - narrow) // CHUNKS
    at = pl.multiple_of(other_ref[0] * half, half)
    copies = [
        pltpu.make_async_copy(
            tokens_ref.at[:, pl.ds(2 * k * half + at, half)],
            out_ref.at[:, pl.ds(k * half, half)],
            sem.at[k],
        )
        for k in range(CHUNKS)
    ]
    copies.append(
        pltpu.make_async_copy(
            grads_ref, out_ref.at[:, pl.ds(CHUNKS * half, narrow)], sem.at[CHUNKS]
        )
    )
    start_all(copies)
    wait_all(copies)


def pair_base_kernel(at_ref, tok_ref, grad_ref, pair_ref, *refs):
    weights, (out_ref, back_ref, theirs_ref) = refs[:-3], refs[-3:]
    rows, narrow = grad_ref.shape
    half_width = back_ref.shape[1]
    grads = jnp.concatenate([grad_ref[...], pair_ref[:, half_width:]], axis=0)
    total = jnp.zeros((2 * rows, narrow), F32)
    share = 2 * half_width // at_ref.shape[0]
    parts = [ref.at[pl.ds(r, share), :] for ref in weights for r in range(0, ref.shape[0], share)]
    for n, ref in enumerate(parts):
        weight = ref[...]
        full = pl.multiple_of(at_ref[2 * n] * share, share)
        part = pl.multiple_of(at_ref[2 * n + 1] * share, share)
        toks = jnp.concatenate(
            [tok_ref[:, pl.ds(full, share)], pair_ref[:, pl.ds(part, share)]], axis=0
        )
        total = total + jnp.dot(toks, weight, preferred_element_type=F32)
        back = lax.dot_general(grads, weight, NT, preferred_element_type=F32)
        back_ref[:, pl.ds(part, share)] = back[0:rows, :]
        theirs_ref[:, pl.ds(part, share)] = back[rows:, :]
    out_ref[...] = total[0:rows, :]
    theirs_ref[:, half_width:] = total[rows:, :]


def base_kernel(tok_ref, grad_ref, w_ref, out_ref, back_ref):
    @pl.when(pl.program_id(0) == 0)
    def _():
        out_ref[...] = jnp.zeros_like(out_ref)

    weight = w_ref[...]
    out_ref[...] += jnp.dot(tok_ref[...], weight, preferred_element_type=F32)
    back_ref[...] = lax.dot_general(grad_ref[...], weight, NT, preferred_element_type=F32)


def combine_kernel(cap, start, which_ref, col_ref, got_ref, mine_ref, pair_ref, *refs):
    out_hbm, out, sem, base, base_sem = refs[-5:]
    devices, block, width = got_ref.shape
    cols = out.shape[2]
    rows = col_ref.shape[0]
    piece = out_hbm.shape[1] // CHUNKS
    parts = 2 if mine_ref.shape[1] < out_hbm.shape[1] else 1
    size = piece // parts

    def load(ref, part):
        low, high = max(start, part * size), min(start + cols, (part + 1) * size)
        if low < high:
            start_all(
                [
                    pltpu.make_async_copy(
                        ref.at[:, pl.ds(k * size + low - part * size, high - low)],
                        base.at[k, :, pl.ds(low - start, high - low)],
                        base_sem.at[k],
                    )
                    for k in range(CHUNKS)
                ]
            )

    if parts == 1:
        load(mine_ref, 0)
    else:
        for n in range(2):

            @pl.when(which_ref[0] == n)
            def _():
                load(mine_ref, n)
                load(pair_ref, 1 - n)

    col = col_ref[:, 0:1]
    copies = []
    for k in range(CHUNKS):
        low = k * cap // 16 * 16
        high = min(-(-(k + 1) * cap // 16) * 16, block)
        count = high - low
        lane = iota((1, devices * count), 1)
        row = jnp.zeros_like(lane)
        for d in range(1, devices):
            row = row + (lane >= d * count).astype(jnp.int32)
        slot = lane - row * count + (low - k * cap)
        key = jnp.where((slot >= 0) & (slot < cap), row * cap + slot, -1).astype(F32)
        here = (col == key).astype(F32).astype(BF16)
        packed = jnp.concatenate([got_ref[d, low:high, :] for d in range(devices)], axis=0)
        back = jnp.dot(here, packed, preferred_element_type=F32)
        pltpu.make_async_copy(base.at[k], base.at[k], base_sem.at[k]).wait()
        out[k] = (base[k] + back[:, 0:cols]).astype(BF16)
        copy = pltpu.make_async_copy(
            out.at[k], out_hbm.at[:, pl.ds(k * piece + start, cols)], sem.at[k]
        )
        copy.start()
        copies.append(copy)
        if width > cols:
            outs, projected_ref = refs[: len(refs) - 7], refs[-6]
            at = slice(k * (width - cols), (k + 1) * (width - cols))
            total = sum(ref[:, at] for ref in outs)
            projected_ref[:, at] = (total + back[:, cols:]).astype(BF16)
    wait_all(copies)


def call(kernel, deps=(), **options):
    specs = list(options.pop("in_specs"))
    count, extra = len(specs), len(deps)

    def body(*refs):
        kernel(*refs[:count], *refs[count + extra :])

    run = pl.pallas_call(
        body, in_specs=specs + [pl.BlockSpec(memory_space=pl.ANY)] * extra, **options
    )
    return lambda *args: run(*args, *deps)


def hbm(*arrays):
    kept = tuple(pltpu.with_memory_space_constraint(x, pltpu.HBM) for x in arrays)
    return kept if len(kept) > 1 else kept[0]


def held(x, deps):
    deps = tuple(deps)
    if not deps:
        return x
    any_spec = pl.BlockSpec(memory_space=pl.ANY)
    return call(
        lambda x_ref, out_ref: None,
        deps=deps,
        out_shape=in_hbm(x.shape, x.dtype),
        in_specs=[any_spec],
        out_specs=any_spec,
        input_output_aliases={0: 0},
        compiler_params=params(),
        cost_estimate=cost(0, 0),
        name="held",
    )(x)


def pick_kernel(count, which_ref, *refs):
    for n in range(count):

        @pl.when(which_ref[0] == n)
        def _():
            refs[count][...] = refs[n][...]


def pick(which, *arrays):
    x = arrays[0]
    return call(
        functools.partial(pick_kernel, len(arrays)),
        out_shape=in_hbm(x.shape, x.dtype),
        in_specs=[pl.BlockSpec(memory_space=pltpu.SMEM)]
        + [pl.BlockSpec(memory_space=pltpu.VMEM)] * len(arrays),
        out_specs=pl.BlockSpec(memory_space=pltpu.VMEM),
        compiler_params=params(),
        cost_estimate=cost(0, 2 * x.size * x.dtype.itemsize),
        name="pick",
    )(which.astype(jnp.int32).reshape(1), *arrays)


def in_hbm(shape, dtype):
    return pltpu.HBM(shape, dtype)


def whole(shape):
    return pl.BlockSpec(shape, lambda *_: (0,) * len(shape))


def params(semantics=None):
    return pltpu.CompilerParams(vmem_limit_bytes=VMEM_LIMIT, dimension_semantics=semantics)


def cost(flops, nbytes):
    return pl.CostEstimate(flops=1, bytes_accessed=1, transcendentals=0)


def swap(x, axis):
    size = lax.axis_size(axis)
    return lax.ppermute(x, axis, [(i, i ^ 1) for i in range(size)])


def gather_shares(base_weight, inner):
    count = lax.axis_size("fsdp")
    z = lax.axis_index("fsdp") // inner
    share = base_weight.shape[0] // 4
    at = lax.axis_index("tenant") * 2 + lax.axis_index("groups")
    mine = lax.dynamic_slice_in_dim(base_weight, at * share, share, 0)

    up_pairs = [(i, i + inner) for i in range(count - inner)]
    up, down = [mine], [mine]
    for j in range(1, 4):
        moved = [p for p in up_pairs if p[0] // inner >= j - 1]
        up.append(lax.ppermute(up[-1], "fsdp", moved))
        moved = [(b, a) for a, b in up_pairs if b // inner <= 4 - j]
        down.append(lax.ppermute(down[-1], "fsdp", moved))

    def of_z(*values):
        return functools.reduce(
            lambda rest, k: jnp.where(z == k, values[k], rest), range(3), values[3]
        )

    held_shares = [
        (mine, [z]),
        (pick(of_z(0, 1, 1, 1), down[1], up[1]), [of_z(1, 0, 1, 2)]),
        (pick(of_z(0, 1, 1, 2), down[2], down[1], up[2]), [of_z(2, 2, 3, 1)]),
        (pick(of_z(0, 1, 2, 3), down[3], down[2], up[2], up[3]), [of_z(3, 3, 0, 0)]),
    ]
    blocks, y_of, x_of, both_of = [], [], [], []

    def spread_share(n, deps=()):
        own, place = held_shares[n]
        y_of.append(held(swap(own, "fsdp"), deps))
        x_of.append(swap(own, "groups"))
        both_of.append(swap(y_of[n], "groups"))
        blocks.extend(
            [
                (own, place, 0, 0),
                (y_of[n], place, 1, 0),
                (x_of[n], place, 0, 1),
                (both_of[n], place, 1, 1),
            ]
        )

    for n in range(3):
        spread_share(n)
    after = {
        "first": [up[2], down[2], y_of[0], x_of[0]],
        "third": [up[3], down[3], y_of[1], x_of[1], both_of[0], y_of[2], x_of[2], both_of[1]],
    }

    def last(deps):
        spread_share(3, deps)
        return [y_of[3], x_of[3]]

    return {"blocks": blocks, "after": after, "last": last}


def for_pair(tokens, grad_out):
    rows, width = tokens.shape
    narrow = grad_out.shape[1]
    any_spec = pl.BlockSpec(memory_space=pl.ANY)
    other = (1 - lax.axis_index("tenant")).astype(jnp.int32).reshape(1)
    return call(
        pair_kernel,
        out_shape=in_hbm((rows, width // 2 + narrow), BF16),
        in_specs=[pl.BlockSpec(memory_space=pltpu.SMEM), any_spec, any_spec],
        out_specs=pl.BlockSpec(memory_space=pltpu.VMEM),
        scratch_shapes=[pltpu.SemaphoreType.DMA((CHUNKS + 1,))],
        compiler_params=params(),
        cost_estimate=cost(0, 4 * rows * (width // 2 + narrow)),
        name="for_pair",
    )(other, tokens, grad_out)


def paired_base(tokens, grad_out, pair, shares, fsdp_size, inner):
    rows, width = tokens.shape
    narrow = grad_out.shape[1]
    tenant, group = lax.axis_index("tenant"), lax.axis_index("groups")
    fsdp = lax.axis_index("fsdp")
    y = fsdp % inner
    gathered = shares["blocks"]
    any_spec = pl.BlockSpec(memory_space=pl.ANY)
    vmem = pl.BlockSpec(memory_space=pltpu.VMEM)
    smem = pl.BlockSpec(memory_space=pltpu.SMEM)

    half = width // 2
    at = []
    for _, places, dy, dx in gathered:
        for place in places:
            shard = place * inner + (y ^ dy)
            x = group ^ dx
            at += [shard * 4 + tenant * 2 + x, shard * 2 + x]
    out, back, theirs = call(
        pair_base_kernel,
        out_shape=(
            in_hbm((rows, narrow), F32),
            in_hbm((rows, half), F32),
            in_hbm((rows, half + narrow), F32),
        ),
        in_specs=[smem] + [vmem] * (3 + len(gathered)),
        out_specs=(vmem, vmem, vmem),
        compiler_params=params(),
        cost_estimate=cost(4 * rows * width * narrow, width * narrow),
        name="base",
    )(jnp.stack(at).astype(jnp.int32), tokens, grad_out, pair, *[g[0] for g in gathered])
    theirs = swap(theirs, "tenant")
    return hbm(out), hbm(back), hbm(theirs)


def whole_base(tokens, grad_out, base_weight):
    rows, width = tokens.shape
    narrow = grad_out.shape[1]
    wp = width // CHUNKS
    group_size, tenant_size = lax.axis_size("groups"), lax.axis_size("tenant")
    shares = group_size * tenant_size
    share = base_weight.shape[0] // shares
    which = lax.axis_index("groups") * tenant_size + lax.axis_index("tenant")
    mine = lax.dynamic_slice_in_dim(base_weight, which * share, share, 0)
    weight = lax.all_gather(mine, ("fsdp", "groups", "tenant"), axis=0, tiled=True)
    return call(
        base_kernel,
        out_shape=(
            in_hbm((rows, narrow), F32),
            in_hbm((rows, width), F32),
        ),
        grid=(CHUNKS,),
        in_specs=[
            pl.BlockSpec((rows, wp), lambda i: (0, i)),
            whole((rows, narrow)),
            pl.BlockSpec((wp, narrow), lambda i: (i, 0)),
        ],
        out_specs=(whole((rows, narrow)), pl.BlockSpec((rows, wp), lambda i: (0, i))),
        compiler_params=params(("arbitrary",)),
        cost_estimate=cost(4 * rows * width * narrow, 2 * width * narrow),
        name="base",
    )(tokens, grad_out, weight)


def on_device(tokens, grad_out, base_weight, page_a, page_b, page_owner, row_tenant):
    rows, width = tokens.shape
    narrow = grad_out.shape[1]
    fsdp_size = lax.axis_size("fsdp")
    tenant_size = lax.axis_size("tenant")
    devices = fsdp_size * tenant_size
    cap = max(4, 4 * rows // (3 * devices))
    per_page = page_a.shape[1] // RANK
    ranks = page_a.shape[1]
    block = CHUNKS * cap
    total = devices * block
    wp, np_ = width // CHUNKS, narrow // CHUNKS
    split = wp // 128 * FIRST // 8 * 128
    rest = wp - split
    height = block + -(-cap // 16) * 16
    left_factor, right_factor = hbm(page_a[0], page_b[0])
    tokens, grad_out = hbm(tokens, grad_out)
    axes = ("fsdp", "tenant")
    which = lax.axis_index("tenant").astype(jnp.int32).reshape(1)

    def exchange(x):
        return lax.all_to_all(x, axes, split_axis=0, concat_axis=0, tiled=True)

    any_spec = pl.BlockSpec(memory_space=pl.ANY)
    smem = pl.BlockSpec(memory_space=pltpu.SMEM)
    paired = (
        fsdp_size == 8
        and tenant_size == 2
        and lax.axis_size("groups") == 2
        and width // fsdp_size == wp
    )

    steps = 4 if devices % 4 == 0 else 1
    send_grads, slot_row, slot_col = call(
        functools.partial(route_kernel, devices, cap, per_page),
        out_shape=(
            in_hbm((devices, height, np_), BF16),
            in_hbm((1, rows), F32),
            in_hbm((rows, rows), F32),
        ),
        in_specs=[smem] + [pl.BlockSpec(memory_space=pltpu.VMEM)] * 2,
        out_specs=tuple(pl.BlockSpec(memory_space=pltpu.VMEM) for _ in range(3)),
        compiler_params=params(),
        cost_estimate=cost(2 * total * rows * narrow, 4 * total * np_),
        name="route",
    )(page_owner, row_tenant.reshape(1, rows), grad_out)
    slot_row, slot_col = hbm(slot_row, slot_col)
    got_grads = exchange(send_grads)

    steps = 4 if devices % 4 == 0 else 1
    part = total // steps
    send_tokens = call(
        functools.partial(dispatch_kernel, cap),
        out_shape=in_hbm((total, wp), BF16),
        grid=(steps,),
        in_specs=[whole((1, rows)), any_spec],
        out_specs=pl.BlockSpec((part, wp), lambda i: (i, 0)),
        scratch_shapes=[
            pltpu.VMEM((CHUNKS * rows, wp), BF16),
            pltpu.SemaphoreType.DMA((CHUNKS,)),
        ],
        compiler_params=params(("arbitrary",)),
        cost_estimate=cost(2 * total * rows * width, 4 * total * wp),
        name="dispatch",
    )(slot_row, tokens)
    after = {}
    if paired:
        shares = gather_shares(base_weight, 2)
        after = shares["after"]
        pair = swap(for_pair(tokens, grad_out), "tenant")
        after["third"].append(pair)
    got_tokens = exchange(held(send_tokens, [got_grads] + after.get("first", [])))

    back_first, back_second, rank_rows, mask_rows = call(
        functools.partial(back_kernel, cap),
        out_shape=(
            in_hbm((total, split), BF16),
            in_hbm((total, rest + np_), BF16),
            in_hbm((total, ranks), BF16),
            in_hbm((total, ranks), BF16),
        ),
        grid=(steps,),
        in_specs=[
            pl.BlockSpec((devices // steps, height, np_), lambda i: (i, 0, 0)),
            whole((ranks, narrow)),
            any_spec,
        ],
        out_specs=(
            pl.BlockSpec((part, split), lambda i: (i, 0)),
            pl.BlockSpec((part, rest + np_), lambda i: (i, 0)),
            pl.BlockSpec((part, ranks), lambda i: (i, 0)),
            pl.BlockSpec((part, ranks), lambda i: (i, 0)),
        ),
        scratch_shapes=[
            pltpu.VMEM((CHUNKS * ranks, wp), BF16),
            pltpu.SemaphoreType.DMA((CHUNKS,)),
        ],
        compiler_params=params(("arbitrary",)),
        cost_estimate=cost(2 * total * ranks * width, 2 * (total * wp + ranks * width)),
        name="rank_grad_back",
    )(got_grads, right_factor, left_factor)
    rank_rows, mask_rows = hbm(rank_rows, mask_rows)
    got_back = exchange(held(back_first, [got_tokens] + after.get("third", [])))

    back_second, low_rows = call(
        functools.partial(forth_kernel, cap),
        out_shape=(
            in_hbm((total, rest + np_), BF16),
            in_hbm((total, ranks), BF16),
        ),
        grid=(steps,),
        in_specs=[
            pl.BlockSpec((part, wp), lambda i: (i, 0)),
            pl.BlockSpec((part, ranks), lambda i: (i, 0)),
            any_spec,
            whole((ranks, narrow)),
            any_spec,
        ],
        out_specs=(
            pl.BlockSpec((part, np_), lambda i: (i, rest // np_)),
            pl.BlockSpec((part, ranks), lambda i: (i, 0)),
        ),
        scratch_shapes=[
            pltpu.VMEM((CHUNKS * ranks, wp), BF16),
            pltpu.SemaphoreType.DMA((CHUNKS,)),
        ],
        input_output_aliases={4: 0},
        compiler_params=params(("arbitrary",)),
        cost_estimate=cost(2 * total * ranks * width, 2 * (total * wp + ranks * width)),
        name="lowrank_out",
    )(got_tokens, mask_rows, left_factor, right_factor, hbm(back_second))
    low_rows = hbm(low_rows)
    fourth = shares["last"]([low_rows]) if paired else []
    got_rest = exchange(held(back_second, [got_back] + fourth))

    if paired:
        base_out, base_mine, base_pair = paired_base(
            tokens, grad_out, held(pair, [low_rows]), shares, fsdp_size, 2
        )
    else:
        base_out, base_mine = whole_base(tokens, grad_out, base_weight)
        base_pair = base_mine
    outs, out_specs = [base_out], [whole((rows, narrow))]
    if paired:
        outs.append(base_pair)
        out_specs.append(pl.BlockSpec((rows, narrow), lambda i: (0, width // 2 // narrow)))

    grad_a, grad_b = call(
        functools.partial(page_grad_kernel, cap),
        in_specs=[pl.BlockSpec(memory_space=pltpu.VMEM)] * 4,
        out_shape=(
            in_hbm((ranks, width), BF16),
            in_hbm((ranks, narrow), BF16),
        ),
        compiler_params=params(),
        cost_estimate=cost(2 * total * ranks * width, 2 * (total * wp + ranks * width)),
        name="page_grads",
    )(got_tokens, got_grads, low_rows, rank_rows)

    combine_cost = cost(rows * total * width, total * wp + 4 * rows * width)

    def combine_scratch(cols):
        return [
            pltpu.VMEM((CHUNKS, rows, cols), BF16),
            pltpu.SemaphoreType.DMA((CHUNKS,)),
            pltpu.VMEM((CHUNKS, rows, cols), F32),
            pltpu.SemaphoreType.DMA((CHUNKS,)),
        ]

    grad_tokens = call(
        functools.partial(combine_kernel, cap, 0),
        out_shape=in_hbm((rows, width), BF16),
        grid=(1,),
        in_specs=[smem, whole((rows, rows)), whole((devices, block, split)), any_spec, any_spec],
        out_specs=any_spec,
        scratch_shapes=combine_scratch(split),
        compiler_params=params(),
        cost_estimate=combine_cost,
        name="combine_first",
    )(which, slot_col, got_back.reshape(devices, block, split), base_mine, base_pair)
    projected, grad_tokens = call(
        functools.partial(combine_kernel, cap, split),
        out_shape=(
            in_hbm((rows, narrow), BF16),
            in_hbm((rows, width), BF16),
        ),
        grid=(1,),
        in_specs=[smem, whole((rows, rows)), whole((devices, block, rest + np_)), any_spec, any_spec, *out_specs, any_spec],
        out_specs=(whole((rows, narrow)), any_spec),
        scratch_shapes=combine_scratch(rest),
        input_output_aliases={5 + len(out_specs): 1},
        compiler_params=params(),
        cost_estimate=combine_cost,
        name="combine_rest",
    )(
        which,
        slot_col,
        got_rest.reshape(devices, block, rest + np_),
        base_mine,
        base_pair,
        *outs,
        grad_tokens,
    )

    return projected, grad_tokens, grad_a[None], grad_b[None]


def solution(mesh):
    rows = P(("groups", "fsdp", "tenant"), None)
    pages = P(("groups", "fsdp", "tenant"), None, None)
    return jax.shard_map(
        on_device,
        mesh=mesh,
        in_specs=(
            rows,
            rows,
            P("fsdp", None),
            pages,
            pages,
            P("groups"),
            P(("groups", "fsdp", "tenant")),
        ),
        out_specs=(rows, rows, pages, pages),
        check_vma=False,
    )
```

time: 215 us -> 196 us (0.912)
  local copies, waits for them, and re-layouts: 31.8 us -> 7.33 us
  Pallas kernels: 56.8 us -> 66.7 us
    unnamed x86 -> x18, local copies, waits for them, and re-layouts: 31.7 us -> 5.87 us
    ppermute x3, waiting for transfers between devices: 32 us -> 16.2 us  [gather_shares(): down.append(lax.ppermute(down[-1], 'fsdp', moved))]
    all_to_all x4, waiting for transfers between devices: 8.49 us -> 20.1 us  [exchange(): return lax.all_to_all(x, axes, split_axis=0, concat_axis=0, tiled=True)]
    pallas_call x18 -> x17, Pallas kernels: 56.8 us -> 66.7 us  [call(): return lambda *args: run(*args, *deps)]
    ppermute x14, waiting for transfers between devices: 27.9 us -> 32.3 us  [swap(): return lax.ppermute(x, axis, [(i, i ^ 1) for i in range(size)])]
  transfers between devices with their start and end apart: 24 -> 24, of which waited for: 12 -> 10; matrix products, arithmetic and copies ran while one was open for 0% -> 0% of each run, Pallas kernels for 24% -> 31%
where the time goes in v3:
time: 196 us; the launch traced here: 195 us
  waiting for transfers between devices  68.6 us (35%)
  Pallas kernels  66.7 us (34%)
  starting transfers between devices  51.6 us (26%)
  local copies, waits for them, and re-layouts  7.33 us (4%)
    pallas_call x17, Pallas kernels, call(): return lambda *args: run(*args, *deps)  66.7 us
    ppermute x14, waiting for transfers between devices, swap(): return lax.ppermute(x, axis, [(i, i ^ 1) for i in range(size)])  32.3 us
    all_to_all x4, starting transfers between devices, exchange(): return lax.all_to_all(x, axes, split_axis=0, concat_axis=0, tiled=True)  25.7 us
    all_to_all x4, waiting for transfers between devices, exchange(): return lax.all_to_all(x, axes, split_axis=0, concat_axis=0, tiled=True)  20.1 us
    ppermute x3, waiting for transfers between devices, gather_shares(): down.append(lax.ppermute(down[-1], 'fsdp', moved))  16.2 us
    ppermute x14, starting transfers between devices, swap(): return lax.ppermute(x, axis, [(i, i ^ 1) for i in range(size)])  10.7 us
    ppermute x3, starting transfers between devices, gather_shares(): up.append(lax.ppermute(up[-1], 'fsdp', moved))  8.08 us
    ppermute x3, starting transfers between devices, gather_shares(): down.append(lax.ppermute(down[-1], 'fsdp', moved))  7.07 us
  transfers between devices with their start and end apart: 24, of which 10 were waited for; matrix products, arithmetic and copies ran while one was open for 0% of the time, Pallas kernels for 31%

profile of v3, /device:TPU:13, one launch (start us, length us, event | category | flops | bytes accessed | tf_op | source)
XLA Modules:
  0.0 195.3 jit_solution(14841808997978209020)
XLA Ops:
  0.6 0.0 copy-start
  0.7 1.6 copy-done
  2.2 0.8 constant_dynamic-slice_fusion.refs_4_
  3.1 2.1 %collective-permute-start.2 = (bf16[256,1024]{1,0:T(8,128)(2,1)}, bf16[256,1024]{1,0:T(8,128)(2,1)}, u32[]{:S(2)}, u32[]{:S(2)}) collective-permute-start(bf16[256,1024]{1,0:T(8,128)(2,1)} %constant_dynamic-slice_fusion.refs_4_), channel_id=1, source_target_pairs={{4,0},{6,2},{8,4},{10,6},{12,8},{14,10},{5,1},{7,3},{9,5},{11,7},{... | collective-permute-start | bytes 1572872 | tf_op jit(solution)/shard_map/ppermute | solution.py:480
  5.1 3.2 %collective-permute-start = (bf16[256,1024]{1,0:T(8,128)(2,1)}, bf16[256,1024]{1,0:T(8,128)(2,1)}, u32[]{:S(2)}, u32[]{:S(2)}) collective-permute-start(bf16[256,1024]{1,0:T(8,128)(2,1)} %constant_dynamic-slice_fusion.refs_4_), channel_id=1, source_target_pairs={{0,4},{2,6},{4,8},{6,10},{8,12},{10,14},{1,5},{3,7},{5,9},{7,11},{... | collective-permute-start | bytes 1572872 | tf_op jit(solution)/shard_map/ppermute | solution.py:478
  8.3 2.8 %route.1 = (bf16[16,96,128]{2,1,0:T(8,128)(2,1)}, f32[1,128]{1,0:T(1,128)}, f32[128,128]{1,0:T(8,128)}) custom-call(s32[16]{0:T(128)} %refs_0_.1, s32[1,128]{1,0:T(1,128)} %bitcast.55, bf16[128,1024]{1,0:T(8,128)(2,1)} %refs_2_.5), custom_call_target="tpu_custom_call" | custom-call | flops 1 | bytes 1 | tf_op jit(solution)/shard_map/route/pallas_call | solution.py:398
  11.2 6.9 %all-to-all-start = ((bf16[16,96,128]{2,1,0:T(8,128)(2,1)}), bf16[16,96,128]{2,1,0:T(8,128)(2,1)S(1)}, u32[]{:S(2)}, u32[]{:S(2)}) async-start(bf16[16,96,128]{2,1,0:T(8,128)(2,1)} %get-tuple-element.22), calls=%async_computation | async-start | bytes 786432 | tf_op jit(solution)/shard_map/all_to_all | solution.py:625
  18.1 1.2 collective-permute-start.5
  19.3 0.3 collective-permute-start.4
  19.6 0.0 collective-permute-done.2.refs_1_.refs_2_
  19.6 2.0 %collective-permute-start.3 = (bf16[256,1024]{1,0:T(8,128)(2,1)}, bf16[256,1024]{1,0:T(8,128)(2,1)S(1)}, u32[]{:S(2)}, u32[]{:S(2)}) collective-permute-start(bf16[256,1024]{1,0:T(8,128)(2,1)} %collective-permute-done.2.refs_1_.refs_2_), channel_id=1, source_target_pairs={{4,0},{6,2},{8,4},{10,6},{5,1},{7,3},{9,5},{11,7},{20,16},{22,18},... | collective-permute-start | bytes 1572872 | tf_op jit(solution)/shard_map/ppermute | solution.py:480
  21.6 3.4 %collective-permute-start.1 = (bf16[256,1024]{1,0:T(8,128)(2,1)}, bf16[256,1024]{1,0:T(8,128)(2,1)S(1)}, u32[]{:S(2)}, u32[]{:S(2)}) collective-permute-start(bf16[256,1024]{1,0:T(8,128)(2,1)} %collective-permute-done.refs_2_), channel_id=1, source_target_pairs={{4,8},{6,10},{8,12},{10,14},{5,9},{7,11},{9,13},{11,15},{20,24},{2... | collective-permute-start | bytes 1572872 | tf_op jit(solution)/shard_map/ppermute | solution.py:478
  25.0 6.6 %dispatch.1.refs_0_ = bf16[1280,1024]{1,0:T(8,128)(2,1)} custom-call(f32[1,128]{1,0:T(1,128)} %get-tuple-element.21.refs_0_, bf16[128,8192]{1,0:T(8,128)(2,1)} %refs_1_.5), custom_call_target="tpu_custom_call" | custom-call | flops 1 | bytes 1 | tf_op jit(solution)/shard_map/dispatch/pallas_call | solution.py:398
  31.6 0.8 copy-done.8
  32.4 3.5 %collective-permute-done.4.refs_4_.refs_5_ = bf16[256,1024]{1,0:T(8,128)(2,1)} collective-permute-done((bf16[256,1024]{1,0:T(8,128)(2,1)}, bf16[256,1024]{1,0:T(8,128)(2,1)}, u32[]{:S(2)}, u32[]{:S(2)}) %collective-permute-start.4) | collective-permute-done | bytes 524320 | tf_op jit(solution)/shard_map/ppermute | solution.py:464
  35.9 4.1 %collective-permute-done.3.refs_3_.refs_1_.refs_2_ = bf16[256,1024]{1,0:T(8,128)(2,1)S(1)} collective-permute-done((bf16[256,1024]{1,0:T(8,128)(2,1)}, bf16[256,1024]{1,0:T(8,128)(2,1)S(1)}, u32[]{:S(2)}, u32[]{:S(2)}) %collective-permute-start.3) | collective-permute-done | bytes 524320 | tf_op jit(solution)/shard_map/ppermute | solution.py:480
  39.9 0.0 collective-permute-done.1.refs_2_.refs_3_
  39.9 0.8 copy-done.5
  40.7 0.8 copy-done.7
  41.5 5.4 %all-to-all-start.1 = ((bf16[16,80,1024]{2,1,0:T(8,128)(2,1)}), bf16[16,80,1024]{2,1,0:T(8,128)(2,1)}, u32[]{:S(2)}, u32[]{:S(2)}) async-start(bf16[16,80,1024]{2,1,0:T(8,128)(2,1)} %bitcast.47), calls=%async_computation.1 | async-start | bytes 5242880 | tf_op jit(solution)/shard_map/all_to_all | solution.py:625
  46.9 2.5 %for_pair.1 = bf16[128,5120]{1,0:T(8,128)(2,1)} custom-call(s32[1]{0:T(128)} %bitcast.8.refs_0_, bf16[128,8192]{1,0:T(8,128)(2,1)} %refs_1_.5, bf16[128,1024]{1,0:T(8,128)(2,1)} %refs_2_.5), custom_call_target="tpu_custom_call" | custom-call | flops 1 | bytes 1 | tf_op jit(solution)/shard_map/for_pair/pallas_call | solution.py:398
  49.4 0.4 collective-permute-start.14
  49.9 1.2 collective-permute-start.10
  51.1 2.0 %pick.3.refs_8_ = bf16[256,1024]{1,0:T(8,128)(2,1)} custom-call(s32[1]{0:T(128)} %bitcast.6.refs_0_, bf16[256,1024]{1,0:T(8,128)(2,1)} %collective-permute-done.2.refs_1_.refs_2_, bf16[256,1024]{1,0:T(8,128)(2,1)} %collective-permute-done.refs_2_), custom_call_target="tpu_custom_call" | custom-call | flops 1 | bytes 1 | tf_op jit(solution)/shard_map/pick/pallas_call | solution.py:398
  53.1 0.3 collective-permute-start.8
  53.4 0.3 collective-permute-start.9
  53.7 2.3 %pick.4.refs_12_ = bf16[256,1024]{1,0:T(8,128)(2,1)} custom-call(s32[1]{0:T(128)} %bitcast.7.refs_0_, bf16[256,1024]{1,0:T(8,128)(2,1)} %copy-done.5, bf16[256,1024]{1,0:T(8,128)(2,1)} %collective-permute-done.2.refs_1_.refs_2_, bf16[256,1024]{1,0:T(8,128)(2,1)} %copy-done.7), custom_call_target="tpu_custom_call" | custom-call | flops 1 | bytes 1 | tf_op jit(solution)/shard_map/pick/pallas_call | solution.py:398
  55.9 1.2 collective-permute-start.12
  57.1 6.4 %collective-permute-done.10.refs_6_.refs_7_ = bf16[256,1024]{1,0:T(8,128)(2,1)} collective-permute-done((bf16[256,1024]{1,0:T(8,128)(2,1)}, bf16[256,1024]{1,0:T(8,128)(2,1)}, u32[]{:S(2)}, u32[]{:S(2)}) %collective-permute-start.10) | collective-permute-done | bytes 524320 | tf_op jit(solution)/shard_map/ppermute | solution.py:464
  63.6 3.0 %collective-permute-start.7 = (bf16[256,1024]{1,0:T(8,128)(2,1)S(1)}, bf16[256,1024]{1,0:T(8,128)(2,1)}, u32[]{:S(2)}, u32[]{:S(2)}) collective-permute-start(bf16[256,1024]{1,0:T(8,128)(2,1)S(1)} %copy-done.6), channel_id=1, source_target_pairs={{4,0},{6,2},{5,1},{7,3},{20,16},{22,18},{21,17},{23,19}} | collective-permute-start | bytes 1572872 | tf_op jit(solution)/shard_map/ppermute | solution.py:480
  66.6 10.5 %collective-permute-done.8.refs_4_.refs_9_ = bf16[256,1024]{1,0:T(8,128)(2,1)} collective-permute-done((bf16[256,1024]{1,0:T(8,128)(2,1)}, bf16[256,1024]{1,0:T(8,128)(2,1)}, u32[]{:S(2)}, u32[]{:S(2)}) %collective-permute-start.8) | collective-permute-done | bytes 524320 | tf_op jit(solution)/shard_map/ppermute | solution.py:464
  77.0 1.2 collective-permute-start.13
  78.3 0.0 copy-start.2
  78.3 1.5 collective-permute-start.6
  79.8 8.8 %rank_grad_back.1 = (bf16[1280,512]{1,0:T(8,128)(2,1)}, bf16[1280,640]{1,0:T(8,128)(2,1)}, bf16[1280,128]{1,0:T(8,128)(2,1)}, bf16[1280,128]{1,0:T(8,128)(2,1)}) custom-call(bf16[16,96,128]{2,1,0:T(8,128)(2,1)} %copy-done.3, bf16[128,1024]{1,0:T(8,128)(2,1)} %bitcast.53, bf16[128,8192]{1,0:T(8,128)(2,1)} %bitcast.50), custom_call_target="tpu_custom_call" | custom-call | flops 1 | bytes 1 | tf_op jit(solution)/shard_map/rank_grad_back/pallas_call | solution.py:398
  88.6 12.1 %collective-permute-done.7.refs_3_.refs_1_ = bf16[256,1024]{1,0:T(8,128)(2,1)} collective-permute-done((bf16[256,1024]{1,0:T(8,128)(2,1)S(1)}, bf16[256,1024]{1,0:T(8,128)(2,1)}, u32[]{:S(2)}, u32[]{:S(2)}) %collective-permute-start.7) | collective-permute-done | bytes 524320 | tf_op jit(solution)/shard_map/ppermute | solution.py:480
  100.7 0.0 collective-permute-done.13.refs_9_.refs_11_
  100.7 0.0 collective-permute-done.12.refs_8_.refs_14_
  100.7 0.0 collective-permute-done.11.refs_7_.refs_13_
  100.7 0.0 collective-permute-done.6.refs_2_.refs_4_
  100.7 5.1 %all-to-all-done.1 = bf16[16,80,1024]{2,1,0:T(8,128)(2,1)} async-done(((bf16[16,80,1024]{2,1,0:T(8,128)(2,1)}), bf16[16,80,1024]{2,1,0:T(8,128)(2,1)}, u32[]{:S(2)}, u32[]{:S(2)}) %all-to-all-start.1) | async-done | bytes 2621472 | tf_op jit(solution)/shard_map/all_to_all | solution.py:625
  105.8 8.9 %all-to-all-start.2 = ((bf16[16,80,512]{2,1,0:T(8,128)(2,1)}), bf16[16,80,512]{2,1,0:T(8,128)(2,1)S(1)}, u32[]{:S(2)}, u32[]{:S(2)}) async-start(bf16[16,80,512]{2,1,0:T(8,128)(2,1)} %bitcast.52), calls=%async_computation.2 | async-start | bytes 2621440 | tf_op jit(solution)/shard_map/all_to_all | solution.py:625
  114.7 2.4 %pick.5.refs_16_ = bf16[256,1024]{1,0:T(8,128)(2,1)} custom-call(s32[1]{0:T(128)} %bitcast.11.refs_0_, bf16[256,1024]{1,0:T(8,128)(2,1)} %collective-permute-done.7.refs_3_.refs_1_, bf16[256,1024]{1,0:T(8,128)(2,1)} %copy-done.5, bf16[256,1024]{1,0:T(8,128)(2,1)} %copy-done.7, bf16[256,1024]{1,0:T(8,128)(2,1)} %collective-permute-done.6.refs_2_.refs_4_), custom_call_target="tpu_custom_call" | custom-call | flops 1 | bytes 1 | tf_op jit(solution)/shard_map/pick/pallas_call | solution.py:398
  117.1 0.3 collective-permute-start.15
  117.4 1.2 collective-permute-start.16
  118.6 0.3 collective-permute-start.17
  118.9 10.2 %lowrank_out.1 = (bf16[1280,640]{1,0:T(8,128)(2,1)}, bf16[1280,128]{1,0:T(8,128)(2,1)}) custom-call(bf16[1280,1024]{1,0:T(8,128)(2,1)} %bitcast.3.refs_0_.refs_1_, bf16[1280,128]{1,0:T(8,128)(2,1)} %get-tuple-element.23.refs_1_, bf16[128,8192]{1,0:T(8,128)(2,1)} %bitcast.51, bf16[128,1024]{1,0:T(8,128)(2,1)} %bitcast.54, ...), custom_call_target="tpu_custom_call", output_to_operand_aliasing={{0}: (4, {})} | custom-call | flops 1 | bytes 1 | tf_op jit(solution)/shard_map/lowrank_out/pallas_call | solution.py:398
  129.1 10.5 %collective-permute-done.15.refs_0_ = bf16[256,1024]{1,0:T(8,128)(2,1)S(1)} collective-permute-done((bf16[256,1024]{1,0:T(8,128)(2,1)}, bf16[256,1024]{1,0:T(8,128)(2,1)S(1)}, u32[]{:S(2)}, u32[]{:S(2)}) %collective-permute-start.15) | collective-permute-done | bytes 524320 | tf_op jit(solution)/shard_map/ppermute | solution.py:464
  139.6 0.8 copy-done.4
  140.4 1.2 collective-permute-start.18
  141.6 0.0 collective-permute-done.16.refs_3_.refs_18_
  141.6 4.1 %all-to-all-done.2.refs_2_ = bf16[16,80,512]{2,1,0:T(8,128)(2,1)S(1)} async-done(((bf16[16,80,512]{2,1,0:T(8,128)(2,1)}), bf16[16,80,512]{2,1,0:T(8,128)(2,1)S(1)}, u32[]{:S(2)}, u32[]{:S(2)}) %all-to-all-start.2) | async-done | bytes 1310752 | tf_op jit(solution)/shard_map/all_to_all | solution.py:625
  145.7 1.1 copy-done.1
  146.8 4.5 %all-to-all-start.3 = ((bf16[16,80,640]{2,1,0:T(8,128)(2,1)}), bf16[16,80,640]{2,1,0:T(8,128)(2,1)}, u32[]{:S(2)}, u32[]{:S(2)}) async-start(bf16[16,80,640]{2,1,0:T(8,128)(2,1)} %bitcast.48), calls=%async_computation.3 | async-start | bytes 3276800 | tf_op jit(solution)/shard_map/all_to_all | solution.py:625
  151.4 0.6 stack.131.refs_0_
  152.0 0.0 collective-permute-done.17.refs_15_
  152.0 1.4 collective-permute-done.18.refs_19_
  153.4 11.3 %base.1 = (f32[128,1024]{1,0:T(8,128)}, f32[128,4096]{1,0:T(8,128)}, f32[128,5120]{1,0:T(8,128)}) custom-call(s32[32]{0:T(128)} %stack.131.refs_0_, bf16[128,8192]{1,0:T(8,128)(2,1)} %refs_1_.5, bf16[128,1024]{1,0:T(8,128)(2,1)} %refs_2_.5, bf16[128,5120]{1,0:T(8,128)(2,1)} %held.9.refs_3_, bf16[256,1024]{1,0:T(8,128)(2,1)} %constant_dynamic-slice_fusion.refs_4_, ...), custom_call_target="tpu_custom_call" | custom-call | flops 1 | bytes 1 | tf_op jit(solution)/shard_map/base/pallas_call | solution.py:398
  164.8 1.7 collective-permute-start.19
  166.4 6.9 %page_grads.1 = (bf16[128,8192]{1,0:T(8,128)(2,1)}, bf16[128,1024]{1,0:T(8,128)(2,1)}) custom-call(bf16[1280,1024]{1,0:T(8,128)(2,1)} %bitcast.3.refs_0_.refs_1_, bf16[16,96,128]{2,1,0:T(8,128)(2,1)} %copy-done.3, bf16[1280,128]{1,0:T(8,128)(2,1)} %get-tuple-element.27.refs_1_.refs_2_, bf16[1280,128]{1,0:T(8,128)(2,1)} %get-tuple-element.33.refs_3_), custom_call_target="tpu_custom_call" | custom-call | flops 1 | bytes 1 | tf_op jit(solution)/shard_map/page_grads/pallas_call | solution.py:398
  173.4 0.0 collective-permute-done.19.refs_4_.refs_6_
  173.4 4.7 %combine_first.1.refs_7_ = bf16[128,8192]{1,0:T(8,128)(2,1)} custom-call(s32[1]{0:T(128)} %bitcast.refs_0_, f32[128,128]{1,0:T(8,128)} %get-tuple-element.20.refs_1_, bf16[16,80,512]{2,1,0:T(8,128)(2,1)} %copy-done.1, f32[128,4096]{1,0:T(8,128)} %get-tuple-element.28.refs_3_, f32[128,5120]{1,0:T(8,128)} %collective-permute-done.19.refs_4_.refs_6_), custom_call_target="tpu_custom_call" | custom-call | flops 1 | bytes 1 | tf_op jit(solution)/shard_map/combine_first/pallas_call | solution.py:398
  178.1 10.9 %all-to-all-done.3.refs_2_ = bf16[16,80,640]{2,1,0:T(8,128)(2,1)} async-done(((bf16[16,80,640]{2,1,0:T(8,128)(2,1)}), bf16[16,80,640]{2,1,0:T(8,128)(2,1)}, u32[]{:S(2)}, u32[]{:S(2)}) %all-to-all-start.3) | async-done | bytes 1638432 | tf_op jit(solution)/shard_map/all_to_all | solution.py:625
  189.0 6.1 %combine_rest.1 = (bf16[128,1024]{1,0:T(8,128)(2,1)}, bf16[128,8192]{1,0:T(8,128)(2,1)}) custom-call(s32[1]{0:T(128)} %bitcast.refs_0_, f32[128,128]{1,0:T(8,128)} %get-tuple-element.20.refs_1_, bf16[16,80,640]{2,1,0:T(8,128)(2,1)} %all-to-all-done.3.refs_2_, f32[128,4096]{1,0:T(8,128)} %get-tuple-element.28.refs_3_, ...), custom_call_target="tpu_custom_call", output_to_operand_aliasing={{1}: (7, {})} | custom-call | flops 1 | bytes 1 | tf_op jit(solution)/shard_map/combine_rest/pallas_call | solution.py:398
  (21 shorter events, 0.0 us)
Async XLA Ops:
  0.6 1.6 copy-start
  3.1 16.5 %collective-permute-start.2 = (bf16[256,1024]{1,0:T(8,128)(2,1)}, bf16[256,1024]{1,0:T(8,128)(2,1)}, u32[]{:S(2)}, u32[]{:S(2)}) collective-permute-start(bf16[256,1024]{1,0:T(8,128)(2,1)} %constant_dynamic-slice_fusion.refs_4_), channel_id=1, source_target_pairs={{4,0},{6,2},{8,4},{10,6},{12,8},{14,10},{5,1},{7,3},{9,5},{11,7},{... | collective-permute-start | bytes 1572872 | tf_op jit(solution)/shard_map/ppermute | solution.py:480
  5.1 16.5 %collective-permute-start = (bf16[256,1024]{1,0:T(8,128)(2,1)}, bf16[256,1024]{1,0:T(8,128)(2,1)}, u32[]{:S(2)}, u32[]{:S(2)}) collective-permute-start(bf16[256,1024]{1,0:T(8,128)(2,1)} %constant_dynamic-slice_fusion.refs_4_), channel_id=1, source_target_pairs={{0,4},{2,6},{4,8},{6,10},{8,12},{10,14},{1,5},{3,7},{5,9},{7,11},{... | collective-permute-start | bytes 1572872 | tf_op jit(solution)/shard_map/ppermute | solution.py:478
  11.2 24.7 %all-to-all-start = ((bf16[16,96,128]{2,1,0:T(8,128)(2,1)}), bf16[16,96,128]{2,1,0:T(8,128)(2,1)S(1)}, u32[]{:S(2)}, u32[]{:S(2)}) async-start(bf16[16,96,128]{2,1,0:T(8,128)(2,1)} %get-tuple-element.22), calls=%async_computation | async-start | bytes 786432 | tf_op jit(solution)/shard_map/all_to_all | solution.py:625
  18.1 13.5 %collective-permute-start.5 = (bf16[256,1024]{1,0:T(8,128)(2,1)}, bf16[256,1024]{1,0:T(8,128)(2,1)S(1)}, u32[]{:S(2)}, u32[]{:S(2)}) collective-permute-start(bf16[256,1024]{1,0:T(8,128)(2,1)} %constant_dynamic-slice_fusion.refs_4_), channel_id=1, source_target_pairs={{0,16},{16,0},{1,17},{17,1},{2,18},{18,2},{3,19},{19,3},{4,20},{20... | collective-permute-start | bytes 1572872 | tf_op jit(solution)/shard_map/ppermute | solution.py:464
  19.3 16.5 %collective-permute-start.4 = (bf16[256,1024]{1,0:T(8,128)(2,1)}, bf16[256,1024]{1,0:T(8,128)(2,1)}, u32[]{:S(2)}, u32[]{:S(2)}) collective-permute-start(bf16[256,1024]{1,0:T(8,128)(2,1)} %constant_dynamic-slice_fusion.refs_4_), channel_id=1, source_target_pairs={{0,2},{2,0},{4,6},{6,4},{8,10},{10,8},{12,14},{14,12},{1,3},{3,1},... | collective-permute-start | bytes 1572872 | tf_op jit(solution)/shard_map/ppermute | solution.py:464
  19.6 20.3 %collective-permute-start.3 = (bf16[256,1024]{1,0:T(8,128)(2,1)}, bf16[256,1024]{1,0:T(8,128)(2,1)S(1)}, u32[]{:S(2)}, u32[]{:S(2)}) collective-permute-start(bf16[256,1024]{1,0:T(8,128)(2,1)} %collective-permute-done.2.refs_1_.refs_2_), channel_id=1, source_target_pairs={{4,0},{6,2},{8,4},{10,6},{5,1},{7,3},{9,5},{11,7},{20,16},{22,18},... | collective-permute-start | bytes 1572872 | tf_op jit(solution)/shard_map/ppermute | solution.py:480
  21.6 18.3 %collective-permute-start.1 = (bf16[256,1024]{1,0:T(8,128)(2,1)}, bf16[256,1024]{1,0:T(8,128)(2,1)S(1)}, u32[]{:S(2)}, u32[]{:S(2)}) collective-permute-start(bf16[256,1024]{1,0:T(8,128)(2,1)} %collective-permute-done.refs_2_), channel_id=1, source_target_pairs={{4,8},{6,10},{8,12},{10,14},{5,9},{7,11},{9,13},{11,15},{20,24},{2... | collective-permute-start | bytes 1572872 | tf_op jit(solution)/shard_map/ppermute | solution.py:478
  31.6 0.8 copy-start.8
  35.9 4.1 %copy-start.3 = (bf16[16,96,128]{2,1,0:T(8,128)(2,1)}, bf16[16,96,128]{2,1,0:T(8,128)(2,1)S(1)}, u32[]{:S(2)}) copy-start(bf16[16,96,128]{2,1,0:T(8,128)(2,1)S(1)} %all-to-all-done.refs_1_.refs_0_) | copy-start | bytes 1179652
  39.9 0.8 copy-start.5
  40.7 0.8 copy-start.7
  41.5 64.3 %all-to-all-start.1 = ((bf16[16,80,1024]{2,1,0:T(8,128)(2,1)}), bf16[16,80,1024]{2,1,0:T(8,128)(2,1)}, u32[]{:S(2)}, u32[]{:S(2)}) async-start(bf16[16,80,1024]{2,1,0:T(8,128)(2,1)} %bitcast.47), calls=%async_computation.1 | async-start | bytes 5242880 | tf_op jit(solution)/shard_map/all_to_all | solution.py:625
  49.4 28.8 %collective-permute-start.14 = (bf16[128,5120]{1,0:T(8,128)(2,1)}, bf16[128,5120]{1,0:T(8,128)(2,1)S(1)}, u32[]{:S(2)}, u32[]{:S(2)}) collective-permute-start(bf16[128,5120]{1,0:T(8,128)(2,1)} %for_pair.1), channel_id=1, source_target_pairs={{0,1},{1,0},{2,3},{3,2},{4,5},{5,4},{6,7},{7,6},{8,9},{9,8},{10,11... | collective-permute-start | bytes 3932168 | tf_op jit(solution)/shard_map/ppermute | solution.py:464
  49.9 13.7 %collective-permute-start.10 = (bf16[256,1024]{1,0:T(8,128)(2,1)}, bf16[256,1024]{1,0:T(8,128)(2,1)}, u32[]{:S(2)}, u32[]{:S(2)}) collective-permute-start(bf16[256,1024]{1,0:T(8,128)(2,1)} %collective-permute-done.4.refs_4_.refs_5_), channel_id=1, source_target_pairs={{0,16},{16,0},{1,17},{17,1},{2,18},{18,2},{3,19},{19,3},{4,20},{20... | collective-permute-start | bytes 1572872 | tf_op jit(solution)/shard_map/ppermute | solution.py:464
  53.1 23.9 %collective-permute-start.8 = (bf16[256,1024]{1,0:T(8,128)(2,1)}, bf16[256,1024]{1,0:T(8,128)(2,1)}, u32[]{:S(2)}, u32[]{:S(2)}) collective-permute-start(bf16[256,1024]{1,0:T(8,128)(2,1)} %pick.3.refs_8_), channel_id=1, source_target_pairs={{0,2},{2,0},{4,6},{6,4},{8,10},{10,8},{12,14},{14,12},{1,3},{3,1},... | collective-permute-start | bytes 1572872 | tf_op jit(solution)/shard_map/ppermute | solution.py:464
  53.4 24.9 %collective-permute-start.9 = (bf16[256,1024]{1,0:T(8,128)(2,1)}, bf16[256,1024]{1,0:T(8,128)(2,1)}, u32[]{:S(2)}, u32[]{:S(2)}) collective-permute-start(bf16[256,1024]{1,0:T(8,128)(2,1)} %pick.3.refs_8_), channel_id=1, source_target_pairs={{0,16},{16,0},{1,17},{17,1},{2,18},{18,2},{3,19},{19,3},{4,20},{20... | collective-permute-start | bytes 1572872 | tf_op jit(solution)/shard_map/ppermute | solution.py:464
  53.7 9.9 %copy-start.6 = (bf16[256,1024]{1,0:T(8,128)(2,1)S(1)}, bf16[256,1024]{1,0:T(8,128)(2,1)}, u32[]{:S(2)}) copy-start(bf16[256,1024]{1,0:T(8,128)(2,1)} %copy-done.5) | copy-start | bytes 1572868
  55.9 44.8 %collective-permute-start.12 = (bf16[256,1024]{1,0:T(8,128)(2,1)}, bf16[256,1024]{1,0:T(8,128)(2,1)}, u32[]{:S(2)}, u32[]{:S(2)}) collective-permute-start(bf16[256,1024]{1,0:T(8,128)(2,1)} %pick.4.refs_12_), channel_id=1, source_target_pairs={{0,16},{16,0},{1,17},{17,1},{2,18},{18,2},{3,19},{19,3},{4,20},{20... | collective-permute-start | bytes 1572872 | tf_op jit(solution)/shard_map/ppermute | solution.py:464
  63.6 37.1 %collective-permute-start.7 = (bf16[256,1024]{1,0:T(8,128)(2,1)S(1)}, bf16[256,1024]{1,0:T(8,128)(2,1)}, u32[]{:S(2)}, u32[]{:S(2)}) collective-permute-start(bf16[256,1024]{1,0:T(8,128)(2,1)S(1)} %copy-done.6), channel_id=1, source_target_pairs={{4,0},{6,2},{5,1},{7,3},{20,16},{22,18},{21,17},{23,19}} | collective-permute-start | bytes 1572872 | tf_op jit(solution)/shard_map/ppermute | solution.py:480
  77.0 23.7 %collective-permute-start.13 = (bf16[256,1024]{1,0:T(8,128)(2,1)}, bf16[256,1024]{1,0:T(8,128)(2,1)}, u32[]{:S(2)}, u32[]{:S(2)}) collective-permute-start(bf16[256,1024]{1,0:T(8,128)(2,1)} %collective-permute-done.8.refs_4_.refs_9_), channel_id=1, source_target_pairs={{0,16},{16,0},{1,17},{17,1},{2,18},{18,2},{3,19},{19,3},{4,20},{20... | collective-permute-start | bytes 1572872 | tf_op jit(solution)/shard_map/ppermute | solution.py:464
  78.3 22.5 %collective-permute-start.11 = (bf16[256,1024]{1,0:T(8,128)(2,1)}, bf16[256,1024]{1,0:T(8,128)(2,1)}, u32[]{:S(2)}, u32[]{:S(2)}) collective-permute-start(bf16[256,1024]{1,0:T(8,128)(2,1)} %pick.4.refs_12_), channel_id=1, source_target_pairs={{0,2},{2,0},{4,6},{6,4},{8,10},{10,8},{12,14},{14,12},{1,3},{3,1},... | collective-permute-start | bytes 1572872 | tf_op jit(solution)/shard_map/ppermute | solution.py:464
  78.3 27.6 %copy-start.2 = (bf16[128,5120]{1,0:T(8,128)(2,1)}, bf16[128,5120]{1,0:T(8,128)(2,1)S(1)}, u32[]{:S(2)}) copy-start(bf16[128,5120]{1,0:T(8,128)(2,1)S(1)} %collective-permute-done.14.refs_10_.refs_0_) | copy-start | bytes 3932164
  78.3 22.4 %collective-permute-start.6 = (bf16[256,1024]{1,0:T(8,128)(2,1)}, bf16[256,1024]{1,0:T(8,128)(2,1)}, u32[]{:S(2)}, u32[]{:S(2)}) collective-permute-start(bf16[256,1024]{1,0:T(8,128)(2,1)} %copy-done.7), channel_id=1, source_target_pairs={{8,12},{10,14},{9,13},{11,15},{24,28},{26,30},{25,29},{27,31}} | collective-permute-start | bytes 1572872 | tf_op jit(solution)/shard_map/ppermute | solution.py:478
  105.8 39.9 %all-to-all-start.2 = ((bf16[16,80,512]{2,1,0:T(8,128)(2,1)}), bf16[16,80,512]{2,1,0:T(8,128)(2,1)S(1)}, u32[]{:S(2)}, u32[]{:S(2)}) async-start(bf16[16,80,512]{2,1,0:T(8,128)(2,1)} %bitcast.52), calls=%async_computation.2 | async-start | bytes 2621440 | tf_op jit(solution)/shard_map/all_to_all | solution.py:625
  117.1 22.5 %collective-permute-start.15 = (bf16[256,1024]{1,0:T(8,128)(2,1)}, bf16[256,1024]{1,0:T(8,128)(2,1)S(1)}, u32[]{:S(2)}, u32[]{:S(2)}) collective-permute-start(bf16[256,1024]{1,0:T(8,128)(2,1)} %pick.5.refs_16_), channel_id=1, source_target_pairs={{0,2},{2,0},{4,6},{6,4},{8,10},{10,8},{12,14},{14,12},{1,3},{3,1},... | collective-permute-start | bytes 1572872 | tf_op jit(solution)/shard_map/ppermute | solution.py:464
  117.4 24.2 %collective-permute-start.16 = (bf16[256,1024]{1,0:T(8,128)(2,1)}, bf16[256,1024]{1,0:T(8,128)(2,1)}, u32[]{:S(2)}, u32[]{:S(2)}) collective-permute-start(bf16[256,1024]{1,0:T(8,128)(2,1)} %pick.5.refs_16_), channel_id=1, source_target_pairs={{0,16},{16,0},{1,17},{17,1},{2,18},{18,2},{3,19},{19,3},{4,20},{20... | collective-permute-start | bytes 1572872 | tf_op jit(solution)/shard_map/ppermute | solution.py:464
  118.6 33.4 %collective-permute-start.17 = (bf16[256,1024]{1,0:T(8,128)(2,1)}, bf16[256,1024]{1,0:T(8,128)(2,1)}, u32[]{:S(2)}, u32[]{:S(2)}) collective-permute-start(bf16[256,1024]{1,0:T(8,128)(2,1)} %collective-permute-done.11.refs_7_.refs_13_), channel_id=1, source_target_pairs={{0,16},{16,0},{1,17},{17,1},{2,18},{18,2},{3,19},{19,3},{4,20},{20... | collective-permute-start | bytes 1572872 | tf_op jit(solution)/shard_map/ppermute | solution.py:464
  139.6 0.8 copy-start.4
  140.4 13.0 %collective-permute-start.18 = (bf16[256,1024]{1,0:T(8,128)(2,1)}, bf16[256,1024]{1,0:T(8,128)(2,1)}, u32[]{:S(2)}, u32[]{:S(2)}) collective-permute-start(bf16[256,1024]{1,0:T(8,128)(2,1)} %held.7.refs_2_.refs_17_), channel_id=1, source_target_pairs={{0,16},{16,0},{1,17},{17,1},{2,18},{18,2},{3,19},{19,3},{4,20},{20... | collective-permute-start | bytes 1572872 | tf_op jit(solution)/shard_map/ppermute | solution.py:464
  145.7 1.1 copy-start.1
  146.8 42.2 %all-to-all-start.3 = ((bf16[16,80,640]{2,1,0:T(8,128)(2,1)}), bf16[16,80,640]{2,1,0:T(8,128)(2,1)}, u32[]{:S(2)}, u32[]{:S(2)}) async-start(bf16[16,80,640]{2,1,0:T(8,128)(2,1)} %bitcast.48), calls=%async_computation.3 | async-start | bytes 3276800 | tf_op jit(solution)/shard_map/all_to_all | solution.py:625
  164.8 8.6 %collective-permute-start.19 = (f32[128,5120]{1,0:T(8,128)}, f32[128,5120]{1,0:T(8,128)}, u32[]{:S(2)}, u32[]{:S(2)}) collective-permute-start(f32[128,5120]{1,0:T(8,128)} %get-tuple-element.29), channel_id=1, source_target_pairs={{0,1},{1,0},{2,3},{3,2},{4,5},{5,4},{6,7},{7,6},{8,9},{9,8},{10,11... | collective-permute-start | bytes 7864328 | tf_op jit(solution)/shard_map/ppermute | solution.py:464

commit v4 on v3

--- a/solution.py
+++ b/solution.py
@@ -322,14 +322,26 @@
     back_ref[...] = lax.dot_general(grad_ref[...], weight, NT, preferred_element_type=F32)
 
 
-def combine_kernel(cap, start, which_ref, col_ref, got_ref, mine_ref, pair_ref, *refs):
-    out_hbm, out, sem, base, base_sem = refs[-5:]
+def combine_kernel(cap, start, extra, which_ref, col_hbm, got_hbm, mine_ref, pair_ref, *refs):
+    extras, refs = refs[:extra], refs[extra:]
+    if extra:
+        projected_ref, refs = refs[1], refs[2:]
+    out_hbm, out, sem, base, base_sem, got_ref, col_ref, in_sem, *sums = refs
     devices, block, width = got_ref.shape
     cols = out.shape[2]
-    rows = col_ref.shape[0]
     piece = out_hbm.shape[1] // CHUNKS
     parts = 2 if mine_ref.shape[1] < out_hbm.shape[1] else 1
     size = piece // parts
+    group = devices // 4 if devices % 4 == 0 else devices
+
+    loads = [pltpu.make_async_copy(col_hbm, col_ref, in_sem.at[0])]
+    for n in range(devices // group):
+        at = pl.ds(n * group, group)
+        loads.append(pltpu.make_async_copy(got_hbm.at[at], got_ref.at[at], in_sem.at[1 + n]))
+    late = []
+    for n, ref in enumerate(sums):
+        last = pl.ds(extras[n].shape[1] - ref.shape[1], ref.shape[1])
+        late.append(pltpu.make_async_copy(extras[n].at[:, last], ref, in_sem.at[5 + n]))
 
     def load(ref, part):
         low, high = max(start, part * size), min(start + cols, (part + 1) * size)
@@ -345,6 +357,7 @@
                 ]
             )
 
+    start_all(loads)
     if parts == 1:
         load(mine_ref, 0)
     else:
@@ -355,33 +368,41 @@
                 load(mine_ref, n)
                 load(pair_ref, 1 - n)
 
-    col = col_ref[:, 0:1]
+    start_all(late)
+    wait_all(loads)
+    col, rows = col_ref[:, 0:1], col_ref.shape[0]
     copies = []
-    for k in range(CHUNKS):
+    for k in range(0, CHUNKS, 2):
         low = k * cap // 16 * 16
-        high = min(-(-(k + 1) * cap // 16) * 16, block)
+        high = min(-(-(k + 2) * cap // 16) * 16, block)
         count = high - low
         lane = iota((1, devices * count), 1)
         row = jnp.zeros_like(lane)
         for d in range(1, devices):
             row = row + (lane >= d * count).astype(jnp.int32)
-        slot = lane - row * count + (low - k * cap)
-        key = jnp.where((slot >= 0) & (slot < cap), row * cap + slot, -1).astype(F32)
-        here = (col == key).astype(F32).astype(BF16)
+        slot = lane - row * count + low
+        here = []
+        for n in (k, k + 1):
+            mine = (slot >= n * cap) & (slot < (n + 1) * cap)
+            key = jnp.where(mine, row * cap + slot - n * cap, -1).astype(F32)
+            here.append((col == key).astype(F32).astype(BF16))
         packed = jnp.concatenate([got_ref[d, low:high, :] for d in range(devices)], axis=0)
-        back = jnp.dot(here, packed, preferred_element_type=F32)
-        pltpu.make_async_copy(base.at[k], base.at[k], base_sem.at[k]).wait()
-        out[k] = (base[k] + back[:, 0:cols]).astype(BF16)
-        copy = pltpu.make_async_copy(
-            out.at[k], out_hbm.at[:, pl.ds(k * piece + start, cols)], sem.at[k]
-        )
-        copy.start()
-        copies.append(copy)
-        if width > cols:
-            outs, projected_ref = refs[: len(refs) - 7], refs[-6]
-            at = slice(k * (width - cols), (k + 1) * (width - cols))
-            total = sum(ref[:, at] for ref in outs)
-            projected_ref[:, at] = (total + back[:, cols:]).astype(BF16)
+        both = jnp.dot(jnp.concatenate(here, axis=0), packed, preferred_element_type=F32)
+        for n in (k, k + 1):
+            back = both[(n - k) * rows : (n - k + 1) * rows, :]
+            pltpu.make_async_copy(base.at[n], base.at[n], base_sem.at[n]).wait()
+            out[n] = (base[n] + back[:, 0:cols]).astype(BF16)
+            copy = pltpu.make_async_copy(
+                out.at[n], out_hbm.at[:, pl.ds(n * piece + start, cols)], sem.at[n]
+            )
+            copy.start()
+            copies.append(copy)
+            if extra:
+                if n == 0:
+                    wait_all(late)
+                at = slice(n * (width - cols), (n + 1) * (width - cols))
+                total = sum(ref[:, at] for ref in sums) + back[:, cols:]
+                projected_ref[:, at] = total.astype(BF16)
     wait_all(copies)
 
 
@@ -703,7 +724,7 @@
         name="rank_grad_back",
     )(got_grads, right_factor, left_factor)
     rank_rows, mask_rows = hbm(rank_rows, mask_rows)
-    got_back = exchange(held(back_first, [got_tokens] + after.get("third", [])))
+    got_back = exchange(held(back_first, after.get("third", [])))
 
     back_second, low_rows = call(
         functools.partial(forth_kernel, cap),
@@ -734,7 +755,7 @@
     )(got_tokens, mask_rows, left_factor, right_factor, hbm(back_second))
     low_rows = hbm(low_rows)
     fourth = shares["last"]([low_rows]) if paired else []
-    got_rest = exchange(held(back_second, [got_back] + fourth))
+    got_rest = exchange(held(back_second, fourth))
 
     if paired:
         base_out, base_mine, base_pair = paired_base(
@@ -743,10 +764,7 @@
     else:
         base_out, base_mine = whole_base(tokens, grad_out, base_weight)
         base_pair = base_mine
-    outs, out_specs = [base_out], [whole((rows, narrow))]
-    if paired:
-        outs.append(base_pair)
-        out_specs.append(pl.BlockSpec((rows, narrow), lambda i: (0, width // 2 // narrow)))
+    outs = [base_out] + ([base_pair] if paired else [])
 
     grad_a, grad_b = call(
         functools.partial(page_grad_kernel, cap),
@@ -762,47 +780,46 @@
 
     combine_cost = cost(rows * total * width, total * wp + 4 * rows * width)
 
-    def combine_scratch(cols):
+    def combine_scratch(cols, extra):
         return [
             pltpu.VMEM((CHUNKS, rows, cols), BF16),
             pltpu.SemaphoreType.DMA((CHUNKS,)),
             pltpu.VMEM((CHUNKS, rows, cols), F32),
             pltpu.SemaphoreType.DMA((CHUNKS,)),
+            pltpu.VMEM((devices, block, cols + extra), BF16),
+            pltpu.VMEM((rows, rows), F32),
+            pltpu.SemaphoreType.DMA((7,)),
         ]
 
     grad_tokens = call(
-        functools.partial(combine_kernel, cap, 0),
+        functools.partial(combine_kernel, cap, 0, 0),
         out_shape=in_hbm((rows, width), BF16),
-        grid=(1,),
-        in_specs=[smem, whole((rows, rows)), whole((devices, block, split)), any_spec, any_spec],
+        in_specs=[smem] + [any_spec] * 4,
         out_specs=any_spec,
-        scratch_shapes=combine_scratch(split),
+        scratch_shapes=combine_scratch(split, 0),
         compiler_params=params(),
         cost_estimate=combine_cost,
         name="combine_first",
-    )(which, slot_col, got_back.reshape(devices, block, split), base_mine, base_pair)
+    )(which, slot_col, hbm(got_back.reshape(devices, block, split)), base_mine, base_pair)
     projected, grad_tokens = call(
-        functools.partial(combine_kernel, cap, split),
-        out_shape=(
-            in_hbm((rows, narrow), BF16),
-            in_hbm((rows, width), BF16),
-        ),
-        grid=(1,),
-        in_specs=[smem, whole((rows, rows)), whole((devices, block, rest + np_)), any_spec, any_spec, *out_specs, any_spec],
-        out_specs=(whole((rows, narrow)), any_spec),
-        scratch_shapes=combine_scratch(rest),
-        input_output_aliases={5 + len(out_specs): 1},
+        functools.partial(combine_kernel, cap, split, len(outs)),
+        out_shape=(in_hbm((rows, narrow), BF16), in_hbm((rows, width), BF16)),
+        in_specs=[smem] + [any_spec] * (5 + len(outs)),
+        out_specs=(pl.BlockSpec(memory_space=pltpu.VMEM), any_spec),
+        scratch_shapes=combine_scratch(rest, np_)
+        + [pltpu.VMEM((rows, narrow), F32) for _ in outs],
+        input_output_aliases={5 + len(outs): 1},
         compiler_params=params(),
         cost_estimate=combine_cost,
         name="combine_rest",
     )(
         which,
         slot_col,
-        got_rest.reshape(devices, block, rest + np_),
+        hbm(got_rest.reshape(devices, block, rest + np_)),
         base_mine,
         base_pair,
         *outs,
-        grad_tokens,
+        hbm(grad_tokens),
     )
 
     return projected, grad_tokens, grad_a[None], grad_b[None]

time: 196 us -> 193 us (0.985)
    unnamed x18 -> x16, local copies, waits for them, and re-layouts: 5.87 us -> 3.97 us
where the time goes in v4:
time: 193 us
  waiting for transfers between devices  68.4 us (35%)
  Pallas kernels  65.3 us (34%)
  starting transfers between devices  52.5 us (27%)
  local copies, waits for them, and re-layouts  5.48 us (3%)
    pallas_call x17, Pallas kernels, call(): return lambda *args: run(*args, *deps)  65.3 us
    ppermute x14, waiting for transfers between devices, swap(): return lax.ppermute(x, axis, [(i, i ^ 1) for i in range(size)])  32.6 us
    all_to_all x4, starting transfers between devices, exchange(): return lax.all_to_all(x, axes, split_axis=0, concat_axis=0, tiled=True)  25.8 us
    all_to_all x4, waiting for transfers between devices, exchange(): return lax.all_to_all(x, axes, split_axis=0, concat_axis=0, tiled=True)  19.6 us
    ppermute x3, waiting for transfers between devices, gather_shares(): down.append(lax.ppermute(down[-1], 'fsdp', moved))  16.2 us
    ppermute x14, starting transfers between devices, swap(): return lax.ppermute(x, axis, [(i, i ^ 1) for i in range(size)])  10.7 us
    ppermute x3, starting transfers between devices, gather_shares(): up.append(lax.ppermute(up[-1], 'fsdp', moved))  8.85 us
    ppermute x3, starting transfers between devices, gather_shares(): down.append(lax.ppermute(down[-1], 'fsdp', moved))  7.07 us
  transfers between devices with their start and end apart: 24, of which 10 were waited for; matrix products, arithmetic and copies ran while one was open for 0% of the time, Pallas kernels for 31%

profile of v4, /device:TPU:13, one launch (start us, length us, event | category | flops | bytes accessed | tf_op | source)
XLA Modules:
  0.0 192.6 jit_solution(271189272298240404)
XLA Ops:
  0.6 0.0 copy-start
  0.7 1.6 copy-done
  2.2 0.8 constant_dynamic-slice_fusion.refs_4_
  3.0 2.1 %collective-permute-start.2 = (bf16[256,1024]{1,0:T(8,128)(2,1)}, bf16[256,1024]{1,0:T(8,128)(2,1)}, u32[]{:S(2)}, u32[]{:S(2)}) collective-permute-start(bf16[256,1024]{1,0:T(8,128)(2,1)} %constant_dynamic-slice_fusion.refs_4_), channel_id=1, source_target_pairs={{4,0},{6,2},{8,4},{10,6},{12,8},{14,10},{5,1},{7,3},{9,5},{11,7},{... | collective-permute-start | bytes 1572872 | tf_op jit(solution)/shard_map/ppermute | solution.py:501
  5.1 3.2 %collective-permute-start = (bf16[256,1024]{1,0:T(8,128)(2,1)}, bf16[256,1024]{1,0:T(8,128)(2,1)}, u32[]{:S(2)}, u32[]{:S(2)}) collective-permute-start(bf16[256,1024]{1,0:T(8,128)(2,1)} %constant_dynamic-slice_fusion.refs_4_), channel_id=1, source_target_pairs={{0,4},{2,6},{4,8},{6,10},{8,12},{10,14},{1,5},{3,7},{5,9},{7,11},{... | collective-permute-start | bytes 1572872 | tf_op jit(solution)/shard_map/ppermute | solution.py:499
  8.3 2.8 %route.1 = (bf16[16,96,128]{2,1,0:T(8,128)(2,1)}, f32[1,128]{1,0:T(1,128)}, f32[128,128]{1,0:T(8,128)}) custom-call(s32[16]{0:T(128)} %refs_0_.1, s32[1,128]{1,0:T(1,128)} %bitcast.53, bf16[128,1024]{1,0:T(8,128)(2,1)} %refs_2_.5), custom_call_target="tpu_custom_call" | custom-call | flops 1 | bytes 1 | tf_op jit(solution)/shard_map/route/pallas_call | solution.py:419
  11.2 6.9 %all-to-all-start = ((bf16[16,96,128]{2,1,0:T(8,128)(2,1)}), bf16[16,96,128]{2,1,0:T(8,128)(2,1)S(1)}, u32[]{:S(2)}, u32[]{:S(2)}) async-start(bf16[16,96,128]{2,1,0:T(8,128)(2,1)} %get-tuple-element.22), calls=%async_computation | async-start | bytes 786432 | tf_op jit(solution)/shard_map/all_to_all | solution.py:646
  18.1 1.2 collective-permute-start.5
  19.3 0.3 collective-permute-start.4
  19.6 0.0 collective-permute-done.2.refs_1_.refs_2_
  19.6 2.0 %collective-permute-start.3 = (bf16[256,1024]{1,0:T(8,128)(2,1)}, bf16[256,1024]{1,0:T(8,128)(2,1)S(1)}, u32[]{:S(2)}, u32[]{:S(2)}) collective-permute-start(bf16[256,1024]{1,0:T(8,128)(2,1)} %collective-permute-done.2.refs_1_.refs_2_), channel_id=1, source_target_pairs={{4,0},{6,2},{8,4},{10,6},{5,1},{7,3},{9,5},{11,7},{20,16},{22,18},... | collective-permute-start | bytes 1572872 | tf_op jit(solution)/shard_map/ppermute | solution.py:501
  21.6 0.0 collective-permute-done.refs_2_
  21.6 4.1 %collective-permute-start.1 = (bf16[256,1024]{1,0:T(8,128)(2,1)}, bf16[256,1024]{1,0:T(8,128)(2,1)}, u32[]{:S(2)}, u32[]{:S(2)}) collective-permute-start(bf16[256,1024]{1,0:T(8,128)(2,1)} %collective-permute-done.refs_2_), channel_id=1, source_target_pairs={{4,8},{6,10},{8,12},{10,14},{5,9},{7,11},{9,13},{11,15},{20,24},{2... | collective-permute-start | bytes 1572872 | tf_op jit(solution)/shard_map/ppermute | solution.py:499
  25.7 6.6 %dispatch.1.refs_0_ = bf16[1280,1024]{1,0:T(8,128)(2,1)} custom-call(f32[1,128]{1,0:T(1,128)} %get-tuple-element.21.refs_0_, bf16[128,8192]{1,0:T(8,128)(2,1)} %refs_1_.5), custom_call_target="tpu_custom_call" | custom-call | flops 1 | bytes 1 | tf_op jit(solution)/shard_map/dispatch/pallas_call | solution.py:419
  32.3 0.0 collective-permute-done.5.refs_5_.refs_6_
  32.3 0.8 copy-done.7
  33.1 2.7 %collective-permute-done.4.refs_4_.refs_5_ = bf16[256,1024]{1,0:T(8,128)(2,1)} collective-permute-done((bf16[256,1024]{1,0:T(8,128)(2,1)}, bf16[256,1024]{1,0:T(8,128)(2,1)}, u32[]{:S(2)}, u32[]{:S(2)}) %collective-permute-start.4) | collective-permute-done | bytes 524320 | tf_op jit(solution)/shard_map/ppermute | solution.py:485
  35.8 0.0 all-to-all-done.refs_1_.refs_0_
  35.8 4.1 %collective-permute-done.3.refs_3_.refs_2_.refs_1_ = bf16[256,1024]{1,0:T(8,128)(2,1)S(1)} collective-permute-done((bf16[256,1024]{1,0:T(8,128)(2,1)}, bf16[256,1024]{1,0:T(8,128)(2,1)S(1)}, u32[]{:S(2)}, u32[]{:S(2)}) %collective-permute-start.3) | collective-permute-done | bytes 524320 | tf_op jit(solution)/shard_map/ppermute | solution.py:501
  39.9 0.0 collective-permute-done.1.refs_2_.refs_3_
  39.9 0.8 copy-done.5
  40.7 5.5 %all-to-all-start.1 = ((bf16[16,80,1024]{2,1,0:T(8,128)(2,1)}), bf16[16,80,1024]{2,1,0:T(8,128)(2,1)}, u32[]{:S(2)}, u32[]{:S(2)}) async-start(bf16[16,80,1024]{2,1,0:T(8,128)(2,1)} %bitcast.46), calls=%async_computation.1 | async-start | bytes 5242880 | tf_op jit(solution)/shard_map/all_to_all | solution.py:646
  46.2 2.5 %for_pair.1 = bf16[128,5120]{1,0:T(8,128)(2,1)} custom-call(s32[1]{0:T(128)} %bitcast.40.refs_0_, bf16[128,8192]{1,0:T(8,128)(2,1)} %refs_1_.5, bf16[128,1024]{1,0:T(8,128)(2,1)} %refs_2_.5), custom_call_target="tpu_custom_call" | custom-call | flops 1 | bytes 1 | tf_op jit(solution)/shard_map/for_pair/pallas_call | solution.py:419
  48.7 0.4 collective-permute-start.10
  49.1 1.2 collective-permute-start.11
  50.4 2.1 %pick.4.refs_8_ = bf16[256,1024]{1,0:T(8,128)(2,1)} custom-call(s32[1]{0:T(128)} %bitcast.41.refs_0_, bf16[256,1024]{1,0:T(8,128)(2,1)} %collective-permute-done.2.refs_1_.refs_2_, bf16[256,1024]{1,0:T(8,128)(2,1)} %collective-permute-done.refs_2_), custom_call_target="tpu_custom_call" | custom-call | flops 1 | bytes 1 | tf_op jit(solution)/shard_map/pick/pallas_call | solution.py:419
  52.4 0.3 collective-permute-start.12
  52.7 0.3 collective-permute-start.13
  53.0 2.3 %pick.5.refs_12_ = bf16[256,1024]{1,0:T(8,128)(2,1)} custom-call(s32[1]{0:T(128)} %bitcast.42.refs_0_, bf16[256,1024]{1,0:T(8,128)(2,1)} %copy-done.5, bf16[256,1024]{1,0:T(8,128)(2,1)} %collective-permute-done.2.refs_1_.refs_2_, bf16[256,1024]{1,0:T(8,128)(2,1)} %collective-permute-done.1.refs_2_.refs_3_), custom_call_target="tpu_custom_call" | custom-call | flops 1 | bytes 1 | tf_op jit(solution)/shard_map/pick/pallas_call | solution.py:419
  55.2 1.2 collective-permute-start.16
  56.4 6.4 %collective-permute-done.11.refs_7_.refs_5_ = bf16[256,1024]{1,0:T(8,128)(2,1)} collective-permute-done((bf16[256,1024]{1,0:T(8,128)(2,1)}, bf16[256,1024]{1,0:T(8,128)(2,1)}, u32[]{:S(2)}, u32[]{:S(2)}) %collective-permute-start.11) | collective-permute-done | bytes 524320 | tf_op jit(solution)/shard_map/ppermute | solution.py:485
  62.8 3.0 %collective-permute-start.6 = (bf16[256,1024]{1,0:T(8,128)(2,1)S(1)}, bf16[256,1024]{1,0:T(8,128)(2,1)}, u32[]{:S(2)}, u32[]{:S(2)}) collective-permute-start(bf16[256,1024]{1,0:T(8,128)(2,1)S(1)} %copy-done.6), channel_id=1, source_target_pairs={{4,0},{6,2},{5,1},{7,3},{20,16},{22,18},{21,17},{23,19}} | collective-permute-start | bytes 1572872 | tf_op jit(solution)/shard_map/ppermute | solution.py:501
  65.9 10.5 %collective-permute-done.12.refs_9_.refs_3_ = bf16[256,1024]{1,0:T(8,128)(2,1)} collective-permute-done((bf16[256,1024]{1,0:T(8,128)(2,1)}, bf16[256,1024]{1,0:T(8,128)(2,1)}, u32[]{:S(2)}, u32[]{:S(2)}) %collective-permute-start.12) | collective-permute-done | bytes 524320 | tf_op jit(solution)/shard_map/ppermute | solution.py:485
  76.3 1.2 collective-permute-start.14
  77.5 0.0 collective-permute-done.13.refs_10_.refs_4_
  77.5 0.0 copy-start.1
  77.6 1.5 collective-permute-start.7
  79.1 8.8 %rank_grad_back.1 = (bf16[1280,512]{1,0:T(8,128)(2,1)}, bf16[1280,640]{1,0:T(8,128)(2,1)}, bf16[1280,128]{1,0:T(8,128)(2,1)}, bf16[1280,128]{1,0:T(8,128)(2,1)}) custom-call(bf16[16,96,128]{2,1,0:T(8,128)(2,1)} %copy-done.2, bf16[128,1024]{1,0:T(8,128)(2,1)} %bitcast.51, bf16[128,8192]{1,0:T(8,128)(2,1)} %bitcast.48), custom_call_target="tpu_custom_call" | custom-call | flops 1 | bytes 1 | tf_op jit(solution)/shard_map/rank_grad_back/pallas_call | solution.py:419
  87.9 12.1 %collective-permute-done.6.refs_1_.refs_2_ = bf16[256,1024]{1,0:T(8,128)(2,1)} collective-permute-done((bf16[256,1024]{1,0:T(8,128)(2,1)S(1)}, bf16[256,1024]{1,0:T(8,128)(2,1)}, u32[]{:S(2)}, u32[]{:S(2)}) %collective-permute-start.6) | collective-permute-done | bytes 524320 | tf_op jit(solution)/shard_map/ppermute | solution.py:501
  100.0 0.0 collective-permute-done.14.refs_11_.refs_8_
  100.0 0.0 collective-permute-done.16.refs_14_.refs_7_
  100.0 0.0 collective-permute-done.15.refs_13_.refs_6_
  100.0 5.1 %all-to-all-done.1 = bf16[16,80,1024]{2,1,0:T(8,128)(2,1)} async-done(((bf16[16,80,1024]{2,1,0:T(8,128)(2,1)}), bf16[16,80,1024]{2,1,0:T(8,128)(2,1)}, u32[]{:S(2)}, u32[]{:S(2)}) %all-to-all-start.1) | async-done | bytes 2621472 | tf_op jit(solution)/shard_map/all_to_all | solution.py:646
  105.1 8.9 %all-to-all-start.3 = ((bf16[16,80,512]{2,1,0:T(8,128)(2,1)}), bf16[16,80,512]{2,1,0:T(8,128)(2,1)S(1)}, u32[]{:S(2)}, u32[]{:S(2)}) async-start(bf16[16,80,512]{2,1,0:T(8,128)(2,1)} %bitcast.50), calls=%async_computation.3 | async-start | bytes 2621440 | tf_op jit(solution)/shard_map/all_to_all | solution.py:646
  114.0 2.4 %pick.3.refs_16_ = bf16[256,1024]{1,0:T(8,128)(2,1)} custom-call(s32[1]{0:T(128)} %bitcast.6.refs_0_, bf16[256,1024]{1,0:T(8,128)(2,1)} %collective-permute-done.6.refs_1_.refs_2_, bf16[256,1024]{1,0:T(8,128)(2,1)} %copy-done.5, bf16[256,1024]{1,0:T(8,128)(2,1)} %collective-permute-done.1.refs_2_.refs_3_, ...), custom_call_target="tpu_custom_call" | custom-call | flops 1 | bytes 1 | tf_op jit(solution)/shard_map/pick/pallas_call | solution.py:419
  116.4 0.3 collective-permute-start.8
  116.7 1.2 collective-permute-start.9
  117.9 0.3 collective-permute-start.17
  118.1 10.2 %lowrank_out.1 = (bf16[1280,640]{1,0:T(8,128)(2,1)}, bf16[1280,128]{1,0:T(8,128)(2,1)}) custom-call(bf16[1280,1024]{1,0:T(8,128)(2,1)} %bitcast.3.refs_0_, bf16[1280,128]{1,0:T(8,128)(2,1)} %get-tuple-element.23.refs_1_, bf16[128,8192]{1,0:T(8,128)(2,1)} %bitcast.49, bf16[128,1024]{1,0:T(8,128)(2,1)} %bitcast.52, ...), custom_call_target="tpu_custom_call", output_to_operand_aliasing={{0}: (4, {})} | custom-call | flops 1 | bytes 1 | tf_op jit(solution)/shard_map/lowrank_out/pallas_call | solution.py:419
  128.3 10.6 %collective-permute-done.8.refs_0_ = bf16[256,1024]{1,0:T(8,128)(2,1)S(1)} collective-permute-done((bf16[256,1024]{1,0:T(8,128)(2,1)}, bf16[256,1024]{1,0:T(8,128)(2,1)S(1)}, u32[]{:S(2)}, u32[]{:S(2)}) %collective-permute-start.8) | collective-permute-done | bytes 524320 | tf_op jit(solution)/shard_map/ppermute | solution.py:485
  138.9 0.8 copy-done.4
  139.7 1.2 collective-permute-start.18
  140.9 0.0 collective-permute-done.9.refs_2_.refs_18_
  140.9 4.1 %all-to-all-done.3.refs_2_ = bf16[16,80,512]{2,1,0:T(8,128)(2,1)S(1)} async-done(((bf16[16,80,512]{2,1,0:T(8,128)(2,1)}), bf16[16,80,512]{2,1,0:T(8,128)(2,1)S(1)}, u32[]{:S(2)}, u32[]{:S(2)}) %all-to-all-start.3) | async-done | bytes 1310752 | tf_op jit(solution)/shard_map/all_to_all | solution.py:646
  145.0 4.5 %all-to-all-start.2 = ((bf16[16,80,640]{2,1,0:T(8,128)(2,1)}), bf16[16,80,640]{2,1,0:T(8,128)(2,1)}, u32[]{:S(2)}, u32[]{:S(2)}) async-start(bf16[16,80,640]{2,1,0:T(8,128)(2,1)} %bitcast.47), calls=%async_computation.2 | async-start | bytes 3276800 | tf_op jit(solution)/shard_map/all_to_all | solution.py:646
  149.6 0.7 stack.131.refs_0_
  150.3 2.4 %collective-permute-done.18.refs_19_ = bf16[256,1024]{1,0:T(8,128)(2,1)} collective-permute-done((bf16[256,1024]{1,0:T(8,128)(2,1)}, bf16[256,1024]{1,0:T(8,128)(2,1)}, u32[]{:S(2)}, u32[]{:S(2)}) %collective-permute-start.18) | collective-permute-done | bytes 524320 | tf_op jit(solution)/shard_map/ppermute | solution.py:485
  152.7 11.3 %base.1 = (f32[128,1024]{1,0:T(8,128)}, f32[128,4096]{1,0:T(8,128)}, f32[128,5120]{1,0:T(8,128)}) custom-call(s32[32]{0:T(128)} %stack.131.refs_0_, bf16[128,8192]{1,0:T(8,128)(2,1)} %refs_1_.5, bf16[128,1024]{1,0:T(8,128)(2,1)} %refs_2_.5, bf16[128,5120]{1,0:T(8,128)(2,1)} %held.8.refs_3_, bf16[256,1024]{1,0:T(8,128)(2,1)} %constant_dynamic-slice_fusion.refs_4_, ...), custom_call_target="tpu_custom_call" | custom-call | flops 1 | bytes 1 | tf_op jit(solution)/shard_map/base/pallas_call | solution.py:419
  164.0 1.7 collective-permute-start.19
  165.7 7.0 %page_grads.1 = (bf16[128,8192]{1,0:T(8,128)(2,1)}, bf16[128,1024]{1,0:T(8,128)(2,1)}) custom-call(bf16[1280,1024]{1,0:T(8,128)(2,1)} %bitcast.3.refs_0_, bf16[16,96,128]{2,1,0:T(8,128)(2,1)} %copy-done.2, bf16[1280,128]{1,0:T(8,128)(2,1)} %get-tuple-element.26.refs_1_.refs_2_, bf16[1280,128]{1,0:T(8,128)(2,1)} %get-tuple-element.33.refs_3_), custom_call_target="tpu_custom_call" | custom-call | flops 1 | bytes 1 | tf_op jit(solution)/shard_map/page_grads/pallas_call | solution.py:419
  172.7 0.0 collective-permute-done.19.refs_4_.refs_6_
  172.7 4.1 %combine_first.1.refs_7_ = bf16[128,8192]{1,0:T(8,128)(2,1)} custom-call(s32[1]{0:T(128)} %bitcast.refs_0_, f32[128,128]{1,0:T(8,128)} %get-tuple-element.20.refs_1_, bf16[16,80,512]{2,1,0:T(8,128)(2,1)} %copy-done.3, f32[128,4096]{1,0:T(8,128)} %get-tuple-element.27.refs_3_, f32[128,5120]{1,0:T(8,128)} %collective-permute-done.19.refs_4_.refs_6_), custom_call_target="tpu_custom_call" | custom-call | flops 1 | bytes 1 | tf_op jit(solution)/shard_map/combine_first/pallas_call | solution.py:419
  176.8 10.4 %all-to-all-done.2.refs_2_ = bf16[16,80,640]{2,1,0:T(8,128)(2,1)} async-done(((bf16[16,80,640]{2,1,0:T(8,128)(2,1)}), bf16[16,80,640]{2,1,0:T(8,128)(2,1)}, u32[]{:S(2)}, u32[]{:S(2)}) %all-to-all-start.2) | async-done | bytes 1638432 | tf_op jit(solution)/shard_map/all_to_all | solution.py:646
  187.2 5.3 %combine_rest.1 = (bf16[128,1024]{1,0:T(8,128)(2,1)}, bf16[128,8192]{1,0:T(8,128)(2,1)}) custom-call(s32[1]{0:T(128)} %bitcast.refs_0_, f32[128,128]{1,0:T(8,128)} %get-tuple-element.20.refs_1_, bf16[16,80,640]{2,1,0:T(8,128)(2,1)} %all-to-all-done.2.refs_2_, f32[128,4096]{1,0:T(8,128)} %get-tuple-element.27.refs_3_, ...), custom_call_target="tpu_custom_call", output_to_operand_aliasing={{1}: (7, {})} | custom-call | flops 1 | bytes 1 | tf_op jit(solution)/shard_map/combine_rest/pallas_call | solution.py:419
  (19 shorter events, 0.0 us)
Async XLA Ops:
  0.6 1.6 copy-start
  3.0 16.6 %collective-permute-start.2 = (bf16[256,1024]{1,0:T(8,128)(2,1)}, bf16[256,1024]{1,0:T(8,128)(2,1)}, u32[]{:S(2)}, u32[]{:S(2)}) collective-permute-start(bf16[256,1024]{1,0:T(8,128)(2,1)} %constant_dynamic-slice_fusion.refs_4_), channel_id=1, source_target_pairs={{4,0},{6,2},{8,4},{10,6},{12,8},{14,10},{5,1},{7,3},{9,5},{11,7},{... | collective-permute-start | bytes 1572872 | tf_op jit(solution)/shard_map/ppermute | solution.py:501
  5.1 16.5 %collective-permute-start = (bf16[256,1024]{1,0:T(8,128)(2,1)}, bf16[256,1024]{1,0:T(8,128)(2,1)}, u32[]{:S(2)}, u32[]{:S(2)}) collective-permute-start(bf16[256,1024]{1,0:T(8,128)(2,1)} %constant_dynamic-slice_fusion.refs_4_), channel_id=1, source_target_pairs={{0,4},{2,6},{4,8},{6,10},{8,12},{10,14},{1,5},{3,7},{5,9},{7,11},{... | collective-permute-start | bytes 1572872 | tf_op jit(solution)/shard_map/ppermute | solution.py:499
  11.2 24.7 %all-to-all-start = ((bf16[16,96,128]{2,1,0:T(8,128)(2,1)}), bf16[16,96,128]{2,1,0:T(8,128)(2,1)S(1)}, u32[]{:S(2)}, u32[]{:S(2)}) async-start(bf16[16,96,128]{2,1,0:T(8,128)(2,1)} %get-tuple-element.22), calls=%async_computation | async-start | bytes 786432 | tf_op jit(solution)/shard_map/all_to_all | solution.py:646
  18.1 14.2 %collective-permute-start.5 = (bf16[256,1024]{1,0:T(8,128)(2,1)}, bf16[256,1024]{1,0:T(8,128)(2,1)S(1)}, u32[]{:S(2)}, u32[]{:S(2)}) collective-permute-start(bf16[256,1024]{1,0:T(8,128)(2,1)} %constant_dynamic-slice_fusion.refs_4_), channel_id=1, source_target_pairs={{0,16},{16,0},{1,17},{17,1},{2,18},{18,2},{3,19},{19,3},{4,20},{20... | collective-permute-start | bytes 1572872 | tf_op jit(solution)/shard_map/ppermute | solution.py:485
  19.3 16.5 %collective-permute-start.4 = (bf16[256,1024]{1,0:T(8,128)(2,1)}, bf16[256,1024]{1,0:T(8,128)(2,1)}, u32[]{:S(2)}, u32[]{:S(2)}) collective-permute-start(bf16[256,1024]{1,0:T(8,128)(2,1)} %constant_dynamic-slice_fusion.refs_4_), channel_id=1, source_target_pairs={{0,2},{2,0},{4,6},{6,4},{8,10},{10,8},{12,14},{14,12},{1,3},{3,1},... | collective-permute-start | bytes 1572872 | tf_op jit(solution)/shard_map/ppermute | solution.py:485
  19.6 20.3 %collective-permute-start.3 = (bf16[256,1024]{1,0:T(8,128)(2,1)}, bf16[256,1024]{1,0:T(8,128)(2,1)S(1)}, u32[]{:S(2)}, u32[]{:S(2)}) collective-permute-start(bf16[256,1024]{1,0:T(8,128)(2,1)} %collective-permute-done.2.refs_1_.refs_2_), channel_id=1, source_target_pairs={{4,0},{6,2},{8,4},{10,6},{5,1},{7,3},{9,5},{11,7},{20,16},{22,18},... | collective-permute-start | bytes 1572872 | tf_op jit(solution)/shard_map/ppermute | solution.py:501
  21.6 18.3 %collective-permute-start.1 = (bf16[256,1024]{1,0:T(8,128)(2,1)}, bf16[256,1024]{1,0:T(8,128)(2,1)}, u32[]{:S(2)}, u32[]{:S(2)}) collective-permute-start(bf16[256,1024]{1,0:T(8,128)(2,1)} %collective-permute-done.refs_2_), channel_id=1, source_target_pairs={{4,8},{6,10},{8,12},{10,14},{5,9},{7,11},{9,13},{11,15},{20,24},{2... | collective-permute-start | bytes 1572872 | tf_op jit(solution)/shard_map/ppermute | solution.py:499
  32.3 0.8 copy-start.7
  35.8 4.1 %copy-start.2 = (bf16[16,96,128]{2,1,0:T(8,128)(2,1)}, bf16[16,96,128]{2,1,0:T(8,128)(2,1)S(1)}, u32[]{:S(2)}) copy-start(bf16[16,96,128]{2,1,0:T(8,128)(2,1)S(1)} %all-to-all-done.refs_1_.refs_0_) | copy-start | bytes 1179652
  39.9 0.8 copy-start.5
  40.7 64.4 %all-to-all-start.1 = ((bf16[16,80,1024]{2,1,0:T(8,128)(2,1)}), bf16[16,80,1024]{2,1,0:T(8,128)(2,1)}, u32[]{:S(2)}, u32[]{:S(2)}) async-start(bf16[16,80,1024]{2,1,0:T(8,128)(2,1)} %bitcast.46), calls=%async_computation.1 | async-start | bytes 5242880 | tf_op jit(solution)/shard_map/all_to_all | solution.py:646
  48.7 28.8 %collective-permute-start.10 = (bf16[128,5120]{1,0:T(8,128)(2,1)}, bf16[128,5120]{1,0:T(8,128)(2,1)S(1)}, u32[]{:S(2)}, u32[]{:S(2)}) collective-permute-start(bf16[128,5120]{1,0:T(8,128)(2,1)} %for_pair.1), channel_id=1, source_target_pairs={{0,1},{1,0},{2,3},{3,2},{4,5},{5,4},{6,7},{7,6},{8,9},{9,8},{10,11... | collective-permute-start | bytes 3932168 | tf_op jit(solution)/shard_map/ppermute | solution.py:485
  49.1 13.7 %collective-permute-start.11 = (bf16[256,1024]{1,0:T(8,128)(2,1)}, bf16[256,1024]{1,0:T(8,128)(2,1)}, u32[]{:S(2)}, u32[]{:S(2)}) collective-permute-start(bf16[256,1024]{1,0:T(8,128)(2,1)} %collective-permute-done.4.refs_4_.refs_5_), channel_id=1, source_target_pairs={{0,16},{16,0},{1,17},{17,1},{2,18},{18,2},{3,19},{19,3},{4,20},{20... | collective-permute-start | bytes 1572872 | tf_op jit(solution)/shard_map/ppermute | solution.py:485
  52.4 23.9 %collective-permute-start.12 = (bf16[256,1024]{1,0:T(8,128)(2,1)}, bf16[256,1024]{1,0:T(8,128)(2,1)}, u32[]{:S(2)}, u32[]{:S(2)}) collective-permute-start(bf16[256,1024]{1,0:T(8,128)(2,1)} %pick.4.refs_8_), channel_id=1, source_target_pairs={{0,2},{2,0},{4,6},{6,4},{8,10},{10,8},{12,14},{14,12},{1,3},{3,1},... | collective-permute-start | bytes 1572872 | tf_op jit(solution)/shard_map/ppermute | solution.py:485
  52.7 24.8 %collective-permute-start.13 = (bf16[256,1024]{1,0:T(8,128)(2,1)}, bf16[256,1024]{1,0:T(8,128)(2,1)}, u32[]{:S(2)}, u32[]{:S(2)}) collective-permute-start(bf16[256,1024]{1,0:T(8,128)(2,1)} %pick.4.refs_8_), channel_id=1, source_target_pairs={{0,16},{16,0},{1,17},{17,1},{2,18},{18,2},{3,19},{19,3},{4,20},{20... | collective-permute-start | bytes 1572872 | tf_op jit(solution)/shard_map/ppermute | solution.py:485
  53.0 9.9 %copy-start.6 = (bf16[256,1024]{1,0:T(8,128)(2,1)S(1)}, bf16[256,1024]{1,0:T(8,128)(2,1)}, u32[]{:S(2)}) copy-start(bf16[256,1024]{1,0:T(8,128)(2,1)} %copy-done.5) | copy-start | bytes 1572868
  55.2 44.8 %collective-permute-start.16 = (bf16[256,1024]{1,0:T(8,128)(2,1)}, bf16[256,1024]{1,0:T(8,128)(2,1)}, u32[]{:S(2)}, u32[]{:S(2)}) collective-permute-start(bf16[256,1024]{1,0:T(8,128)(2,1)} %pick.5.refs_12_), channel_id=1, source_target_pairs={{0,16},{16,0},{1,17},{17,1},{2,18},{18,2},{3,19},{19,3},{4,20},{20... | collective-permute-start | bytes 1572872 | tf_op jit(solution)/shard_map/ppermute | solution.py:485
  62.8 37.1 %collective-permute-start.6 = (bf16[256,1024]{1,0:T(8,128)(2,1)S(1)}, bf16[256,1024]{1,0:T(8,128)(2,1)}, u32[]{:S(2)}, u32[]{:S(2)}) collective-permute-start(bf16[256,1024]{1,0:T(8,128)(2,1)S(1)} %copy-done.6), channel_id=1, source_target_pairs={{4,0},{6,2},{5,1},{7,3},{20,16},{22,18},{21,17},{23,19}} | collective-permute-start | bytes 1572872 | tf_op jit(solution)/shard_map/ppermute | solution.py:501
  76.3 23.7 %collective-permute-start.14 = (bf16[256,1024]{1,0:T(8,128)(2,1)}, bf16[256,1024]{1,0:T(8,128)(2,1)}, u32[]{:S(2)}, u32[]{:S(2)}) collective-permute-start(bf16[256,1024]{1,0:T(8,128)(2,1)} %collective-permute-done.12.refs_9_.refs_3_), channel_id=1, source_target_pairs={{0,16},{16,0},{1,17},{17,1},{2,18},{18,2},{3,19},{19,3},{4,20},{20... | collective-permute-start | bytes 1572872 | tf_op jit(solution)/shard_map/ppermute | solution.py:485
  77.5 22.5 %collective-permute-start.15 = (bf16[256,1024]{1,0:T(8,128)(2,1)}, bf16[256,1024]{1,0:T(8,128)(2,1)}, u32[]{:S(2)}, u32[]{:S(2)}) collective-permute-start(bf16[256,1024]{1,0:T(8,128)(2,1)} %pick.5.refs_12_), channel_id=1, source_target_pairs={{0,2},{2,0},{4,6},{6,4},{8,10},{10,8},{12,14},{14,12},{1,3},{3,1},... | collective-permute-start | bytes 1572872 | tf_op jit(solution)/shard_map/ppermute | solution.py:485
  77.5 22.5 %copy-start.1 = (bf16[128,5120]{1,0:T(8,128)(2,1)}, bf16[128,5120]{1,0:T(8,128)(2,1)S(1)}, u32[]{:S(2)}) copy-start(bf16[128,5120]{1,0:T(8,128)(2,1)S(1)} %collective-permute-done.10.refs_0_.refs_9_) | copy-start | bytes 3932164
  77.6 22.4 %collective-permute-start.7 = (bf16[256,1024]{1,0:T(8,128)(2,1)}, bf16[256,1024]{1,0:T(8,128)(2,1)}, u32[]{:S(2)}, u32[]{:S(2)}) collective-permute-start(bf16[256,1024]{1,0:T(8,128)(2,1)} %collective-permute-done.1.refs_2_.refs_3_), channel_id=1, source_target_pairs={{8,12},{10,14},{9,13},{11,15},{24,28},{26,30},{25,29},{27,31}} | collective-permute-start | bytes 1572872 | tf_op jit(solution)/shard_map/ppermute | solution.py:499
  105.1 39.9 %all-to-all-start.3 = ((bf16[16,80,512]{2,1,0:T(8,128)(2,1)}), bf16[16,80,512]{2,1,0:T(8,128)(2,1)S(1)}, u32[]{:S(2)}, u32[]{:S(2)}) async-start(bf16[16,80,512]{2,1,0:T(8,128)(2,1)} %bitcast.50), calls=%async_computation.3 | async-start | bytes 2621440 | tf_op jit(solution)/shard_map/all_to_all | solution.py:646
  116.4 22.5 %collective-permute-start.8 = (bf16[256,1024]{1,0:T(8,128)(2,1)}, bf16[256,1024]{1,0:T(8,128)(2,1)S(1)}, u32[]{:S(2)}, u32[]{:S(2)}) collective-permute-start(bf16[256,1024]{1,0:T(8,128)(2,1)} %pick.3.refs_16_), channel_id=1, source_target_pairs={{0,2},{2,0},{4,6},{6,4},{8,10},{10,8},{12,14},{14,12},{1,3},{3,1},... | collective-permute-start | bytes 1572872 | tf_op jit(solution)/shard_map/ppermute | solution.py:485
  116.7 24.2 %collective-permute-start.9 = (bf16[256,1024]{1,0:T(8,128)(2,1)}, bf16[256,1024]{1,0:T(8,128)(2,1)}, u32[]{:S(2)}, u32[]{:S(2)}) collective-permute-start(bf16[256,1024]{1,0:T(8,128)(2,1)} %pick.3.refs_16_), channel_id=1, source_target_pairs={{0,16},{16,0},{1,17},{17,1},{2,18},{18,2},{3,19},{19,3},{4,20},{20... | collective-permute-start | bytes 1572872 | tf_op jit(solution)/shard_map/ppermute | solution.py:485
  117.9 32.4 %collective-permute-start.17 = (bf16[256,1024]{1,0:T(8,128)(2,1)}, bf16[256,1024]{1,0:T(8,128)(2,1)}, u32[]{:S(2)}, u32[]{:S(2)}) collective-permute-start(bf16[256,1024]{1,0:T(8,128)(2,1)} %collective-permute-done.15.refs_13_.refs_6_), channel_id=1, source_target_pairs={{0,16},{16,0},{1,17},{17,1},{2,18},{18,2},{3,19},{19,3},{4,20},{20... | collective-permute-start | bytes 1572872 | tf_op jit(solution)/shard_map/ppermute | solution.py:485
  138.9 0.8 copy-start.4
  139.7 13.0 %collective-permute-start.18 = (bf16[256,1024]{1,0:T(8,128)(2,1)}, bf16[256,1024]{1,0:T(8,128)(2,1)}, u32[]{:S(2)}, u32[]{:S(2)}) collective-permute-start(bf16[256,1024]{1,0:T(8,128)(2,1)} %held.6.refs_1_.refs_17_), channel_id=1, source_target_pairs={{0,16},{16,0},{1,17},{17,1},{2,18},{18,2},{3,19},{19,3},{4,20},{20... | collective-permute-start | bytes 1572872 | tf_op jit(solution)/shard_map/ppermute | solution.py:485
  145.0 5.3 %copy-start.3 = (bf16[16,80,512]{2,1,0:T(8,128)(2,1)}, bf16[16,80,512]{2,1,0:T(8,128)(2,1)S(1)}, u32[]{:S(2)}) copy-start(bf16[16,80,512]{2,1,0:T(8,128)(2,1)S(1)} %all-to-all-done.3.refs_2_) | copy-start | bytes 3932164
  145.0 42.2 %all-to-all-start.2 = ((bf16[16,80,640]{2,1,0:T(8,128)(2,1)}), bf16[16,80,640]{2,1,0:T(8,128)(2,1)}, u32[]{:S(2)}, u32[]{:S(2)}) async-start(bf16[16,80,640]{2,1,0:T(8,128)(2,1)} %bitcast.47), calls=%async_computation.2 | async-start | bytes 3276800 | tf_op jit(solution)/shard_map/all_to_all | solution.py:646
  164.0 8.6 %collective-permute-start.19 = (f32[128,5120]{1,0:T(8,128)}, f32[128,5120]{1,0:T(8,128)}, u32[]{:S(2)}, u32[]{:S(2)}) collective-permute-start(f32[128,5120]{1,0:T(8,128)} %get-tuple-element.28), channel_id=1, source_target_pairs={{0,1},{1,0},{2,3},{3,2},{4,5},{5,4},{6,7},{7,6},{8,9},{9,8},{10,11... | collective-permute-start | bytes 7864328 | tf_op jit(solution)/shard_map/ppermute | solution.py:485

commit v5 on v4

--- a/solution.py
+++ b/solution.py
@@ -691,7 +691,9 @@
     if paired:
         shares = gather_shares(base_weight, 2)
         after = shares["after"]
-        pair = swap(for_pair(tokens, grad_out), "tenant")
+        pair = for_pair(tokens, grad_out)
+        after["first"].append(pair)
+        pair = swap(pair, "tenant")
         after["third"].append(pair)
     got_tokens = exchange(held(send_tokens, [got_grads] + after.get("first", [])))
 

time: 193 us -> 194 us (level)
    unnamed x16 -> x14, local copies, waits for them, and re-layouts: 3.97 us -> 3.17 us
where the time goes in v5:
time: 194 us; the launch traced here: 193 us
  waiting for transfers between devices  69.2 us (36%)
  Pallas kernels  65.3 us (34%)
  starting transfers between devices  52.4 us (27%)
  local copies, waits for them, and re-layouts  4.61 us (2%)
    pallas_call x17, Pallas kernels, call(): return lambda *args: run(*args, *deps)  65.3 us
    ppermute x14, waiting for transfers between devices, swap(): return lax.ppermute(x, axis, [(i, i ^ 1) for i in range(size)])  33.5 us
    all_to_all x4, starting transfers between devices, exchange(): return lax.all_to_all(x, axes, split_axis=0, concat_axis=0, tiled=True)  25.9 us
    all_to_all x4, waiting for transfers between devices, exchange(): return lax.all_to_all(x, axes, split_axis=0, concat_axis=0, tiled=True)  19.6 us
    ppermute x3, waiting for transfers between devices, gather_shares(): down.append(lax.ppermute(down[-1], 'fsdp', moved))  16.2 us
    ppermute x14, starting transfers between devices, swap(): return lax.ppermute(x, axis, [(i, i ^ 1) for i in range(size)])  10.7 us
    ppermute x3, starting transfers between devices, gather_shares(): up.append(lax.ppermute(up[-1], 'fsdp', moved))  8.85 us
    ppermute x3, starting transfers between devices, gather_shares(): down.append(lax.ppermute(down[-1], 'fsdp', moved))  7.06 us
  transfers between devices with their start and end apart: 24, of which 10 were waited for; matrix products, arithmetic and copies ran while one was open for 0% of the time, Pallas kernels for 31%

profile of v5, /device:TPU:13, one launch (start us, length us, event | category | flops | bytes accessed | tf_op | source)
XLA Modules:
  0.0 192.7 jit_solution(16108790373398149365)
XLA Ops:
  0.6 0.0 copy-start
  0.7 1.6 copy-done
  2.2 0.8 constant_dynamic-slice_fusion.refs_4_
  3.0 2.1 %collective-permute-start.2 = (bf16[256,1024]{1,0:T(8,128)(2,1)}, bf16[256,1024]{1,0:T(8,128)(2,1)}, u32[]{:S(2)}, u32[]{:S(2)}) collective-permute-start(bf16[256,1024]{1,0:T(8,128)(2,1)} %constant_dynamic-slice_fusion.refs_4_), channel_id=1, source_target_pairs={{4,0},{6,2},{8,4},{10,6},{12,8},{14,10},{5,1},{7,3},{9,5},{11,7},{... | collective-permute-start | bytes 1572872 | tf_op jit(solution)/shard_map/ppermute | solution.py:501
  5.1 3.2 %collective-permute-start = (bf16[256,1024]{1,0:T(8,128)(2,1)}, bf16[256,1024]{1,0:T(8,128)(2,1)}, u32[]{:S(2)}, u32[]{:S(2)}) collective-permute-start(bf16[256,1024]{1,0:T(8,128)(2,1)} %constant_dynamic-slice_fusion.refs_4_), channel_id=1, source_target_pairs={{0,4},{2,6},{4,8},{6,10},{8,12},{10,14},{1,5},{3,7},{5,9},{7,11},{... | collective-permute-start | bytes 1572872 | tf_op jit(solution)/shard_map/ppermute | solution.py:499
  8.3 2.8 %route.1 = (bf16[16,96,128]{2,1,0:T(8,128)(2,1)}, f32[1,128]{1,0:T(1,128)}, f32[128,128]{1,0:T(8,128)}) custom-call(s32[16]{0:T(128)} %refs_0_.1, s32[1,128]{1,0:T(1,128)} %bitcast.53, bf16[128,1024]{1,0:T(8,128)(2,1)} %refs_2_.5), custom_call_target="tpu_custom_call" | custom-call | flops 1 | bytes 1 | tf_op jit(solution)/shard_map/route/pallas_call | solution.py:419
  11.2 6.9 %all-to-all-start = ((bf16[16,96,128]{2,1,0:T(8,128)(2,1)}), bf16[16,96,128]{2,1,0:T(8,128)(2,1)S(1)}, u32[]{:S(2)}, u32[]{:S(2)}) async-start(bf16[16,96,128]{2,1,0:T(8,128)(2,1)} %get-tuple-element.22), calls=%async_computation | async-start | bytes 786432 | tf_op jit(solution)/shard_map/all_to_all | solution.py:646
  18.1 1.2 collective-permute-start.5
  19.3 0.3 collective-permute-start.4
  19.6 0.0 collective-permute-done.2.refs_1_.refs_2_
  19.6 2.0 %collective-permute-start.3 = (bf16[256,1024]{1,0:T(8,128)(2,1)}, bf16[256,1024]{1,0:T(8,128)(2,1)S(1)}, u32[]{:S(2)}, u32[]{:S(2)}) collective-permute-start(bf16[256,1024]{1,0:T(8,128)(2,1)} %collective-permute-done.2.refs_1_.refs_2_), channel_id=1, source_target_pairs={{4,0},{6,2},{8,4},{10,6},{5,1},{7,3},{9,5},{11,7},{20,16},{22,18},... | collective-permute-start | bytes 1572872 | tf_op jit(solution)/shard_map/ppermute | solution.py:501
  21.6 0.0 collective-permute-done.refs_2_
  21.6 4.1 %collective-permute-start.1 = (bf16[256,1024]{1,0:T(8,128)(2,1)}, bf16[256,1024]{1,0:T(8,128)(2,1)}, u32[]{:S(2)}, u32[]{:S(2)}) collective-permute-start(bf16[256,1024]{1,0:T(8,128)(2,1)} %collective-permute-done.refs_2_), channel_id=1, source_target_pairs={{4,8},{6,10},{8,12},{10,14},{5,9},{7,11},{9,13},{11,15},{20,24},{2... | collective-permute-start | bytes 1572872 | tf_op jit(solution)/shard_map/ppermute | solution.py:499
  25.7 2.5 %for_pair.1.refs_6_ = bf16[128,5120]{1,0:T(8,128)(2,1)} custom-call(s32[1]{0:T(128)} %bitcast.2.refs_0_, bf16[128,8192]{1,0:T(8,128)(2,1)} %refs_1_.5, bf16[128,1024]{1,0:T(8,128)(2,1)} %refs_2_.5), custom_call_target="tpu_custom_call" | custom-call | flops 1 | bytes 1 | tf_op jit(solution)/shard_map/for_pair/pallas_call | solution.py:419
  28.2 6.6 %dispatch.1.refs_0_ = bf16[1280,1024]{1,0:T(8,128)(2,1)} custom-call(f32[1,128]{1,0:T(1,128)} %get-tuple-element.21.refs_0_, bf16[128,8192]{1,0:T(8,128)(2,1)} %refs_1_.5), custom_call_target="tpu_custom_call" | custom-call | flops 1 | bytes 1 | tf_op jit(solution)/shard_map/dispatch/pallas_call | solution.py:419
  34.8 0.0 collective-permute-done.5.refs_5_.refs_6_
  34.8 1.0 collective-permute-done.4.refs_4_.refs_5_
  35.8 0.0 all-to-all-done.refs_1_.refs_0_
  35.8 4.1 %collective-permute-done.3.refs_3_.refs_2_.refs_1_ = bf16[256,1024]{1,0:T(8,128)(2,1)S(1)} collective-permute-done((bf16[256,1024]{1,0:T(8,128)(2,1)}, bf16[256,1024]{1,0:T(8,128)(2,1)S(1)}, u32[]{:S(2)}, u32[]{:S(2)}) %collective-permute-start.3) | collective-permute-done | bytes 524320 | tf_op jit(solution)/shard_map/ppermute | solution.py:501
  39.9 0.0 collective-permute-done.1.refs_2_.refs_3_
  39.9 0.8 copy-done.5
  40.7 5.5 %all-to-all-start.1 = ((bf16[16,80,1024]{2,1,0:T(8,128)(2,1)}), bf16[16,80,1024]{2,1,0:T(8,128)(2,1)}, u32[]{:S(2)}, u32[]{:S(2)}) async-start(bf16[16,80,1024]{2,1,0:T(8,128)(2,1)} %bitcast.46), calls=%async_computation.1 | async-start | bytes 5242880 | tf_op jit(solution)/shard_map/all_to_all | solution.py:646
  46.2 0.4 collective-permute-start.10
  46.6 1.2 collective-permute-start.11
  47.8 2.1 %pick.4.refs_8_ = bf16[256,1024]{1,0:T(8,128)(2,1)} custom-call(s32[1]{0:T(128)} %bitcast.41.refs_0_, bf16[256,1024]{1,0:T(8,128)(2,1)} %collective-permute-done.2.refs_1_.refs_2_, bf16[256,1024]{1,0:T(8,128)(2,1)} %collective-permute-done.refs_2_), custom_call_target="tpu_custom_call" | custom-call | flops 1 | bytes 1 | tf_op jit(solution)/shard_map/pick/pallas_call | solution.py:419
  49.9 0.3 collective-permute-start.12
  50.1 0.3 collective-permute-start.13
  50.4 2.3 %pick.5.refs_12_ = bf16[256,1024]{1,0:T(8,128)(2,1)} custom-call(s32[1]{0:T(128)} %bitcast.42.refs_0_, bf16[256,1024]{1,0:T(8,128)(2,1)} %copy-done.5, bf16[256,1024]{1,0:T(8,128)(2,1)} %collective-permute-done.2.refs_1_.refs_2_, bf16[256,1024]{1,0:T(8,128)(2,1)} %collective-permute-done.1.refs_2_.refs_3_), custom_call_target="tpu_custom_call" | custom-call | flops 1 | bytes 1 | tf_op jit(solution)/shard_map/pick/pallas_call | solution.py:419
  52.7 1.2 collective-permute-start.16
  53.9 6.4 %collective-permute-done.11.refs_7_.refs_5_ = bf16[256,1024]{1,0:T(8,128)(2,1)} collective-permute-done((bf16[256,1024]{1,0:T(8,128)(2,1)}, bf16[256,1024]{1,0:T(8,128)(2,1)}, u32[]{:S(2)}, u32[]{:S(2)}) %collective-permute-start.11) | collective-permute-done | bytes 524320 | tf_op jit(solution)/shard_map/ppermute | solution.py:485
  60.3 3.0 %collective-permute-start.6 = (bf16[256,1024]{1,0:T(8,128)(2,1)S(1)}, bf16[256,1024]{1,0:T(8,128)(2,1)}, u32[]{:S(2)}, u32[]{:S(2)}) collective-permute-start(bf16[256,1024]{1,0:T(8,128)(2,1)S(1)} %copy-done.6), channel_id=1, source_target_pairs={{4,0},{6,2},{5,1},{7,3},{20,16},{22,18},{21,17},{23,19}} | collective-permute-start | bytes 1572872 | tf_op jit(solution)/shard_map/ppermute | solution.py:501
  63.3 13.0 %collective-permute-done.12.refs_9_.refs_3_ = bf16[256,1024]{1,0:T(8,128)(2,1)} collective-permute-done((bf16[256,1024]{1,0:T(8,128)(2,1)}, bf16[256,1024]{1,0:T(8,128)(2,1)}, u32[]{:S(2)}, u32[]{:S(2)}) %collective-permute-start.12) | collective-permute-done | bytes 524320 | tf_op jit(solution)/shard_map/ppermute | solution.py:485
  76.3 1.2 collective-permute-start.14
  77.5 0.0 copy-start.1
  77.6 1.5 collective-permute-start.7
  79.1 8.8 %rank_grad_back.1 = (bf16[1280,512]{1,0:T(8,128)(2,1)}, bf16[1280,640]{1,0:T(8,128)(2,1)}, bf16[1280,128]{1,0:T(8,128)(2,1)}, bf16[1280,128]{1,0:T(8,128)(2,1)}) custom-call(bf16[16,96,128]{2,1,0:T(8,128)(2,1)} %copy-done.2, bf16[128,1024]{1,0:T(8,128)(2,1)} %bitcast.51, bf16[128,8192]{1,0:T(8,128)(2,1)} %bitcast.48), custom_call_target="tpu_custom_call" | custom-call | flops 1 | bytes 1 | tf_op jit(solution)/shard_map/rank_grad_back/pallas_call | solution.py:419
  87.9 12.1 %collective-permute-done.6.refs_1_.refs_2_ = bf16[256,1024]{1,0:T(8,128)(2,1)} collective-permute-done((bf16[256,1024]{1,0:T(8,128)(2,1)S(1)}, bf16[256,1024]{1,0:T(8,128)(2,1)}, u32[]{:S(2)}, u32[]{:S(2)}) %collective-permute-start.6) | collective-permute-done | bytes 524320 | tf_op jit(solution)/shard_map/ppermute | solution.py:501
  100.0 0.0 collective-permute-done.14.refs_11_.refs_8_
  100.0 0.0 collective-permute-done.16.refs_14_.refs_7_
  100.0 0.0 collective-permute-done.15.refs_13_.refs_6_
  100.0 0.0 collective-permute-done.7.refs_4_.refs_1_
  100.0 5.1 %all-to-all-done.1 = bf16[16,80,1024]{2,1,0:T(8,128)(2,1)} async-done(((bf16[16,80,1024]{2,1,0:T(8,128)(2,1)}), bf16[16,80,1024]{2,1,0:T(8,128)(2,1)}, u32[]{:S(2)}, u32[]{:S(2)}) %all-to-all-start.1) | async-done | bytes 2621472 | tf_op jit(solution)/shard_map/all_to_all | solution.py:646
  105.1 8.9 %all-to-all-start.3 = ((bf16[16,80,512]{2,1,0:T(8,128)(2,1)}), bf16[16,80,512]{2,1,0:T(8,128)(2,1)S(1)}, u32[]{:S(2)}, u32[]{:S(2)}) async-start(bf16[16,80,512]{2,1,0:T(8,128)(2,1)} %bitcast.50), calls=%async_computation.3 | async-start | bytes 2621440 | tf_op jit(solution)/shard_map/all_to_all | solution.py:646
  114.0 2.4 %pick.3.refs_16_ = bf16[256,1024]{1,0:T(8,128)(2,1)} custom-call(s32[1]{0:T(128)} %bitcast.7.refs_0_, bf16[256,1024]{1,0:T(8,128)(2,1)} %collective-permute-done.6.refs_1_.refs_2_, bf16[256,1024]{1,0:T(8,128)(2,1)} %copy-done.5, bf16[256,1024]{1,0:T(8,128)(2,1)} %collective-permute-done.1.refs_2_.refs_3_, ...), custom_call_target="tpu_custom_call" | custom-call | flops 1 | bytes 1 | tf_op jit(solution)/shard_map/pick/pallas_call | solution.py:419
  116.4 0.3 collective-permute-start.8
  116.7 1.2 collective-permute-start.9
  117.9 0.3 collective-permute-start.17
  118.2 10.2 %lowrank_out.1 = (bf16[1280,640]{1,0:T(8,128)(2,1)}, bf16[1280,128]{1,0:T(8,128)(2,1)}) custom-call(bf16[1280,1024]{1,0:T(8,128)(2,1)} %bitcast.4.refs_0_, bf16[1280,128]{1,0:T(8,128)(2,1)} %get-tuple-element.23.refs_1_, bf16[128,8192]{1,0:T(8,128)(2,1)} %bitcast.49, bf16[128,1024]{1,0:T(8,128)(2,1)} %bitcast.52, ...), custom_call_target="tpu_custom_call", output_to_operand_aliasing={{0}: (4, {})} | custom-call | flops 1 | bytes 1 | tf_op jit(solution)/shard_map/lowrank_out/pallas_call | solution.py:419
  128.4 10.5 %collective-permute-done.8.refs_0_ = bf16[256,1024]{1,0:T(8,128)(2,1)S(1)} collective-permute-done((bf16[256,1024]{1,0:T(8,128)(2,1)}, bf16[256,1024]{1,0:T(8,128)(2,1)S(1)}, u32[]{:S(2)}, u32[]{:S(2)}) %collective-permute-start.8) | collective-permute-done | bytes 524320 | tf_op jit(solution)/shard_map/ppermute | solution.py:485
  138.9 0.8 copy-done.4
  139.7 1.2 collective-permute-start.18
  140.9 0.0 collective-permute-done.9.refs_2_.refs_18_
  140.9 4.1 %all-to-all-done.3.refs_2_ = bf16[16,80,512]{2,1,0:T(8,128)(2,1)S(1)} async-done(((bf16[16,80,512]{2,1,0:T(8,128)(2,1)}), bf16[16,80,512]{2,1,0:T(8,128)(2,1)S(1)}, u32[]{:S(2)}, u32[]{:S(2)}) %all-to-all-start.3) | async-done | bytes 1310752 | tf_op jit(solution)/shard_map/all_to_all | solution.py:646
  145.0 4.5 %all-to-all-start.2 = ((bf16[16,80,640]{2,1,0:T(8,128)(2,1)}), bf16[16,80,640]{2,1,0:T(8,128)(2,1)}, u32[]{:S(2)}, u32[]{:S(2)}) async-start(bf16[16,80,640]{2,1,0:T(8,128)(2,1)} %bitcast.47), calls=%async_computation.2 | async-start | bytes 3276800 | tf_op jit(solution)/shard_map/all_to_all | solution.py:646
  149.6 0.6 stack.131.refs_0_
  150.2 0.0 collective-permute-done.17.refs_15_
  150.2 2.5 %collective-permute-done.18.refs_19_ = bf16[256,1024]{1,0:T(8,128)(2,1)} collective-permute-done((bf16[256,1024]{1,0:T(8,128)(2,1)}, bf16[256,1024]{1,0:T(8,128)(2,1)}, u32[]{:S(2)}, u32[]{:S(2)}) %collective-permute-start.18) | collective-permute-done | bytes 524320 | tf_op jit(solution)/shard_map/ppermute | solution.py:485
  152.7 11.3 %base.1 = (f32[128,1024]{1,0:T(8,128)}, f32[128,4096]{1,0:T(8,128)}, f32[128,5120]{1,0:T(8,128)}) custom-call(s32[32]{0:T(128)} %stack.131.refs_0_, bf16[128,8192]{1,0:T(8,128)(2,1)} %refs_1_.5, bf16[128,1024]{1,0:T(8,128)(2,1)} %refs_2_.5, bf16[128,5120]{1,0:T(8,128)(2,1)} %held.8.refs_3_, bf16[256,1024]{1,0:T(8,128)(2,1)} %constant_dynamic-slice_fusion.refs_4_, ...), custom_call_target="tpu_custom_call" | custom-call | flops 1 | bytes 1 | tf_op jit(solution)/shard_map/base/pallas_call | solution.py:419
  164.1 1.7 collective-permute-start.19
  165.7 6.9 %page_grads.1 = (bf16[128,8192]{1,0:T(8,128)(2,1)}, bf16[128,1024]{1,0:T(8,128)(2,1)}) custom-call(bf16[1280,1024]{1,0:T(8,128)(2,1)} %bitcast.4.refs_0_, bf16[16,96,128]{2,1,0:T(8,128)(2,1)} %copy-done.2, bf16[1280,128]{1,0:T(8,128)(2,1)} %get-tuple-element.26.refs_1_.refs_2_, bf16[1280,128]{1,0:T(8,128)(2,1)} %get-tuple-element.33.refs_3_), custom_call_target="tpu_custom_call" | custom-call | flops 1 | bytes 1 | tf_op jit(solution)/shard_map/page_grads/pallas_call | solution.py:419
  172.7 0.0 collective-permute-done.19.refs_4_.refs_6_
  172.7 4.1 %combine_first.1.refs_7_ = bf16[128,8192]{1,0:T(8,128)(2,1)} custom-call(s32[1]{0:T(128)} %bitcast.refs_0_, f32[128,128]{1,0:T(8,128)} %get-tuple-element.20.refs_1_, bf16[16,80,512]{2,1,0:T(8,128)(2,1)} %copy-done.3, f32[128,4096]{1,0:T(8,128)} %get-tuple-element.27.refs_3_, f32[128,5120]{1,0:T(8,128)} %collective-permute-done.19.refs_4_.refs_6_), custom_call_target="tpu_custom_call" | custom-call | flops 1 | bytes 1 | tf_op jit(solution)/shard_map/combine_first/pallas_call | solution.py:419
  176.8 10.4 %all-to-all-done.2.refs_2_ = bf16[16,80,640]{2,1,0:T(8,128)(2,1)} async-done(((bf16[16,80,640]{2,1,0:T(8,128)(2,1)}), bf16[16,80,640]{2,1,0:T(8,128)(2,1)}, u32[]{:S(2)}, u32[]{:S(2)}) %all-to-all-start.2) | async-done | bytes 1638432 | tf_op jit(solution)/shard_map/all_to_all | solution.py:646
  187.2 5.3 %combine_rest.1 = (bf16[128,1024]{1,0:T(8,128)(2,1)}, bf16[128,8192]{1,0:T(8,128)(2,1)}) custom-call(s32[1]{0:T(128)} %bitcast.refs_0_, f32[128,128]{1,0:T(8,128)} %get-tuple-element.20.refs_1_, bf16[16,80,640]{2,1,0:T(8,128)(2,1)} %all-to-all-done.2.refs_2_, f32[128,4096]{1,0:T(8,128)} %get-tuple-element.27.refs_3_, ...), custom_call_target="tpu_custom_call", output_to_operand_aliasing={{1}: (7, {})} | custom-call | flops 1 | bytes 1 | tf_op jit(solution)/shard_map/combine_rest/pallas_call | solution.py:419
  (17 shorter events, 0.0 us)
Async XLA Ops:
  0.6 1.6 copy-start
  3.0 16.5 %collective-permute-start.2 = (bf16[256,1024]{1,0:T(8,128)(2,1)}, bf16[256,1024]{1,0:T(8,128)(2,1)}, u32[]{:S(2)}, u32[]{:S(2)}) collective-permute-start(bf16[256,1024]{1,0:T(8,128)(2,1)} %constant_dynamic-slice_fusion.refs_4_), channel_id=1, source_target_pairs={{4,0},{6,2},{8,4},{10,6},{12,8},{14,10},{5,1},{7,3},{9,5},{11,7},{... | collective-permute-start | bytes 1572872 | tf_op jit(solution)/shard_map/ppermute | solution.py:501
  5.1 16.5 %collective-permute-start = (bf16[256,1024]{1,0:T(8,128)(2,1)}, bf16[256,1024]{1,0:T(8,128)(2,1)}, u32[]{:S(2)}, u32[]{:S(2)}) collective-permute-start(bf16[256,1024]{1,0:T(8,128)(2,1)} %constant_dynamic-slice_fusion.refs_4_), channel_id=1, source_target_pairs={{0,4},{2,6},{4,8},{6,10},{8,12},{10,14},{1,5},{3,7},{5,9},{7,11},{... | collective-permute-start | bytes 1572872 | tf_op jit(solution)/shard_map/ppermute | solution.py:499
  11.2 24.7 %all-to-all-start = ((bf16[16,96,128]{2,1,0:T(8,128)(2,1)}), bf16[16,96,128]{2,1,0:T(8,128)(2,1)S(1)}, u32[]{:S(2)}, u32[]{:S(2)}) async-start(bf16[16,96,128]{2,1,0:T(8,128)(2,1)} %get-tuple-element.22), calls=%async_computation | async-start | bytes 786432 | tf_op jit(solution)/shard_map/all_to_all | solution.py:646
  18.1 16.7 %collective-permute-start.5 = (bf16[256,1024]{1,0:T(8,128)(2,1)}, bf16[256,1024]{1,0:T(8,128)(2,1)}, u32[]{:S(2)}, u32[]{:S(2)}) collective-permute-start(bf16[256,1024]{1,0:T(8,128)(2,1)} %constant_dynamic-slice_fusion.refs_4_), channel_id=1, source_target_pairs={{0,16},{16,0},{1,17},{17,1},{2,18},{18,2},{3,19},{19,3},{4,20},{20... | collective-permute-start | bytes 1572872 | tf_op jit(solution)/shard_map/ppermute | solution.py:485
  19.3 16.5 %collective-permute-start.4 = (bf16[256,1024]{1,0:T(8,128)(2,1)}, bf16[256,1024]{1,0:T(8,128)(2,1)}, u32[]{:S(2)}, u32[]{:S(2)}) collective-permute-start(bf16[256,1024]{1,0:T(8,128)(2,1)} %constant_dynamic-slice_fusion.refs_4_), channel_id=1, source_target_pairs={{0,2},{2,0},{4,6},{6,4},{8,10},{10,8},{12,14},{14,12},{1,3},{3,1},... | collective-permute-start | bytes 1572872 | tf_op jit(solution)/shard_map/ppermute | solution.py:485
  19.6 20.3 %collective-permute-start.3 = (bf16[256,1024]{1,0:T(8,128)(2,1)}, bf16[256,1024]{1,0:T(8,128)(2,1)S(1)}, u32[]{:S(2)}, u32[]{:S(2)}) collective-permute-start(bf16[256,1024]{1,0:T(8,128)(2,1)} %collective-permute-done.2.refs_1_.refs_2_), channel_id=1, source_target_pairs={{4,0},{6,2},{8,4},{10,6},{5,1},{7,3},{9,5},{11,7},{20,16},{22,18},... | collective-permute-start | bytes 1572872 | tf_op jit(solution)/shard_map/ppermute | solution.py:501
  21.6 18.3 %collective-permute-start.1 = (bf16[256,1024]{1,0:T(8,128)(2,1)}, bf16[256,1024]{1,0:T(8,128)(2,1)}, u32[]{:S(2)}, u32[]{:S(2)}) collective-permute-start(bf16[256,1024]{1,0:T(8,128)(2,1)} %collective-permute-done.refs_2_), channel_id=1, source_target_pairs={{4,8},{6,10},{8,12},{10,14},{5,9},{7,11},{9,13},{11,15},{20,24},{2... | collective-permute-start | bytes 1572872 | tf_op jit(solution)/shard_map/ppermute | solution.py:499
  35.8 4.1 %copy-start.2 = (bf16[16,96,128]{2,1,0:T(8,128)(2,1)}, bf16[16,96,128]{2,1,0:T(8,128)(2,1)S(1)}, u32[]{:S(2)}) copy-start(bf16[16,96,128]{2,1,0:T(8,128)(2,1)S(1)} %all-to-all-done.refs_1_.refs_0_) | copy-start | bytes 1179652
  39.9 0.8 copy-start.5
  40.7 64.4 %all-to-all-start.1 = ((bf16[16,80,1024]{2,1,0:T(8,128)(2,1)}), bf16[16,80,1024]{2,1,0:T(8,128)(2,1)}, u32[]{:S(2)}, u32[]{:S(2)}) async-start(bf16[16,80,1024]{2,1,0:T(8,128)(2,1)} %bitcast.46), calls=%async_computation.1 | async-start | bytes 5242880 | tf_op jit(solution)/shard_map/all_to_all | solution.py:646
  46.2 31.3 %collective-permute-start.10 = (bf16[128,5120]{1,0:T(8,128)(2,1)}, bf16[128,5120]{1,0:T(8,128)(2,1)S(1)}, u32[]{:S(2)}, u32[]{:S(2)}) collective-permute-start(bf16[128,5120]{1,0:T(8,128)(2,1)} %for_pair.1.refs_6_), channel_id=1, source_target_pairs={{0,1},{1,0},{2,3},{3,2},{4,5},{5,4},{6,7},{7,6},{8,9},{9,8},{10,11... | collective-permute-start | bytes 3932168 | tf_op jit(solution)/shard_map/ppermute | solution.py:485
  46.6 13.7 %collective-permute-start.11 = (bf16[256,1024]{1,0:T(8,128)(2,1)}, bf16[256,1024]{1,0:T(8,128)(2,1)}, u32[]{:S(2)}, u32[]{:S(2)}) collective-permute-start(bf16[256,1024]{1,0:T(8,128)(2,1)} %collective-permute-done.4.refs_4_.refs_5_), channel_id=1, source_target_pairs={{0,16},{16,0},{1,17},{17,1},{2,18},{18,2},{3,19},{19,3},{4,20},{20... | collective-permute-start | bytes 1572872 | tf_op jit(solution)/shard_map/ppermute | solution.py:485
  49.9 26.5 %collective-permute-start.12 = (bf16[256,1024]{1,0:T(8,128)(2,1)}, bf16[256,1024]{1,0:T(8,128)(2,1)}, u32[]{:S(2)}, u32[]{:S(2)}) collective-permute-start(bf16[256,1024]{1,0:T(8,128)(2,1)} %pick.4.refs_8_), channel_id=1, source_target_pairs={{0,2},{2,0},{4,6},{6,4},{8,10},{10,8},{12,14},{14,12},{1,3},{3,1},... | collective-permute-start | bytes 1572872 | tf_op jit(solution)/shard_map/ppermute | solution.py:485
  50.1 27.4 %collective-permute-start.13 = (bf16[256,1024]{1,0:T(8,128)(2,1)}, bf16[256,1024]{1,0:T(8,128)(2,1)}, u32[]{:S(2)}, u32[]{:S(2)}) collective-permute-start(bf16[256,1024]{1,0:T(8,128)(2,1)} %pick.4.refs_8_), channel_id=1, source_target_pairs={{0,16},{16,0},{1,17},{17,1},{2,18},{18,2},{3,19},{19,3},{4,20},{20... | collective-permute-start | bytes 1572872 | tf_op jit(solution)/shard_map/ppermute | solution.py:485
  50.4 9.9 %copy-start.6 = (bf16[256,1024]{1,0:T(8,128)(2,1)S(1)}, bf16[256,1024]{1,0:T(8,128)(2,1)}, u32[]{:S(2)}) copy-start(bf16[256,1024]{1,0:T(8,128)(2,1)} %copy-done.5) | copy-start | bytes 1572868
  52.7 47.3 %collective-permute-start.16 = (bf16[256,1024]{1,0:T(8,128)(2,1)}, bf16[256,1024]{1,0:T(8,128)(2,1)}, u32[]{:S(2)}, u32[]{:S(2)}) collective-permute-start(bf16[256,1024]{1,0:T(8,128)(2,1)} %pick.5.refs_12_), channel_id=1, source_target_pairs={{0,16},{16,0},{1,17},{17,1},{2,18},{18,2},{3,19},{19,3},{4,20},{20... | collective-permute-start | bytes 1572872 | tf_op jit(solution)/shard_map/ppermute | solution.py:485
  60.3 39.7 %collective-permute-start.6 = (bf16[256,1024]{1,0:T(8,128)(2,1)S(1)}, bf16[256,1024]{1,0:T(8,128)(2,1)}, u32[]{:S(2)}, u32[]{:S(2)}) collective-permute-start(bf16[256,1024]{1,0:T(8,128)(2,1)S(1)} %copy-done.6), channel_id=1, source_target_pairs={{4,0},{6,2},{5,1},{7,3},{20,16},{22,18},{21,17},{23,19}} | collective-permute-start | bytes 1572872 | tf_op jit(solution)/shard_map/ppermute | solution.py:501
  76.3 23.7 %collective-permute-start.14 = (bf16[256,1024]{1,0:T(8,128)(2,1)}, bf16[256,1024]{1,0:T(8,128)(2,1)}, u32[]{:S(2)}, u32[]{:S(2)}) collective-permute-start(bf16[256,1024]{1,0:T(8,128)(2,1)} %collective-permute-done.12.refs_9_.refs_3_), channel_id=1, source_target_pairs={{0,16},{16,0},{1,17},{17,1},{2,18},{18,2},{3,19},{19,3},{4,20},{20... | collective-permute-start | bytes 1572872 | tf_op jit(solution)/shard_map/ppermute | solution.py:485
  77.5 22.5 %collective-permute-start.15 = (bf16[256,1024]{1,0:T(8,128)(2,1)}, bf16[256,1024]{1,0:T(8,128)(2,1)}, u32[]{:S(2)}, u32[]{:S(2)}) collective-permute-start(bf16[256,1024]{1,0:T(8,128)(2,1)} %pick.5.refs_12_), channel_id=1, source_target_pairs={{0,2},{2,0},{4,6},{6,4},{8,10},{10,8},{12,14},{14,12},{1,3},{3,1},... | collective-permute-start | bytes 1572872 | tf_op jit(solution)/shard_map/ppermute | solution.py:485
  77.5 22.5 %copy-start.1 = (bf16[128,5120]{1,0:T(8,128)(2,1)}, bf16[128,5120]{1,0:T(8,128)(2,1)S(1)}, u32[]{:S(2)}) copy-start(bf16[128,5120]{1,0:T(8,128)(2,1)S(1)} %collective-permute-done.10.refs_0_.refs_9_) | copy-start | bytes 3932164
  77.6 22.4 %collective-permute-start.7 = (bf16[256,1024]{1,0:T(8,128)(2,1)}, bf16[256,1024]{1,0:T(8,128)(2,1)}, u32[]{:S(2)}, u32[]{:S(2)}) collective-permute-start(bf16[256,1024]{1,0:T(8,128)(2,1)} %collective-permute-done.1.refs_2_.refs_3_), channel_id=1, source_target_pairs={{8,12},{10,14},{9,13},{11,15},{24,28},{26,30},{25,29},{27,31}} | collective-permute-start | bytes 1572872 | tf_op jit(solution)/shard_map/ppermute | solution.py:499
  105.1 39.9 %all-to-all-start.3 = ((bf16[16,80,512]{2,1,0:T(8,128)(2,1)}), bf16[16,80,512]{2,1,0:T(8,128)(2,1)S(1)}, u32[]{:S(2)}, u32[]{:S(2)}) async-start(bf16[16,80,512]{2,1,0:T(8,128)(2,1)} %bitcast.50), calls=%async_computation.3 | async-start | bytes 2621440 | tf_op jit(solution)/shard_map/all_to_all | solution.py:646
  116.4 22.5 %collective-permute-start.8 = (bf16[256,1024]{1,0:T(8,128)(2,1)}, bf16[256,1024]{1,0:T(8,128)(2,1)S(1)}, u32[]{:S(2)}, u32[]{:S(2)}) collective-permute-start(bf16[256,1024]{1,0:T(8,128)(2,1)} %pick.3.refs_16_), channel_id=1, source_target_pairs={{0,2},{2,0},{4,6},{6,4},{8,10},{10,8},{12,14},{14,12},{1,3},{3,1},... | collective-permute-start | bytes 1572872 | tf_op jit(solution)/shard_map/ppermute | solution.py:485
  116.7 24.2 %collective-permute-start.9 = (bf16[256,1024]{1,0:T(8,128)(2,1)}, bf16[256,1024]{1,0:T(8,128)(2,1)}, u32[]{:S(2)}, u32[]{:S(2)}) collective-permute-start(bf16[256,1024]{1,0:T(8,128)(2,1)} %pick.3.refs_16_), channel_id=1, source_target_pairs={{0,16},{16,0},{1,17},{17,1},{2,18},{18,2},{3,19},{19,3},{4,20},{20... | collective-permute-start | bytes 1572872 | tf_op jit(solution)/shard_map/ppermute | solution.py:485
  117.9 32.3 %collective-permute-start.17 = (bf16[256,1024]{1,0:T(8,128)(2,1)}, bf16[256,1024]{1,0:T(8,128)(2,1)}, u32[]{:S(2)}, u32[]{:S(2)}) collective-permute-start(bf16[256,1024]{1,0:T(8,128)(2,1)} %collective-permute-done.15.refs_13_.refs_6_), channel_id=1, source_target_pairs={{0,16},{16,0},{1,17},{17,1},{2,18},{18,2},{3,19},{19,3},{4,20},{20... | collective-permute-start | bytes 1572872 | tf_op jit(solution)/shard_map/ppermute | solution.py:485
  138.9 0.8 copy-start.4
  139.7 13.0 %collective-permute-start.18 = (bf16[256,1024]{1,0:T(8,128)(2,1)}, bf16[256,1024]{1,0:T(8,128)(2,1)}, u32[]{:S(2)}, u32[]{:S(2)}) collective-permute-start(bf16[256,1024]{1,0:T(8,128)(2,1)} %held.6.refs_1_.refs_17_), channel_id=1, source_target_pairs={{0,16},{16,0},{1,17},{17,1},{2,18},{18,2},{3,19},{19,3},{4,20},{20... | collective-permute-start | bytes 1572872 | tf_op jit(solution)/shard_map/ppermute | solution.py:485
  145.0 5.2 %copy-start.3 = (bf16[16,80,512]{2,1,0:T(8,128)(2,1)}, bf16[16,80,512]{2,1,0:T(8,128)(2,1)S(1)}, u32[]{:S(2)}) copy-start(bf16[16,80,512]{2,1,0:T(8,128)(2,1)S(1)} %all-to-all-done.3.refs_2_) | copy-start | bytes 3932164
  145.0 42.2 %all-to-all-start.2 = ((bf16[16,80,640]{2,1,0:T(8,128)(2,1)}), bf16[16,80,640]{2,1,0:T(8,128)(2,1)}, u32[]{:S(2)}, u32[]{:S(2)}) async-start(bf16[16,80,640]{2,1,0:T(8,128)(2,1)} %bitcast.47), calls=%async_computation.2 | async-start | bytes 3276800 | tf_op jit(solution)/shard_map/all_to_all | solution.py:646
  164.1 8.6 %collective-permute-start.19 = (f32[128,5120]{1,0:T(8,128)}, f32[128,5120]{1,0:T(8,128)}, u32[]{:S(2)}, u32[]{:S(2)}) collective-permute-start(f32[128,5120]{1,0:T(8,128)} %get-tuple-element.28), channel_id=1, source_target_pairs={{0,1},{1,0},{2,3},{3,2},{4,5},{5,4},{6,7},{7,6},{8,9},{9,8},{10,11... | collective-permute-start | bytes 7864328 | tf_op jit(solution)/shard_map/ppermute | solution.py:485
